TPU v7x, 32 devices: a whole 2x2x4 slice. The times are simulated.
32 devices in a mesh: grp: 4 (over y, x), smp: 8 (over z, core).
Axes of the slice: x: 2, y: 2, z: 4, core: 2. Of those that a mesh axis runs over, the one named last changes fastest.
Arguments:
- currents: bfloat16 [2, 8, 262144], P(None, None, ('grp', 'smp')), may hold values from -6 to 6
- near_blocks: bfloat16 [2, 8192, 32, 256], P(None, ('grp', 'smp')), may hold values from -0.25 to 0.25
- near_list: int32 [8192, 8], P(('grp', 'smp')), may hold values from 0 to 8191, as said below
- near_count: int32 [8192], P(('grp', 'smp')), may hold values from 1 to 8, as said below
- radiation: bfloat16 [2, 8192, 32, 128], P(None, ('grp', 'smp')), may hold values from -0.75 to 0.75
- interp: bfloat16 [64, 1024], replicated, may hold values from -0.75 to 0.75
- shift_angle: float32 [8, 1024], replicated, may hold values from -3.140625 to 3.140625
- translation: bfloat16 [2, 316, 2048], P(None, None, ('grp', 'smp')), may hold values from -0.0625 to 0.0625
- trans_box: int32 [1024, 12], replicated, may hold values from 0 to 1023
- trans_off: int32 [1024, 12], replicated, may hold values from 0 to 315
Outputs:
- product_field: float32 [2, 8, 262144], P(None, None, ('grp', 'smp'))
Inputs may be any that keep to these rules, and one draw needn't show every extreme that they name: `near_list`: entry 0 of row c is c itself, and every entry of row c lies within 256 clusters of c. Slots 0 to near_count[c] - 1 of row c of near_list are live; the other slots are ignored.
All inputs are finite; a program needn't handle non-finite values.
Results may differ from a plain program's by a relative error of at most 0.0056.
Values may be sent and summed in bfloat16 or wider, within the bound.
No kernel may reach another device: no remote copies, remote signals or barrier semaphores. Data moves between devices by JAX's collectives and lax.ppermute only.
A program may use at most 128 MiB of HBM per device.

v0:
```python
import jax
import jax.numpy as jnp
from jax import lax
from jax.sharding import PartitionSpec as P

R = 8
U = 32
NBR = 8
K0 = 64
K1 = 1024
IL = 12


def passed_along(array, axis, by):
    size = lax.axis_size(axis)
    pairs = [(i, i + by) for i in range(size) if 0 <= i + by < size]
    return lax.ppermute(array, axis, pairs)


def product(pattern, left_side, right_side):
    return jnp.einsum(pattern, left_side, right_side, preferred_element_type=jnp.float32)


def complex_terms(pattern, left_side, right_side, conjugate):
    if conjugate:
        real_part = product(pattern, left_side[0], right_side[0]) + product(
            pattern, left_side[1], right_side[1]
        )
        imag_part = product(pattern, left_side[1], right_side[0]) - product(
            pattern, left_side[0], right_side[1]
        )
    else:
        real_part = product(pattern, left_side[0], right_side[0]) - product(
            pattern, left_side[1], right_side[1]
        )
        imag_part = product(pattern, left_side[1], right_side[0]) + product(
            pattern, left_side[0], right_side[1]
        )
    return jnp.stack([real_part, imag_part])


def aggregate(current_block, radiation_block, interp, shift_angle):
    leaf_pattern = complex_terms("rcu,cuq->rcq", current_block, radiation_block, False).astype(
        jnp.bfloat16
    )
    clusters_here = leaf_pattern.shape[2]
    upward = jnp.dot(
        leaf_pattern.reshape(2, R, clusters_here, 2, K0), interp, preferred_element_type=jnp.float32
    )
    upward = upward.reshape(2, R, clusters_here // 8, 8, 2, K1)
    cosine = jnp.cos(shift_angle)[:, None, :]
    sine_part = jnp.sin(shift_angle)[:, None, :]
    real_part = upward[0] * cosine - upward[1] * sine_part
    imag_part = upward[0] * sine_part + upward[1] * cosine
    summed = jnp.stack([real_part.sum(axis=2), imag_part.sum(axis=2)])
    return summed.reshape(2, R, clusters_here // 8, 2 * K1).astype(jnp.bfloat16)


def disaggregate(received, radiation_block, interp, shift_angle):
    boxes_here = received.shape[2]
    widened = received.astype(jnp.float32).reshape(2, R, boxes_here, 1, 2, K1)
    cosine = jnp.cos(shift_angle)[:, None, :]
    sine_part = jnp.sin(shift_angle)[:, None, :]
    real_part = widened[0] * cosine + widened[1] * sine_part
    imag_part = widened[1] * cosine - widened[0] * sine_part
    shifted = jnp.stack([real_part, imag_part]).astype(jnp.bfloat16)
    downward = jnp.dot(shifted, interp.T, preferred_element_type=jnp.float32).astype(jnp.bfloat16)
    downward = downward.reshape(2, R, boxes_here * 8, 2 * K0)
    return complex_terms("rcq,cuq->rcu", downward, radiation_block, True)


def local(
    currents,
    near_blocks,
    near_list,
    near_count,
    radiation,
    interp,
    shift_angle,
    translation,
    trans_box,
    trans_off,
):
    below_rows = passed_along(currents, ("grp", "smp"), 1)
    above_rows = passed_along(currents, ("grp", "smp"), -1)
    clusters_here = near_list.shape[0]
    extended = jnp.concatenate([below_rows, currents, above_rows], axis=2).reshape(
        2, R, 3 * clusters_here, U
    )
    extended_rows = extended.transpose(2, 0, 1, 3).reshape(3 * clusters_here, 2 * R * U)
    device = lax.axis_index(("grp", "smp"))
    local_index = near_list - (device * clusters_here - clusters_here)
    slots = jnp.arange(NBR, dtype=jnp.int32)
    live_mask = slots[None, :] < near_count[:, None]
    row_ids = jnp.arange(3 * clusters_here, dtype=jnp.int32)
    picker = jnp.logical_and(
        local_index[:, :, None] == row_ids[None, None, :], live_mask[:, :, None]
    )
    picker = picker.astype(jnp.bfloat16).reshape(clusters_here * NBR, 3 * clusters_here)
    gathered_near = jnp.dot(picker, extended_rows, preferred_element_type=jnp.float32).astype(
        jnp.bfloat16
    )
    gathered_near = gathered_near.reshape(clusters_here, NBR, 2, R, U).transpose(2, 3, 0, 1, 4)
    gathered_near = gathered_near.reshape(2, R, clusters_here, NBR * U)
    near_field = complex_terms("cum,rcm->rcu", near_blocks, gathered_near, False)
    current_grid = currents.reshape(2, R, clusters_here, U)
    box_pattern = aggregate(current_grid, radiation, interp, shift_angle)
    spread = lax.all_to_all(box_pattern, ("grp", "smp"), split_axis=3, concat_axis=2, tiled=True)
    all_boxes = spread.shape[2]
    samples_here = spread.shape[3]
    lane_width = R * samples_here
    box_rows = spread.transpose(0, 2, 1, 3).reshape(2, all_boxes, lane_width)
    box_real = box_rows[0]
    box_imag = box_rows[1]
    operator_rows = jnp.tile(translation, (1, 1, R))
    operator_real = operator_rows[0]
    operator_imag = operator_rows[1]

    def turn(column, totals):
        partners = lax.dynamic_slice_in_dim(trans_box, column, 1, 1)[:, 0]
        offsets = lax.dynamic_slice_in_dim(trans_off, column, 1, 1)[:, 0]
        part_real = jnp.take(box_real, partners, axis=0).astype(jnp.float32)
        part_imag = jnp.take(box_imag, partners, axis=0).astype(jnp.float32)
        oper_real = jnp.take(operator_real, offsets, axis=0).astype(jnp.float32)
        oper_imag = jnp.take(operator_imag, offsets, axis=0).astype(jnp.float32)
        real_total = totals[0] + oper_real * part_real - oper_imag * part_imag
        imag_total = totals[1] + oper_real * part_imag + oper_imag * part_real
        return (real_total, imag_total)

    empty = jnp.zeros((all_boxes, lane_width), jnp.float32)
    real_total, imag_total = lax.fori_loop(0, IL, turn, (empty, empty))
    translated = jnp.stack([real_total, imag_total]).astype(jnp.bfloat16)
    translated = translated.reshape(2, all_boxes, R, samples_here).transpose(0, 2, 1, 3)
    received = lax.all_to_all(translated, ("grp", "smp"), split_axis=2, concat_axis=3, tiled=True)
    far_field = disaggregate(received, radiation, interp, shift_angle)
    total = near_field + far_field
    return total.reshape(2, R, clusters_here * U)


def solution(mesh):
    placed = (
        P(None, None, ("grp", "smp")),
        P(None, ("grp", "smp"), None, None),
        P(("grp", "smp"), None),
        P(("grp", "smp")),
        P(None, ("grp", "smp"), None, None),
        P(),
        P(),
        P(None, None, ("grp", "smp")),
        P(),
        P(),
    )
    return jax.shard_map(
        local, mesh=mesh, in_specs=placed, out_specs=P(None, None, ("grp", "smp")), check_vma=False
    )
```

profile of v0, /device:TPU:0, one launch (start us, length us, event | category | flops | bytes accessed | tf_op | source)
XLA Modules:
  0.0 619.7 jit_solution(16560620615003446939)
XLA Ops:
  10.3 13.4 %fusion.103 = f32[2,8,256,2,1024]{4,2,3,1,0:T(8,128)} fusion(bf16[1,8,256,2,64]{2,4,3,1,0:T(8,128)(2,1)S(1)} %bitcast.168, bf16[1,8,256,2,64]{2,4,3,1,0:T(8,128)(2,1)S(1)} %bitcast.167, bf16[64,1024]{1,0:T(8,128)(2,1)S(1)} %copy-done), kind=kOutput, calls=%fused_computation.96 | convolution fusion | flops 1074266112 | bytes 34734080 | tf_op jit(solution)/shard_map/dot_general | solution.py:47
  23.7 16.7 %subtract_reduce_fusion = (bf16[8,32,2,1024]{3,1,2,0:T(8,128)(2,1)S(1)}, bf16[8,32,2,1024]{3,1,2,0:T(8,128)(2,1)S(1)}) fusion(f32[2,8,256,2,1024]{4,2,3,1,0:T(8,128)} %fusion.103, f32[8,1024]{1,0:T(8,128)S(1)} %get-tuple-element.284, f32[8,1024]{1,0:T(8,128)S(1)} %get-tuple-element.283), kind=kLoop, calls=%fused_computation.35 | loop fusion | flops 32505856 | bytes 35717120 | tf_op jit(solution)/shard_map/reduce_sum | solution.py:55
  46.4 8.7 %copy.178 = bf16[2,8,32,2048]{2,1,0,3:T(8,128)(2,1)} copy(bf16[2,8,32,2048]{3,2,1,0:T(8,128)(2,1)S(1)} %pad_maximum_fusion) | data formatting | bytes 4194304 | tf_op jit(solution)/shard_map/stack | solution.py:55
  55.1 13.3 %reshape.212 = bf16[32,2,16384]{2,1,0:T(2,128)(2,1)} reshape(bf16[2048,2,8,32]{3,2,1,0:T(8,128)(2,1)} %bitcast.153) | data formatting | bytes 4194304
  68.4 7.3 %all-to-all-start = ((bf16[32,2,16384]{2,1,0:T(2,128)(2,1)}), bf16[32,2,16384]{2,1,0:T(2,128)(2,1)S(1)}, u32[]{:S(2)}, u32[]{:S(2)}) async-start(bf16[32,2,16384]{2,1,0:T(2,128)(2,1)} %reshape.212), calls=%async_computation | async-start | bytes 4194304 | tf_op jit(solution)/shard_map/all_to_all | solution.py:108
  80.6 45.2 %all-to-all-done = bf16[32,2,16384]{2,1,0:T(2,128)(2,1)S(1)} async-done(((bf16[32,2,16384]{2,1,0:T(2,128)(2,1)}), bf16[32,2,16384]{2,1,0:T(2,128)(2,1)S(1)}, u32[]{:S(2)}, u32[]{:S(2)}) %all-to-all-start) | async-done | bytes 2097184 | tf_op jit(solution)/shard_map/all_to_all | solution.py:108
  125.8 6.6 %reshape.213 = bf16[2048,2,8,32]{3,2,1,0:T(8,128)(2,1)} reshape(bf16[32,2,16384]{2,1,0:T(2,128)(2,1)S(1)} %all-to-all-done) | data formatting | bytes 4194304
  132.4 9.8 %copy.180 = bf16[2,8,32,32,64]{4,3,2,1,0:T(8,128)(2,1)} copy(bf16[2,8,32,32,64]{3,1,0,4,2:T(8,128)(2,1)} %bitcast.154) | data formatting | bytes 4194304 | tf_op jit(solution)/shard_map/all_to_all | solution.py:108
  153.5 321.1 %while.16 = (s32[]{:T(128)}, f32[1024,512]{1,0:T(8,128)}, f32[1024,512]{1,0:T(8,128)}, s32[1024,12]{0,1:T(8,128)}, s32[1024,12]{0,1:T(8,128)}, /*index=5*/bf16[1...) while((s32[]{:T(128)}, f32[1024,512]{1,0:T(8,128)}, ...), condition=%wide.region_3.6_spmd.clone, body=%wide.region_2.5_spmd.clone.sunk | while | flops 9457667 | bytes 27249816 | solution.py:131
  200.9 5.2 fusion.135
  227.8 5.2 fusion.135
  254.6 5.2 fusion.135
  281.4 5.2 fusion.135
  308.3 5.2 fusion.135
  335.1 5.2 fusion.135
  362.0 5.2 fusion.135
  484.4 7.9 %reshape.214 = bf16[32,2,16384]{2,1,0:T(2,128)(2,1)} reshape(bf16[1024,2,8,64]{3,2,1,0:T(8,128)(2,1)} %bitcast.158) | data formatting | bytes 4194304
  492.3 5.6 all-to-all-start.1
  509.5 7.0 %reshape.162 = bf16[256,8,2,8,32]{4,3,2,1,0:T(8,128)(2,1)} reshape(bf16[2048,512]{1,0:T(8,128)(2,1)S(1)} %fusion.31) | data formatting | bytes 4194304 | tf_op jit(solution)/shard_map/reshape | solution.py:103
  516.6 6.4 %fusion.116 = (bf16[1,8,256,8,32]{4,1,0,3,2:T(8,128)(2,1)}, bf16[1,8,256,8,32]{4,1,0,3,2:T(8,128)(2,1)}) fusion(bf16[2,8,256,8,32]{4,1,0,3,2:T(8,128)(2,1)} %bitcast.155), kind=kLoop, calls=%fused_computation.115 | loop fusion | bytes 4194304 | tf_op jit(solution)/shard_map/slice | solution.py:34
  550.6 8.1 %reshape.215 = bf16[1024,2,8,64]{3,2,1,0:T(8,128)(2,1)} reshape(bf16[32,2,16384]{2,1,0:T(2,128)(2,1)} %all-to-all-done.1) | data formatting | bytes 4194304
  574.7 6.6 %copy.190 = f32[1,8,32,32,64]{4,3,2,1,0:T(8,128)} copy(f32[1,8,32,32,64]{4,2,3,1,0:T(8,128)} %get-tuple-element.270) | data formatting | bytes 4194304 | tf_op jit(solution)/shard_map/slice | solution.py:64
  586.5 7.7 %add_convert_fusion = (bf16[1,8,32,8,2,1024]{5,3,4,2,1,0:T(8,128)(2,1)S(1)}, bf16[1,8,32,8,2,1024]{5,3,4,2,1,0:T(8,128)(2,1)}) fusion(f32[8,1024]{1,0:T(8,128)S(1)} %copy-done.9, f32[8,32,2,1024]{3,2,1,0:T(2,128)} %mul.166, f32[8,1024]{1,0:T(8,128)S(1)} %copy-done.7, f32[8,32,2,1024]{3,2,1,0:T(2,128)S(1)} %mul.162), kind=kLoop, calls=%fused_computation.33 | loop fusion | flops 33554432 | bytes 21037056 | tf_op jit(solution)/shard_map/convert.2
  594.2 7.0 %fusion.50 = bf16[2,8,32,8,2,64]{5,3,4,2,1,0:T(8,128)(2,1)S(1)} fusion(bf16[1,8,32,8,2,1024]{5,3,4,2,1,0:T(8,128)(2,1)} %get-tuple-element.274, bf16[1,8,32,8,2,1024]{5,3,4,2,1,0:T(8,128)(2,1)S(1)} %get-tuple-element.273, bf16[64,1024]{1,0:T(8,128)(2,1)S(1)} %copy-done), kind=kOutput, calls=%fused_computation.73 | convolution fusion | flops 1082654720 | bytes 17956864 | tf_op jit(solution)/shard_map/dot_general | solution.py:67
  (284 shorter events, 404.4 us)
Async XLA Ops:
  0.0 10.3 %copy-start = (bf16[64,1024]{1,0:T(8,128)(2,1)S(1)}, bf16[64,1024]{1,0:T(8,128)(2,1)}, u32[]{:S(2)}) copy-start(bf16[64,1024]{1,0:T(8,128)(2,1)} %param.21) | copy-start | bytes 393220
  10.3 13.4 %copy-start.6 = (f32[8,1024]{1,0:T(8,128)}, f32[8,1024]{1,0:T(8,128)S(1)}, u32[]{:S(2)}) copy-start(f32[8,1024]{1,0:T(8,128)S(1)} %get-tuple-element.283) | copy-start | bytes 98308
  10.3 13.4 %copy-start.8 = (f32[8,1024]{1,0:T(8,128)}, f32[8,1024]{1,0:T(8,128)S(1)}, u32[]{:S(2)}) copy-start(f32[8,1024]{1,0:T(8,128)S(1)} %get-tuple-element.284) | copy-start | bytes 98308
  68.4 11.7 %copy-start.12 = (s32[256,8]{0,1:T(8,128)S(1)}, s32[256,8]{0,1:T(8,128)}, u32[]{:S(2)}) copy-start(s32[256,8]{0,1:T(8,128)} %param.18) | copy-start | bytes 24580
  68.4 12.0 %copy-start.13 = (s32[256]{0:T(256)S(1)}, s32[256]{0:T(256)}, u32[]{:S(2)}) copy-start(s32[256]{0:T(256)} %param.19) | copy-start | bytes 3076
  68.4 12.2 %copy-start.10 = (bf16[2,316,64]{1,2,0:T(8,128)(2,1)S(1)}, bf16[2,316,64]{1,2,0:T(8,128)(2,1)}, u32[]{:S(2)}) copy-start(bf16[2,316,64]{1,2,0:T(8,128)(2,1)} %param.23) | copy-start | bytes 242692
  68.4 57.4 %all-to-all-start = ((bf16[32,2,16384]{2,1,0:T(2,128)(2,1)}), bf16[32,2,16384]{2,1,0:T(2,128)(2,1)S(1)}, u32[]{:S(2)}, u32[]{:S(2)}) async-start(bf16[32,2,16384]{2,1,0:T(2,128)(2,1)} %reshape.212), calls=%async_computation | async-start | bytes 4194304 | tf_op jit(solution)/shard_map/all_to_all | solution.py:108
  75.7 422.2 %collective-permute-start = (bf16[2,8,8192]{2,1,0:T(8,128)(2,1)}, bf16[2,8,8192]{2,1,0:T(8,128)(2,1)}, u32[]{:S(2)}, u32[]{:S(2)}) collective-permute-start(bf16[2,8,8192]{2,1,0:T(8,128)(2,1)} %param.16), channel_id=1, source_target_pairs={{0,1},{1,2},{2,3},{3,4},{4,5},{5,6},{6,7},{7,8},{8,9},{9,10},{10,1... | collective-permute-start | bytes 786440 | tf_op jit(solution)/shard_map/ppermute | solution.py:17
  78.6 419.3 %collective-permute-start.1 = (bf16[2,8,8192]{2,1,0:T(8,128)(2,1)}, bf16[2,8,8192]{2,1,0:T(8,128)(2,1)}, u32[]{:S(2)}, u32[]{:S(2)}) collective-permute-start(bf16[2,8,8192]{2,1,0:T(8,128)(2,1)} %param.16), channel_id=1, source_target_pairs={{1,0},{2,1},{3,2},{4,3},{5,4},{6,5},{7,6},{8,7},{9,8},{10,9},{11,1... | collective-permute-start | bytes 786440 | tf_op jit(solution)/shard_map/ppermute | solution.py:17
  170.0 5.1 copy-start.1
  195.8 5.1 copy-start.1
  222.6 5.1 copy-start.1
  249.5 5.1 copy-start.1
  276.3 5.1 copy-start.1
  303.2 5.1 copy-start.1
  330.0 5.1 copy-start.1
  356.8 5.1 copy-start.1
  383.7 5.1 copy-start.1
  410.5 5.1 copy-start.1
  437.3 5.1 copy-start.1
  464.2 5.1 copy-start.1
  492.3 58.3 %all-to-all-start.1 = ((bf16[32,2,16384]{2,1,0:T(2,128)(2,1)}), bf16[32,2,16384]{2,1,0:T(2,128)(2,1)}, u32[]{:S(2)}, u32[]{:S(2)}) async-start(bf16[32,2,16384]{2,1,0:T(2,128)(2,1)} %reshape.214), calls=%async_computation.1 | async-start | bytes 4194304 | tf_op jit(solution)/shard_map/all_to_all | solution.py:134
  581.3 5.2 copy-start.7
  581.3 5.2 copy-start.9
  (5 other events, 16.9 us)
where the time goes:
time: 626 us; the launch traced here: 620 us
  local copies, waits for them, and re-layouts  405 us (65%)
  other arithmetic  93.6 us (15%)
  matrix products  57.8 us (9%)
  waiting for transfers between devices  45.2 us (7%)
  starting transfers between devices  17.2 us (3%)
    add x12, other arithmetic, turn(): imag_total = totals[1] + oper_real * part_imag + oper_imag * part_real  61.9 us
    gather x12, local copies, waits for them, and re-layouts, turn(): oper_imag = jnp.take(operator_imag, offsets, axis=0).astype(jnp.float32)  61 us
    gather x12, local copies, waits for them, and re-layouts, turn(): oper_real = jnp.take(operator_real, offsets, axis=0).astype(jnp.float32)  61 us
    gather x12, local copies, waits for them, and re-layouts, turn(): part_imag = jnp.take(box_imag, partners, axis=0).astype(jnp.float32)  61 us
    gather x12, local copies, waits for them, and re-layouts, turn(): part_real = jnp.take(box_real, partners, axis=0).astype(jnp.float32)  60.8 us
    all_to_all x1, waiting for transfers between devices, local(): lax.all_to_all(box_pattern, ('grp', 'smp'), split_axis=3, concat_axis=2,...  45.2 us
    unnamed x32, local copies, waits for them, and re-layouts  39.2 us
    dot_general x12, matrix products, product(): jnp.einsum(pattern, left_side, right_side, preferred_element_type=jnp.flo...  33.4 us
  transfers between devices with their start and end apart: 4, of which 1 were waited for; matrix products, arithmetic and copies ran while one was open for 68% of the time, Pallas kernels for 0%

commit v1 on v0

v1 whole, which is shorter than its diff:
```python
import functools

import jax
import jax.numpy as jnp
from jax import lax
from jax.experimental import pallas as pl
from jax.experimental.pallas import tpu as pltpu
from jax.sharding import Mesh
from jax.sharding import PartitionSpec as P

R = 8
U = 32
NBR = 8
K0 = 64
K1 = 1024
IL = 12
CHILDREN = 8
WIDE = CHILDREN * U
LANES = 128
HALF = 64
CHIPS = K1 // LANES
DEPTH = 2 * CHILDREN * K0
ALL = ("grp", "hi", "mid", "core")
INSIDE = ("grp", "mid")
F32 = jnp.float32
BF16 = jnp.bfloat16
ROOM = pltpu.CompilerParams(vmem_limit_bytes=58 * 2**20)


def cost(megabytes):
    return pl.CostEstimate(flops=10**6, bytes_accessed=megabytes * 10**6, transcendentals=0)


def passed_along(array, by):
    size = lax.axis_size(ALL)
    pairs = [(i, i + by) for i in range(size) if 0 <= i + by < size]
    return lax.ppermute(array, ALL, pairs)


def across(array, axis):
    return lax.ppermute(array, axis, [(0, 1), (1, 0)])


def swap_halves(array):
    return pltpu.roll(array, HALF, 1)


def low_lanes(rows):
    return lax.broadcasted_iota(jnp.int32, (rows, LANES), 1) < HALF


def times_transposed(left, right):
    return lax.dot_general(left, right, (((1,), (1,)), ((), ())), preferred_element_type=F32)


def own_columns(pieces):
    child = lax.broadcasted_iota(jnp.int32, (R, WIDE), 1) // U
    picked = pieces[0]
    for i in range(1, CHILDREN):
        picked = jnp.where(child == i, pieces[i], picked)
    return picked


def leaf_kernel(hi_ref, cur_ref, rad_ref, own_ref, other_ref):
    low_half = hi_ref[0] == 0
    boxes = cur_ref.shape[2] // WIDE
    low = low_lanes(2 * R)
    row_child = lax.broadcasted_iota(jnp.int32, (2 * R * CHILDREN, WIDE), 0) // (2 * R)
    col_child = lax.broadcasted_iota(jnp.int32, (2 * R * CHILDREN, WIDE), 1) // U
    diagonal = row_child == col_child
    for pair in range(boxes // 2):
        found = []
        for box in (2 * pair, 2 * pair + 1):
            cols = slice(box * WIDE, (box + 1) * WIDE)
            own = [cur_ref[0, :, cols].astype(F32), cur_ref[1, :, cols].astype(F32)]
            spread = jnp.where(diagonal, jnp.concatenate(own * CHILDREN, axis=0), 0.0)
            slab = jnp.concatenate([rad_ref[0, cols, :], rad_ref[1, cols, :]], axis=1)
            found.append(jnp.dot(spread.astype(BF16), slab, preferred_element_type=F32))
        for i in range(CHILDREN):
            by_real = jnp.concatenate([f[2 * R * i : 2 * R * i + R] for f in found], axis=0)
            by_imag = jnp.concatenate([f[2 * R * i + R : 2 * R * (i + 1)] for f in found], axis=0)
            real = by_real[:, :LANES] - by_imag[:, LANES:]
            imag = by_real[:, LANES:] + by_imag[:, :LANES]
            zero = jnp.where(low, real, swap_halves(imag))
            one = jnp.where(low, swap_halves(real), imag)
            rows = slice(pair * 2 * R, (pair + 1) * 2 * R)
            cols = slice(i * LANES, (i + 1) * LANES)
            own_ref[rows, cols] = jnp.where(low_half, zero, one).astype(BF16)
            other_ref[rows, cols] = jnp.where(low_half, one, zero).astype(BF16)


def leaves(hi, currents, radiation):
    width = currents.shape[2]
    rows = width // WIDE * R
    steps = 4
    per_step = width // steps
    shape = jax.ShapeDtypeStruct((rows, DEPTH), BF16)
    spec = pl.BlockSpec((rows // steps, DEPTH), lambda s, *_: (s, 0))
    return pl.pallas_call(
        leaf_kernel,
        grid_spec=pltpu.PrefetchScalarGridSpec(
            num_scalar_prefetch=1,
            grid=(steps,),
            in_specs=[
                pl.BlockSpec((2, R, per_step), lambda s, *_: (0, 0, s)),
                pl.BlockSpec((2, per_step, LANES), lambda s, *_: (0, s, 0)),
            ],
            out_specs=[spec, spec],
        ),
        out_shape=[shape, shape],
        compiler_params=ROOM,
        cost_estimate=cost(1),
        name="leaves",
    )(hi, currents, radiation)


def put_patterns(box_ref, patterns):
    boxes = patterns.shape[0] // R
    for chip in range(box_ref.shape[0]):
        real = patterns[:, 2 * chip * LANES : (2 * chip + 1) * LANES].reshape(boxes, 1, R, LANES)
        imag = patterns[:, (2 * chip + 1) * LANES : (2 * chip + 2) * LANES].reshape(boxes, 1, R, LANES)
        both = jnp.concatenate([real, imag], axis=1).reshape(boxes * 2 * R, LANES)
        box_ref[chip] = both.astype(BF16)


def up_kernel(lhs_ref, interp_ref, angle_ref, box_ref, mat_ref):
    cosine, sine = jnp.cos(angle_ref[...]), jnp.sin(angle_ref[...])
    for chip in range(box_ref.shape[0]):
        cols = slice(chip * LANES, (chip + 1) * LANES)
        to_real = slice(2 * chip * LANES, (2 * chip + 1) * LANES)
        to_imag = slice((2 * chip + 1) * LANES, (2 * chip + 2) * LANES)
        weights = interp_ref[:, cols].astype(F32)
        for i in range(CHILDREN):
            from_real = slice(2 * i * K0, (2 * i + 1) * K0)
            from_imag = slice((2 * i + 1) * K0, (2 * i + 2) * K0)
            even, odd = weights * cosine[i : i + 1, cols], weights * sine[i : i + 1, cols]
            mat_ref[from_real, to_real] = even.astype(BF16)
            mat_ref[from_real, to_imag] = odd.astype(BF16)
            mat_ref[from_imag, to_real] = (-odd).astype(BF16)
            mat_ref[from_imag, to_imag] = even.astype(BF16)
    put_patterns(box_ref, jnp.dot(lhs_ref[...], mat_ref[...], preferred_element_type=F32))


def again_kernel(lhs_ref, mat_ref, box_ref):
    put_patterns(box_ref, jnp.dot(lhs_ref[...], mat_ref[...], preferred_element_type=F32))


def to_boxes(lhs, interp, angle):
    rows = lhs.shape[0]
    steps = 4
    chips = CHIPS // steps
    return pl.pallas_call(
        up_kernel,
        grid=(steps,),
        in_specs=[
            pl.BlockSpec((rows, DEPTH), lambda s: (0, 0)),
            pl.BlockSpec((K0, chips * LANES), lambda s: (0, s)),
            pl.BlockSpec((CHILDREN, chips * LANES), lambda s: (0, s)),
        ],
        out_specs=[
            pl.BlockSpec((chips, 2 * rows, LANES), lambda s: (s, 0, 0)),
            pl.BlockSpec((DEPTH, 2 * chips * LANES), lambda s: (0, s)),
        ],
        out_shape=[
            jax.ShapeDtypeStruct((CHIPS, 2 * rows, LANES), BF16),
            jax.ShapeDtypeStruct((DEPTH, 2 * K1), BF16),
        ],
        compiler_params=ROOM,
        cost_estimate=cost(1),
        name="to_boxes",
    )(lhs, interp, angle)


def to_boxes_again(lhs, matrix):
    rows = lhs.shape[0]
    steps = 4
    chips = CHIPS // steps
    return pl.pallas_call(
        again_kernel,
        grid=(steps,),
        in_specs=[
            pl.BlockSpec((rows, DEPTH), lambda s: (0, 0)),
            pl.BlockSpec((DEPTH, 2 * chips * LANES), lambda s: (0, s)),
        ],
        out_specs=pl.BlockSpec((chips, 2 * rows, LANES), lambda s: (s, 0, 0)),
        out_shape=jax.ShapeDtypeStruct((CHIPS, 2 * rows, LANES), BF16),
        compiler_params=ROOM,
        cost_estimate=cost(70),
        name="to_boxes_again",
    )(lhs, matrix)


def translate_kernel(list_ref, oper_ref, one_ref, two_ref, three_ref, four_ref, out_ref, box_ref, table_ref, sems, *, group):
    step = pl.program_id(0)
    per_step = out_ref.shape[0]

    @pl.when(step == 0)
    def fetch():
        copies = []
        for at, source in enumerate((one_ref, two_ref, three_ref, four_ref)):
            boxes = source.shape[0]
            copies.append(pltpu.make_async_copy(source, box_ref.at[pl.ds(at * boxes, boxes)], sems.at[at]))
        for copy in copies:
            copy.start()

        def spread(at, _):
            for part in range(2):
                some = oper_ref[part, pl.ds(pl.multiple_of(at * R, R), R), :]
                for one in range(R):
                    table_ref[at * R + one, part] = jnp.broadcast_to(some[one : one + 1], (R, LANES))
            return 0

        lax.fori_loop(0, oper_ref.shape[1] // R, spread, 0)
        for copy in copies:
            copy.wait()

    def body(at, _):
        first = (step * per_step + at * group) * (2 * IL)
        done = []
        for k in range(group):
            real = imag = None
            for j in range(IL):
                entry = first + k * 2 * IL + j
                tile = box_ref[list_ref[entry]].astype(F32)
                offset = list_ref[entry + IL]
                by_real, by_imag = table_ref[offset, 0], table_ref[offset, 1]
                box_real, box_imag = tile[:R], tile[R:]
                one = by_real * box_real - by_imag * box_imag
                two = by_real * box_imag + by_imag * box_real
                real = one if j == 0 else real + one
                imag = two if j == 0 else imag + two
            done.append(jnp.concatenate([real, imag], axis=0).astype(BF16))
        for k in range(group):
            out_ref[at * group + k] = done[k]
        return 0

    lax.fori_loop(0, per_step // group, body, 0)


def translate(lists, operators, parts):
    targets = lists.shape[0] // (2 * IL)
    boxes = parts[0].shape[0]
    steps = 2
    per_step = targets // steps
    anywhere = pl.BlockSpec(memory_space=pl.ANY)
    return pl.pallas_call(
        functools.partial(translate_kernel, group=8),
        grid_spec=pltpu.PrefetchScalarGridSpec(
            num_scalar_prefetch=1,
            grid=(steps,),
            in_specs=[pl.BlockSpec(operators.shape, lambda s, *_: (0, 0, 0))] + [anywhere] * 4,
            out_specs=pl.BlockSpec((per_step, 2 * R, LANES), lambda s, *_: (s, 0, 0)),
            scratch_shapes=[
                pltpu.VMEM((4 * boxes, 2 * R, LANES), BF16),
                pltpu.VMEM((operators.shape[1], 2, R, LANES), F32),
                pltpu.SemaphoreType.DMA((4,)),
            ],
        ),
        out_shape=jax.ShapeDtypeStruct((targets, 2 * R, LANES), BF16),
        compiler_params=ROOM,
        cost_estimate=cost(25),
        name="translate",
    )(lists, operators, *parts)


def near_kernel(idx_ref, below_ref, own_ref, above_ref, blocks_ref, out_ref, table_ref, lhs_ref):
    step = pl.program_id(0)
    width = own_ref.shape[2]
    per_source = width // LANES
    clusters = blocks_ref.shape[1] // U
    per_tile = LANES // U
    place = lax.broadcasted_iota(jnp.int32, (2 * R, LANES), 1) // U

    @pl.when(step == 0)
    def fill():
        unrolled = 4
        for at, source in enumerate((below_ref, own_ref, above_ref)):

            def body(some, _):
                for one in range(unrolled):
                    tile = some * unrolled + one
                    cols = pl.ds(pl.multiple_of(tile * LANES, LANES), LANES)
                    parts = [source[0, :, cols].astype(F32), source[1, :, cols].astype(F32)]
                    whole = jnp.concatenate(parts, axis=0)
                    turned = [whole] + [pltpu.roll(whole, n * U, 1) for n in range(1, per_tile)]
                    for a in range(per_tile):
                        copied = turned[(0 - a) % per_tile]
                        for g in range(1, per_tile):
                            copied = jnp.where(place == g, turned[(g - a) % per_tile], copied)
                        table_ref[(at * per_source + tile) * per_tile + a] = copied
                return 0

            lax.fori_loop(0, per_source // unrolled, body, 0)
        table_ref[3 * per_source * per_tile] = jnp.zeros((2 * R, LANES), F32)

    def body(some, _):
        for one in range(CHILDREN):
            c = some * CHILDREN + one
            entry = (step * clusters + c) * NBR
            for half in range(NBR // per_tile):
                joined = table_ref[idx_ref[entry + half * per_tile]]
                for k in range(1, per_tile):
                    joined = jnp.where(place == k, table_ref[idx_ref[entry + half * per_tile + k]], joined)
                first = pl.multiple_of(c * 2 * R, 2 * R)
                lhs_ref[pl.ds(first, 2 * R), half * LANES : (half + 1) * LANES] = joined.astype(BF16)
        return 0

    lax.fori_loop(0, clusters // CHILDREN, body, 0)
    for box in range(clusters // CHILDREN):
        rows = slice(box * 2 * R * CHILDREN, (box + 1) * 2 * R * CHILDREN)
        cols = slice(box * WIDE, (box + 1) * WIDE)
        by_real = times_transposed(lhs_ref[rows, :], blocks_ref[0, cols, :])
        by_imag = times_transposed(lhs_ref[rows, :], blocks_ref[1, cols, :])
        real = []
        imag = []
        for i in range(CHILDREN):
            top = slice(2 * R * i, 2 * R * i + R)
            bottom = slice(2 * R * i + R, 2 * R * (i + 1))
            real.append(by_real[top] - by_imag[bottom])
            imag.append(by_imag[top] + by_real[bottom])
        out_ref[0, :, cols] = own_columns(real)
        out_ref[1, :, cols] = own_columns(imag)


def near_part(index, below, own, above, blocks):
    width = own.shape[2]
    steps = 8
    per_step = width // steps
    whole = pl.BlockSpec((2, R, width), lambda s, *_: (0, 0, 0))
    return pl.pallas_call(
        near_kernel,
        grid_spec=pltpu.PrefetchScalarGridSpec(
            num_scalar_prefetch=1,
            grid=(steps,),
            in_specs=[whole, whole, whole, pl.BlockSpec((2, per_step, NBR * U), lambda s, *_: (0, s, 0))],
            out_specs=pl.BlockSpec((2, R, per_step), lambda s, *_: (0, 0, s)),
            scratch_shapes=[
                pltpu.VMEM((3 * width // U + 1, 2 * R, LANES), F32),
                pltpu.VMEM((per_step // U * 2 * R, NBR * U), BF16),
            ],
        ),
        out_shape=jax.ShapeDtypeStruct((2, R, width), F32),
        compiler_params=ROOM,
        cost_estimate=cost(1),
        name="near_part",
    )(index, below, own, above, blocks)


def down_kernel(got_ref, mat_ref, out_ref, sum_ref):
    step = pl.program_id(0)
    last = pl.num_programs(0) - 1
    pieces = []
    for chip in range(got_ref.shape[0]):
        both = got_ref[chip].astype(F32).reshape(-1, 2, R, LANES)
        pieces += [both[:, 0].reshape(-1, LANES), both[:, 1].reshape(-1, LANES)]
    added = times_transposed(jnp.concatenate(pieces, axis=1).astype(BF16), mat_ref[...])

    @pl.when(step == 0)
    def begin():
        sum_ref[...] = added

    @pl.when(jnp.logical_and(step > 0, step < last))
    def go_on():
        sum_ref[...] += added

    @pl.when(step == last)
    def end():
        out_ref[...] = (sum_ref[...] + added).astype(BF16)


def from_boxes(received, matrix):
    rows = received.shape[1] // 2
    steps = 4
    chips = CHIPS // steps
    return pl.pallas_call(
        down_kernel,
        grid=(steps,),
        in_specs=[
            pl.BlockSpec((chips, 2 * rows, LANES), lambda s: (s, 0, 0)),
            pl.BlockSpec((DEPTH, 2 * chips * LANES), lambda s: (0, s)),
        ],
        out_specs=pl.BlockSpec((rows, DEPTH), lambda s: (0, 0)),
        out_shape=jax.ShapeDtypeStruct((rows, DEPTH), BF16),
        scratch_shapes=[pltpu.VMEM((rows, DEPTH), F32)],
        compiler_params=ROOM,
        cost_estimate=cost(1),
        name="from_boxes",
    )(received, matrix)


def far_kernel(hi_ref, own_ref, other_ref, rad_ref, near_ref, out_ref):
    low_half = hi_ref[0] == 0
    boxes = out_ref.shape[2] // WIDE
    low = low_lanes(2 * R)
    for pair in range(boxes // 2):
        rows = slice(pair * 2 * R, (pair + 1) * 2 * R)
        pieces = [[], []]
        for i in range(CHILDREN):
            cols = slice(i * LANES, (i + 1) * LANES)
            own, other = own_ref[rows, cols].astype(F32), other_ref[rows, cols].astype(F32)
            zero, one = jnp.where(low_half, own, other), jnp.where(low_half, other, own)
            real = jnp.where(low, zero, swap_halves(one))
            imag = jnp.where(low, swap_halves(zero), one)
            for k in range(2):
                part = slice(k * R, (k + 1) * R)
                pieces[k].append(jnp.concatenate([real[part], imag[part]], axis=1))
                pieces[k].append(jnp.concatenate([imag[part], -real[part]], axis=1))
        for k in range(2):
            fields = jnp.concatenate(pieces[k], axis=0).astype(BF16)
            cols = slice((2 * pair + k) * WIDE, (2 * pair + k + 1) * WIDE)
            slab = jnp.concatenate([rad_ref[0, cols, :], rad_ref[1, cols, :]], axis=1)
            terms = times_transposed(fields, slab)
            for part in range(2):
                own = [terms[2 * R * i + part * R : 2 * R * i + (part + 1) * R] for i in range(CHILDREN)]
                out_ref[part, :, cols] = near_ref[part, :, cols] + own_columns(own)


def far_part(hi, own, other, radiation, near_field):
    width = near_field.shape[2]
    rows = own.shape[0]
    steps = 4
    per_step = width // steps
    field = pl.BlockSpec((rows // steps, DEPTH), lambda s, *_: (s, 0))
    wave = pl.BlockSpec((2, R, per_step), lambda s, *_: (0, 0, s))
    return pl.pallas_call(
        far_kernel,
        grid_spec=pltpu.PrefetchScalarGridSpec(
            num_scalar_prefetch=1,
            grid=(steps,),
            in_specs=[field, field, pl.BlockSpec((2, per_step, LANES), lambda s, *_: (0, s, 0)), wave],
            out_specs=wave,
        ),
        out_shape=jax.ShapeDtypeStruct((2, R, width), F32),
        compiler_params=ROOM,
        cost_estimate=cost(1),
        name="far_part",
    )(hi, own, other, radiation, near_field)


def swapped(array):
    return lax.all_to_all(array, INSIDE, split_axis=0, concat_axis=0, tiled=True)


def padded(array):
    return jnp.pad(array, [(0, 0)] * (array.ndim - 1) + [(0, LANES - array.shape[-1])])


def to_owners(boxes, samples):
    rows = boxes.shape[1]
    if samples != LANES:
        boxes = boxes.reshape(CHIPS, rows, LANES // samples, samples).transpose(0, 2, 1, 3).reshape(-1, rows, samples)
    got = swapped(boxes)
    if samples != LANES:
        got = padded(got)
    return got.reshape(-1, 2 * R, LANES)


def from_owners(fields, rows, samples):
    fields = fields.reshape(-1, rows, LANES)
    if samples == LANES:
        return swapped(fields)
    got = swapped(fields[..., :samples]).reshape(CHIPS, LANES // samples, rows, samples)
    return got.transpose(0, 2, 1, 3).reshape(CHIPS, rows, LANES)


def operator_table(translation):
    groups, mids = lax.axis_size("grp"), lax.axis_size("mid")
    core = lax.axis_index("core")
    got = []
    for turned in range(2):
        pairs = [
            (((h * groups + g) * mids + m) * 2 + (c ^ turned), ((g * 2 + h) * mids + m) * 2 + c)
            for g in range(groups)
            for h in range(2)
            for m in range(mids)
            for c in range(2)
        ]
        got.append(lax.ppermute(translation, ALL, pairs).astype(F32))
    low = jnp.where(core == 0, got[0], got[1])
    high = jnp.where(core == 0, got[1], got[0])
    operator = padded(jnp.concatenate([low, high], axis=2))
    return jnp.pad(operator, ((0, 0), (0, -operator.shape[1] % R), (0, 0)))


def target_lists(trans_box, trans_off, hi, core):
    groups, mids = lax.axis_size("grp"), lax.axis_size("mid")
    total = trans_box.shape[0]
    per = total // (groups * mids * 4)
    device, inside = trans_box // per, trans_box % per
    group, side = device // (4 * mids), device // (2 * mids) % 2
    mid, its_core = device // 2 % mids, device % 2
    block = (side ^ hi) * 2 + (its_core ^ core)
    place = (block * (groups * mids) + group * mids + mid) * per + inside
    lists = jnp.concatenate([place, trans_off], axis=1).reshape(groups, 2, mids, 2, per, 2 * IL)
    lists = jnp.where(core == 0, lists[:, :, :, 0], lists[:, :, :, 1])
    first, second = lists[:, 0].reshape(-1), lists[:, 1].reshape(-1)
    return jnp.where(hi == 0, first, second), jnp.where(hi == 0, second, first)


def local(
    currents,
    near_blocks,
    near_list,
    near_count,
    radiation,
    interp,
    shift_angle,
    translation,
    trans_box,
    trans_off,
):
    clusters = near_list.shape[0]
    samples = 2 * translation.shape[2]
    rows = clusters // CHILDREN * 2 * R
    hi, core = lax.axis_index("hi"), lax.axis_index("core")
    side = hi.reshape(1).astype(jnp.int32)
    radiation = radiation.reshape(2, clusters * U, LANES)
    near_blocks = near_blocks.reshape(2, clusters * U, NBR * U)

    below = passed_along(currents, 1)
    above = passed_along(currents, -1)
    first = (lax.axis_index(ALL) - 1) * clusters
    live = jnp.arange(NBR, dtype=jnp.int32)[None, :] < near_count[:, None]
    index = jnp.where(live, near_list - first, 3 * clusters).reshape(-1)

    leaf_own, leaf_other = leaves(side, currents, radiation)
    leaf_partner = across(leaf_other, "hi")
    boxes_own, matrix = to_boxes(leaf_own, interp, shift_angle)
    rows_own = to_owners(boxes_own, samples)
    swapped_own = across(rows_own, "core")
    near_field = near_part(index, below, currents, above, near_blocks)
    leaf_partner, near_field = lax.optimization_barrier((leaf_partner, near_field))
    rows_partner = to_owners(to_boxes_again(leaf_partner, matrix), samples)
    parts = (rows_own, swapped_own, rows_partner, across(rows_partner, "core"))

    operators = operator_table(translation)
    list_own, list_partner = target_lists(trans_box, trans_off, hi, core)
    fields_partner = translate(list_partner, operators, parts)
    down_partner = from_boxes(from_owners(fields_partner, rows, samples), matrix)
    down_other = across(down_partner, "hi")
    fields_own = translate(list_own, operators, parts)
    down_own = from_boxes(from_owners(fields_own, rows, samples), matrix)
    return far_part(side, down_own, down_other, radiation, near_field)


def solution(mesh):
    devices = mesh.devices
    groups, rest = devices.shape
    cut = Mesh(devices.reshape(groups, 2, rest // 4, 2), ALL)
    placed = (
        P(None, None, ALL),
        P(None, ALL, None, None),
        P(ALL, None),
        P(ALL),
        P(None, ALL, None, None),
        P(),
        P(),
        P(None, None, ALL),
        P(),
        P(),
    )
    return jax.shard_map(local, mesh=cut, in_specs=placed, out_specs=P(None, None, ALL), check_vma=False)
```

time: 626 us -> 175 us (0.28)
  local copies, waits for them, and re-layouts: 405 us -> 11.6 us
  other arithmetic: 93.6 us -> 3.19 us
  Pallas kernels: 0 us -> 69.3 us
  matrix products: 57.8 us -> 0 us
  starting transfers between devices: 17.2 us -> 51.1 us
  waiting for transfers between devices: 45.2 us -> 37.5 us
    gather x48 -> x0, local copies, waits for them, and re-layouts: 244 us -> none  [the longest x12 61 us: turn(): oper_imag = jnp.take(operator_imag, offsets, axis=0).astype(jnp.float32)]
    pallas_call x0 -> x9, Pallas kernels: none -> 69.3 us  [the longest x2 23.8 us: translate(): pl.pallas_call(functools.partial(translate_kernel, group=8), grid_spec=pl...]
    add x13 -> x1, other arithmetic: 62.7 us -> 0.24 us  [target_lists(): place = (block * (groups * mids) + group * mids + mid) * per + inside]
    dot_general x15 -> x0, matrix products: 57.8 us -> none  [the longest x12 33.4 us: product(): jnp.einsum(pattern, left_side, right_side, preferred_element_type=jnp.flo...]
    slice x12 -> x1, local copies, waits for them, and re-layouts: 39.9 us -> 1.08 us  [target_lists(): lists = jnp.where(core == 0, lists[:, :, :, 0], lists[:, :, :, 1])]
    unnamed x32 -> x33, local copies, waits for them, and re-layouts: 39.2 us -> 7.98 us
    all_to_all x2 -> x4, starting transfers between devices: 12.9 us -> 40.5 us  [swapped(): lax.all_to_all(array, INSIDE, split_axis=0, concat_axis=0, tiled=True)]
    another operation x57 -> x0, local copies, waits for them, and re-layouts: 20.9 us -> none  [the longest x3 11.1 us: aggregate(): summed = jnp.stack([real_part.sum(axis=2), imag_part.sum(axis=2)])]
  transfers between devices with their start and end apart: 4 -> 12, of which waited for: 1 -> 5; matrix products, arithmetic and copies ran while one was open for 68% -> 6% of each run, Pallas kernels for 0% -> 25%
where the time goes in v1:
time: 175 us; the launch traced here: 173 us
  Pallas kernels  69.3 us (40%)
  starting transfers between devices  51.1 us (29%)
  waiting for transfers between devices  37.5 us (21%)
  local copies, waits for them, and re-layouts  11.6 us (7%)
  other arithmetic  3.19 us (2%)
    all_to_all x4, starting transfers between devices, swapped(): lax.all_to_all(array, INSIDE, split_axis=0, concat_axis=0, tiled=True)  40.5 us
    all_to_all x4, waiting for transfers between devices, swapped(): lax.all_to_all(array, INSIDE, split_axis=0, concat_axis=0, tiled=True)  31 us
    pallas_call x2, Pallas kernels, translate(): pl.pallas_call(functools.partial(translate_kernel, group=8), grid_spec=pl...  23.8 us
    pallas_call x1, Pallas kernels, near_part(): pl.pallas_call(near_kernel, grid_spec=pltpu.PrefetchScalarGridSpec(num_sc...  15.7 us
    pallas_call x2, Pallas kernels, from_boxes(): pl.pallas_call(down_kernel, grid=(steps,), in_specs=[pl.BlockSpec((chips,...  10.3 us
    unnamed x33, local copies, waits for them, and re-layouts  7.98 us
    pallas_call x1, Pallas kernels, far_part(): pl.pallas_call(far_kernel, grid_spec=pltpu.PrefetchScalarGridSpec(num_sca...  5.09 us
    pallas_call x1, Pallas kernels, to_boxes_again(): pl.pallas_call(again_kernel, grid=(steps,), in_specs=[pl.BlockSpec((rows,...  4.96 us
  transfers between devices with their start and end apart: 12, of which 5 were waited for; matrix products, arithmetic and copies ran while one was open for 6% of the time, Pallas kernels for 25%

profile of v1, /device:TPU:0, one launch (start us, length us, event | category | flops | bytes accessed | tf_op | source)
XLA Modules:
  0.0 172.9 jit_solution(1347640387923229826)
XLA Ops:
  0.0 4.8 %leaves.1 = (bf16[256,1024]{1,0:T(8,128)(2,1)}, bf16[256,1024]{1,0:T(8,128)(2,1)}) custom-call(s32[1]{0:T(128)} %bitcast.hi_ref, bf16[2,8,8192]{2,1,0:T(8,128)(2,1)} %own_ref.1, bf16[2,8192,128]{2,1,0:T(8,128)(2,1)} %bitcast.19), custom_call_target="tpu_custom_call" | custom-call | flops 1000000 | bytes 1000000 | tf_op jit(solution)/shard_map/leaves/pallas_call | solution.py:99
  4.8 4.6 %to_boxes.1 = (bf16[8,512,128]{2,1,0:T(8,128)(2,1)}, bf16[1024,2048]{1,0:T(8,128)(2,1)}) custom-call(bf16[256,1024]{1,0:T(8,128)(2,1)} %get-tuple-element.11.lhs_ref, bf16[64,1024]{1,0:T(8,128)(2,1)} %interp_ref.1, f32[8,1024]{1,0:T(8,128)} %angle_ref.1), custom_call_target="tpu_custom_call" | custom-call | flops 1000000 | bytes 1000000 | tf_op jit(solution)/shard_map/to_boxes/pallas_call | solution.py:152
  9.4 6.2 %all-to-all-start = ((bf16[8,512,128]{2,1,0:T(8,128)(2,1)}), bf16[8,512,128]{2,1,0:T(8,128)(2,1)S(1)}, u32[]{:S(2)}, u32[]{:S(2)}) async-start(bf16[8,512,128]{2,1,0:T(8,128)(2,1)} %get-tuple-element.12), calls=%async_computation | async-start | bytes 2097152 | tf_op jit(solution)/shard_map/all_to_all | solution.py:441
  15.6 2.6 %collective-permute-start.3 = (bf16[256,1024]{1,0:T(8,128)(2,1)}, bf16[256,1024]{1,0:T(8,128)(2,1)S(1)}, u32[]{:S(2)}, u32[]{:S(2)}) collective-permute-start(bf16[256,1024]{1,0:T(8,128)(2,1)} %get-tuple-element.13), channel_id=1, source_target_pairs={{0,4},{4,0},{1,5},{5,1},{2,6},{6,2},{3,7},{7,3},{8,12},{12,8},{9,1... | collective-permute-start | bytes 1572872 | tf_op jit(solution)/shard_map/ppermute | solution.py:41
  18.2 1.3 collective-permute-start.4
  19.5 1.3 collective-permute-start.5
  21.7 3.5 %collective-permute-done.5.above_ref = bf16[2,8,8192]{2,1,0:T(8,128)(2,1)S(1)} collective-permute-done((bf16[2,8,8192]{2,1,0:T(8,128)(2,1)S(1)}, bf16[2,8,8192]{2,1,0:T(8,128)(2,1)S(1)}, u32[]{:S(2)}, u32[]{:S(2)}) %collective-permute-start.5) | collective-permute-done | bytes 262176 | tf_op jit(solution)/shard_map/ppermute | solution.py:37
  25.9 15.7 %near_part.1.near_ref = f32[2,8,8192]{2,1,0:T(8,128)} custom-call(s32[2048]{0:T(1024)} %reshape.38.idx_ref, bf16[2,8,8192]{2,1,0:T(8,128)(2,1)} %copy-done.8, bf16[2,8,8192]{2,1,0:T(8,128)(2,1)} %own_ref.1, bf16[2,8,8192]{2,1,0:T(8,128)(2,1)} %copy-done.9, bf16[2,8192,256]{2,1,0:T(8,128)(2,1)} %bitcast.27), custom_call_target="tpu_custom_call" | custom-call | flops 1000000 | bytes 1000000 | tf_op jit(solution)/shard_map/near_part/pallas_call | solution.py:330
  42.4 5.0 %to_boxes_again.1 = bf16[8,512,128]{2,1,0:T(8,128)(2,1)} custom-call(bf16[256,1024]{1,0:T(8,128)(2,1)} %copy-done.7, bf16[1024,2048]{1,0:T(8,128)(2,1)} %get-tuple-element.15.mat_ref), custom_call_target="tpu_custom_call" | custom-call | flops 1000000 | bytes 70000000 | tf_op jit(solution)/shard_map/to_boxes_again/pallas_call | solution.py:178
  47.4 25.2 %all-to-all-start.1 = ((bf16[8,512,128]{2,1,0:T(8,128)(2,1)}), bf16[8,512,128]{2,1,0:T(8,128)(2,1)S(1)}, u32[]{:S(2)}, u32[]{:S(2)}) async-start(bf16[8,512,128]{2,1,0:T(8,128)(2,1)} %to_boxes_again.1), calls=%async_computation.1 | async-start | bytes 2097152 | tf_op jit(solution)/shard_map/all_to_all | solution.py:441
  74.0 2.9 %collective-permute-start = (bf16[2,316,64]{2,1,0:T(8,128)(2,1)}, bf16[2,316,64]{2,1,0:T(8,128)(2,1)}, u32[]{:S(2)}, u32[]{:S(2)}) collective-permute-start(bf16[2,316,64]{2,1,0:T(8,128)(2,1)} %copy.15), channel_id=1, source_target_pairs={{0,0},{1,1},{2,2},{3,3},{16,4},{17,5},{18,6},{19,7},{4,8},{5,9},{6... | collective-permute-start | bytes 242696 | tf_op jit(solution)/shard_map/ppermute | solution.py:478
  77.6 15.1 %all-to-all-done.1 = bf16[8,512,128]{2,1,0:T(8,128)(2,1)S(1)} async-done(((bf16[8,512,128]{2,1,0:T(8,128)(2,1)}), bf16[8,512,128]{2,1,0:T(8,128)(2,1)S(1)}, u32[]{:S(2)}, u32[]{:S(2)}) %all-to-all-start.1) | async-done | bytes 1048608 | tf_op jit(solution)/shard_map/all_to_all | solution.py:441
  94.8 1.8 %copy.18 = s32[4,2,2,1,32,24]{5,4,2,0,1,3:T(8,128)} copy(s32[4,2,2,1,32,24]{4,3,2,1,0,5:T(1,128)} %get-tuple-element.18) | data formatting | bytes 98304
  101.2 11.9 %translate.3 = bf16[256,16,128]{2,1,0:T(8,128)(2,1)} custom-call(s32[6144]{0:T(1024)} %select_n.95.list_ref, f32[2,320,128]{2,1,0:T(8,128)} %select_maximum_fusion.oper_ref, bf16[256,16,128]{2,1,0:T(8,128)(2,1)} %bitcast.22, bf16[256,16,128]{2,1,0:T(8,128)(2,1)} %copy-done.4, bf16[256,16,128]{2,1,0:T(8,128)(2,1)} %bitcast.25, ...), custom_call_target="tpu_custom_call" | custom-call | flops 1000000 | bytes 25000000 | tf_op jit(solution)/shard_map/translate/pallas_call | solution.py:246
  113.1 5.5 %all-to-all-start.3 = ((bf16[8,512,128]{2,1,0:T(8,128)(2,1)}), bf16[8,512,128]{2,1,0:T(8,128)(2,1)S(1)}, u32[]{:S(2)}, u32[]{:S(2)}) async-start(bf16[8,512,128]{2,1,0:T(8,128)(2,1)} %bitcast.29), calls=%async_computation.3 | async-start | bytes 2097152 | tf_op jit(solution)/shard_map/all_to_all | solution.py:441
  119.3 11.9 %translate.2 = bf16[256,16,128]{2,1,0:T(8,128)(2,1)} custom-call(s32[6144]{0:T(1024)} %select_n.89.list_ref, f32[2,320,128]{2,1,0:T(8,128)} %select_maximum_fusion.oper_ref, bf16[256,16,128]{2,1,0:T(8,128)(2,1)} %bitcast.23, bf16[256,16,128]{2,1,0:T(8,128)(2,1)} %copy-done.4, bf16[256,16,128]{2,1,0:T(8,128)(2,1)} %bitcast.26, ...), custom_call_target="tpu_custom_call" | custom-call | flops 1000000 | bytes 25000000 | tf_op jit(solution)/shard_map/translate/pallas_call | solution.py:246
  131.2 2.4 %all-to-all-done.3.got_ref = bf16[8,512,128]{2,1,0:T(8,128)(2,1)S(1)} async-done(((bf16[8,512,128]{2,1,0:T(8,128)(2,1)}), bf16[8,512,128]{2,1,0:T(8,128)(2,1)S(1)}, u32[]{:S(2)}, u32[]{:S(2)}) %all-to-all-start.3) | async-done | bytes 1048608 | tf_op jit(solution)/shard_map/all_to_all | solution.py:441
  133.7 3.6 %all-to-all-start.2 = ((bf16[8,512,128]{2,1,0:T(8,128)(2,1)}), bf16[8,512,128]{2,1,0:T(8,128)(2,1)S(1)}, u32[]{:S(2)}, u32[]{:S(2)}) async-start(bf16[8,512,128]{2,1,0:T(8,128)(2,1)} %bitcast.28), calls=%async_computation.2 | async-start | bytes 2097152 | tf_op jit(solution)/shard_map/all_to_all | solution.py:441
  137.2 5.2 %from_boxes.3 = bf16[256,1024]{1,0:T(8,128)(2,1)} custom-call(bf16[8,512,128]{2,1,0:T(8,128)(2,1)} %copy-done.2, bf16[1024,2048]{1,0:T(8,128)(2,1)} %get-tuple-element.15.mat_ref), custom_call_target="tpu_custom_call" | custom-call | flops 1000000 | bytes 1000000 | tf_op jit(solution)/shard_map/from_boxes/pallas_call | solution.py:375
  142.4 1.9 %collective-permute-start.7 = (bf16[256,1024]{1,0:T(8,128)(2,1)}, bf16[256,1024]{1,0:T(8,128)(2,1)S(1)}, u32[]{:S(2)}, u32[]{:S(2)}) collective-permute-start(bf16[256,1024]{1,0:T(8,128)(2,1)} %from_boxes.3), channel_id=1, source_target_pairs={{0,4},{4,0},{1,5},{5,1},{2,6},{6,2},{3,7},{7,3},{8,12},{12,8},{9,1... | collective-permute-start | bytes 1572872 | tf_op jit(solution)/shard_map/ppermute | solution.py:41
  144.4 13.4 %all-to-all-done.2.got_ref = bf16[8,512,128]{2,1,0:T(8,128)(2,1)S(1)} async-done(((bf16[8,512,128]{2,1,0:T(8,128)(2,1)}), bf16[8,512,128]{2,1,0:T(8,128)(2,1)S(1)}, u32[]{:S(2)}, u32[]{:S(2)}) %all-to-all-start.2) | async-done | bytes 1048608 | tf_op jit(solution)/shard_map/all_to_all | solution.py:441
  158.8 5.2 %from_boxes.2.own_ref = bf16[256,1024]{1,0:T(8,128)(2,1)} custom-call(bf16[8,512,128]{2,1,0:T(8,128)(2,1)} %copy-done.3, bf16[1024,2048]{1,0:T(8,128)(2,1)} %get-tuple-element.15.mat_ref), custom_call_target="tpu_custom_call" | custom-call | flops 1000000 | bytes 1000000 | tf_op jit(solution)/shard_map/from_boxes/pallas_call | solution.py:375
  164.0 3.0 %collective-permute-done.7.other_ref = bf16[256,1024]{1,0:T(8,128)(2,1)S(1)} collective-permute-done((bf16[256,1024]{1,0:T(8,128)(2,1)}, bf16[256,1024]{1,0:T(8,128)(2,1)S(1)}, u32[]{:S(2)}, u32[]{:S(2)}) %collective-permute-start.7) | collective-permute-done | bytes 524320 | tf_op jit(solution)/shard_map/ppermute | solution.py:41
  167.8 5.1 %far_part.1 = f32[2,8,8192]{2,1,0:T(8,128)} custom-call(s32[1]{0:T(128)} %bitcast.hi_ref, bf16[256,1024]{1,0:T(8,128)(2,1)} %from_boxes.2.own_ref, bf16[256,1024]{1,0:T(8,128)(2,1)} %copy-done.6, bf16[2,8192,128]{2,1,0:T(8,128)(2,1)} %bitcast.20, f32[2,8,8192]{2,1,0:T(8,128)} %near_part.1.near_ref), custom_call_target="tpu_custom_call" | custom-call | flops 1000000 | bytes 1000000 | tf_op jit(solution)/shard_map/far_part/pallas_call | solution.py:425
  (55 shorter events, 13.7 us)
Async XLA Ops:
  0.0 18.2 %copy-start.5 = (bf16[2,8,8192]{2,1,0:T(8,128)(2,1)S(1)}, bf16[2,8,8192]{2,1,0:T(8,128)(2,1)}, u32[]{:S(2)}) copy-start(bf16[2,8,8192]{2,1,0:T(8,128)(2,1)} %own_ref.1) | copy-start | bytes 786436
  0.0 20.8 %copy-start.14 = (s32[256]{0:T(256)S(1)}, s32[256]{0:T(256)}, u32[]{:S(2)}) copy-start(s32[256]{0:T(256)} %param.13) | copy-start | bytes 3076
  0.0 20.8 %copy-start.13 = (s32[256,8]{0,1:T(8,128)S(1)}, s32[256,8]{0,1:T(8,128)}, u32[]{:S(2)}) copy-start(s32[256,8]{0,1:T(8,128)} %param.12) | copy-start | bytes 24580
  9.4 38.0 %all-to-all-start = ((bf16[8,512,128]{2,1,0:T(8,128)(2,1)}), bf16[8,512,128]{2,1,0:T(8,128)(2,1)S(1)}, u32[]{:S(2)}, u32[]{:S(2)}) async-start(bf16[8,512,128]{2,1,0:T(8,128)(2,1)} %get-tuple-element.12), calls=%async_computation | async-start | bytes 2097152 | tf_op jit(solution)/shard_map/all_to_all | solution.py:441
  15.6 26.0 %collective-permute-start.3 = (bf16[256,1024]{1,0:T(8,128)(2,1)}, bf16[256,1024]{1,0:T(8,128)(2,1)S(1)}, u32[]{:S(2)}, u32[]{:S(2)}) collective-permute-start(bf16[256,1024]{1,0:T(8,128)(2,1)} %get-tuple-element.13), channel_id=1, source_target_pairs={{0,4},{4,0},{1,5},{5,1},{2,6},{6,2},{3,7},{7,3},{8,12},{12,8},{9,1... | collective-permute-start | bytes 1572872 | tf_op jit(solution)/shard_map/ppermute | solution.py:41
  18.2 3.5 %collective-permute-start.4 = (bf16[2,8,8192]{2,1,0:T(8,128)(2,1)S(1)}, bf16[2,8,8192]{2,1,0:T(8,128)(2,1)S(1)}, u32[]{:S(2)}, u32[]{:S(2)}) collective-permute-start(bf16[2,8,8192]{2,1,0:T(8,128)(2,1)S(1)} %copy-done.5), channel_id=1, source_target_pairs={{0,1},{1,2},{2,3},{3,4},{4,5},{5,6},{6,7},{7,8},{8,9},{9,10},{10,1... | collective-permute-start | bytes 786440 | tf_op jit(solution)/shard_map/ppermute | solution.py:37
  19.5 5.7 %collective-permute-start.5 = (bf16[2,8,8192]{2,1,0:T(8,128)(2,1)S(1)}, bf16[2,8,8192]{2,1,0:T(8,128)(2,1)S(1)}, u32[]{:S(2)}, u32[]{:S(2)}) collective-permute-start(bf16[2,8,8192]{2,1,0:T(8,128)(2,1)S(1)} %copy-done.5), channel_id=1, source_target_pairs={{1,0},{2,1},{3,2},{4,3},{5,4},{6,5},{7,6},{8,7},{9,8},{10,9},{11,1... | collective-permute-start | bytes 786440 | tf_op jit(solution)/shard_map/ppermute | solution.py:37
  21.7 3.5 %copy-start.8 = (bf16[2,8,8192]{2,1,0:T(8,128)(2,1)}, bf16[2,8,8192]{2,1,0:T(8,128)(2,1)S(1)}, u32[]{:S(2)}) copy-start(bf16[2,8,8192]{2,1,0:T(8,128)(2,1)S(1)} %collective-permute-done.4.below_ref) | copy-start | bytes 786436
  41.6 31.0 %copy-start.10 = (bf16[2,316,64]{1,2,0:T(8,128)(2,1)S(1)}, bf16[2,316,64]{1,2,0:T(8,128)(2,1)}, u32[]{:S(2)}) copy-start(bf16[2,316,64]{1,2,0:T(8,128)(2,1)} %param.17) | copy-start | bytes 242692
  41.6 35.2 %copy-start.12 = (s32[1024,12]{0,1:T(8,128)S(1)}, s32[1024,12]{0,1:T(8,128)}, u32[]{:S(2)}) copy-start(s32[1024,12]{0,1:T(8,128)} %param.18) | copy-start | bytes 147460
  41.6 35.5 %copy-start.11 = (s32[1024,12]{0,1:T(8,128)S(1)}, s32[1024,12]{0,1:T(8,128)}, u32[]{:S(2)}) copy-start(s32[1024,12]{0,1:T(8,128)} %param.19) | copy-start | bytes 147460
  47.4 52.8 %copy-start = (bf16[8,512,128]{2,1,0:T(8,128)(2,1)}, bf16[8,512,128]{2,1,0:T(8,128)(2,1)S(1)}, u32[]{:S(2)}) copy-start(bf16[8,512,128]{2,1,0:T(8,128)(2,1)S(1)} %all-to-all-done) | copy-start | bytes 3145732
  47.4 45.2 %all-to-all-start.1 = ((bf16[8,512,128]{2,1,0:T(8,128)(2,1)}), bf16[8,512,128]{2,1,0:T(8,128)(2,1)S(1)}, u32[]{:S(2)}, u32[]{:S(2)}) async-start(bf16[8,512,128]{2,1,0:T(8,128)(2,1)} %to_boxes_again.1), calls=%async_computation.1 | async-start | bytes 2097152 | tf_op jit(solution)/shard_map/all_to_all | solution.py:441
  73.4 24.9 %collective-permute-start.1 = (bf16[2,316,64]{2,1,0:T(8,128)(2,1)}, bf16[2,316,64]{2,1,0:T(8,128)(2,1)}, u32[]{:S(2)}, u32[]{:S(2)}) collective-permute-start(bf16[2,316,64]{2,1,0:T(8,128)(2,1)} %copy.15), channel_id=1, source_target_pairs={{1,0},{0,1},{3,2},{2,3},{17,4},{16,5},{19,6},{18,7},{5,8},{4,9},{7... | collective-permute-start | bytes 242696 | tf_op jit(solution)/shard_map/ppermute | solution.py:478
  74.0 24.3 %collective-permute-start = (bf16[2,316,64]{2,1,0:T(8,128)(2,1)}, bf16[2,316,64]{2,1,0:T(8,128)(2,1)}, u32[]{:S(2)}, u32[]{:S(2)}) collective-permute-start(bf16[2,316,64]{2,1,0:T(8,128)(2,1)} %copy.15), channel_id=1, source_target_pairs={{0,0},{1,1},{2,2},{3,3},{16,4},{17,5},{18,6},{19,7},{4,8},{5,9},{6... | collective-permute-start | bytes 242696 | tf_op jit(solution)/shard_map/ppermute | solution.py:478
  77.5 22.8 %collective-permute-start.2 = (bf16[256,16,128]{2,1,0:T(8,128)(2,1)S(1)}, bf16[256,16,128]{2,1,0:T(8,128)(2,1)S(1)}, u32[]{:S(2)}, u32[]{:S(2)}) collective-permute-start(bf16[256,16,128]{2,1,0:T(8,128)(2,1)S(1)} %bitcast.21), channel_id=1, source_target_pairs={{0,1},{1,0},{2,3},{3,2},{4,5},{5,4},{6,7},{7,6},{8,9},{9,8},{10,11... | collective-permute-start | bytes 3145736 | tf_op jit(solution)/shard_map/ppermute | solution.py:41
  92.6 7.6 %copy-start.1 = (bf16[8,512,128]{2,1,0:T(8,128)(2,1)}, bf16[8,512,128]{2,1,0:T(8,128)(2,1)S(1)}, u32[]{:S(2)}) copy-start(bf16[8,512,128]{2,1,0:T(8,128)(2,1)S(1)} %all-to-all-done.1) | copy-start | bytes 3145732
  92.6 7.6 %collective-permute-start.6 = (bf16[256,16,128]{2,1,0:T(8,128)(2,1)S(1)}, bf16[256,16,128]{2,1,0:T(8,128)(2,1)}, u32[]{:S(2)}, u32[]{:S(2)}) collective-permute-start(bf16[256,16,128]{2,1,0:T(8,128)(2,1)S(1)} %bitcast.24), channel_id=1, source_target_pairs={{0,1},{1,0},{2,3},{3,2},{4,5},{5,4},{6,7},{7,6},{8,9},{9,8},{10,11... | collective-permute-start | bytes 3145736 | tf_op jit(solution)/shard_map/ppermute | solution.py:41
  100.2 1.0 copy-start.4
  113.1 20.6 %all-to-all-start.3 = ((bf16[8,512,128]{2,1,0:T(8,128)(2,1)}), bf16[8,512,128]{2,1,0:T(8,128)(2,1)S(1)}, u32[]{:S(2)}, u32[]{:S(2)}) async-start(bf16[8,512,128]{2,1,0:T(8,128)(2,1)} %bitcast.29), calls=%async_computation.3 | async-start | bytes 2097152 | tf_op jit(solution)/shard_map/all_to_all | solution.py:441
  133.7 3.6 %copy-start.2 = (bf16[8,512,128]{2,1,0:T(8,128)(2,1)}, bf16[8,512,128]{2,1,0:T(8,128)(2,1)S(1)}, u32[]{:S(2)}) copy-start(bf16[8,512,128]{2,1,0:T(8,128)(2,1)S(1)} %all-to-all-done.3.got_ref) | copy-start | bytes 3145732
  133.7 24.1 %all-to-all-start.2 = ((bf16[8,512,128]{2,1,0:T(8,128)(2,1)}), bf16[8,512,128]{2,1,0:T(8,128)(2,1)S(1)}, u32[]{:S(2)}, u32[]{:S(2)}) async-start(bf16[8,512,128]{2,1,0:T(8,128)(2,1)} %bitcast.28), calls=%async_computation.2 | async-start | bytes 2097152 | tf_op jit(solution)/shard_map/all_to_all | solution.py:441
  142.4 24.6 %collective-permute-start.7 = (bf16[256,1024]{1,0:T(8,128)(2,1)}, bf16[256,1024]{1,0:T(8,128)(2,1)S(1)}, u32[]{:S(2)}, u32[]{:S(2)}) collective-permute-start(bf16[256,1024]{1,0:T(8,128)(2,1)} %from_boxes.3), channel_id=1, source_target_pairs={{0,4},{4,0},{1,5},{5,1},{2,6},{6,2},{3,7},{7,3},{8,12},{12,8},{9,1... | collective-permute-start | bytes 1572872 | tf_op jit(solution)/shard_map/ppermute | solution.py:41
  157.8 1.0 copy-start.3
  (3 other events, 2.3 us)

commit v2 on v1

--- a/solution.py
+++ b/solution.py
@@ -185,7 +185,7 @@
         out_specs=pl.BlockSpec((chips, 2 * rows, LANES), lambda s: (s, 0, 0)),
         out_shape=jax.ShapeDtypeStruct((CHIPS, 2 * rows, LANES), BF16),
         compiler_params=ROOM,
-        cost_estimate=cost(70),
+        cost_estimate=cost(4000),
         name="to_boxes_again",
     )(lhs, matrix)
 
@@ -517,28 +517,33 @@
     radiation = radiation.reshape(2, clusters * U, LANES)
     near_blocks = near_blocks.reshape(2, clusters * U, NBR * U)
 
-    below = passed_along(currents, 1)
-    above = passed_along(currents, -1)
     first = (lax.axis_index(ALL) - 1) * clusters
     live = jnp.arange(NBR, dtype=jnp.int32)[None, :] < near_count[:, None]
     index = jnp.where(live, near_list - first, 3 * clusters).reshape(-1)
+    lists = target_lists(trans_box, trans_off, hi, core)
 
     leaf_own, leaf_other = leaves(side, currents, radiation)
     leaf_partner = across(leaf_other, "hi")
     boxes_own, matrix = to_boxes(leaf_own, interp, shift_angle)
     rows_own = to_owners(boxes_own, samples)
     swapped_own = across(rows_own, "core")
+
+    leaf_partner, lists, index, late_currents, translation = lax.optimization_barrier(
+        (leaf_partner, lists, index, currents, translation)
+    )
+    rows_partner = to_owners(to_boxes_again(leaf_partner, matrix), samples)
+    below = passed_along(late_currents, 1)
+    above = passed_along(late_currents, -1)
+    operators = operator_table(translation)
+    parts = (rows_own, swapped_own, rows_partner, across(rows_partner, "core"))
+    parts, operators, below, above = lax.optimization_barrier((parts, operators, below, above))
+
+    fields_partner = translate(lists[1], operators, parts)
+    down_partner = from_boxes(from_owners(fields_partner, rows, samples), matrix)
+    fields_own = translate(lists[0], operators, parts)
+    down_partner, index = lax.optimization_barrier((down_partner, index))
+    down_other = across(down_partner, "hi")
     near_field = near_part(index, below, currents, above, near_blocks)
-    leaf_partner, near_field = lax.optimization_barrier((leaf_partner, near_field))
-    rows_partner = to_owners(to_boxes_again(leaf_partner, matrix), samples)
-    parts = (rows_own, swapped_own, rows_partner, across(rows_partner, "core"))
-
-    operators = operator_table(translation)
-    list_own, list_partner = target_lists(trans_box, trans_off, hi, core)
-    fields_partner = translate(list_partner, operators, parts)
-    down_partner = from_boxes(from_owners(fields_partner, rows, samples), matrix)
-    down_other = across(down_partner, "hi")
-    fields_own = translate(list_own, operators, parts)
     down_own = from_boxes(from_owners(fields_own, rows, samples), matrix)
     return far_part(side, down_own, down_other, radiation, near_field)
 

time: 175 us -> 166 us (0.949)
  waiting for transfers between devices: 37.5 us -> 32.2 us
  local copies, waits for them, and re-layouts: 11.6 us -> 8.45 us
  starting transfers between devices: 51.1 us -> 53.4 us
  other arithmetic: 3.19 us -> 1.25 us
    all_to_all x4, waiting for transfers between devices: 31 us -> 14.8 us  [swapped(): lax.all_to_all(array, INSIDE, split_axis=0, concat_axis=0, tiled=True)]
    ppermute x4, waiting for transfers between devices: 3.01 us -> 17.2 us  [across(): return lax.ppermute(array, axis, [(0, 1), (1, 0)])]
    unnamed x33 -> x32, local copies, waits for them, and re-layouts: 7.98 us -> 4.61 us
    ppermute x2, waiting for transfers between devices: 3.48 us -> 0.18 us  [passed_along(): return lax.ppermute(array, ALL, pairs)]
  transfers between devices with their start and end apart: 12 -> 12, of which waited for: 5 -> 5; matrix products, arithmetic and copies ran while one was open for 6% -> 3% of each run, Pallas kernels for 25% -> 26%
where the time goes in v2:
time: 166 us; the launch traced here: 165 us
  Pallas kernels  69.3 us (42%)
  starting transfers between devices  53.4 us (32%)
  waiting for transfers between devices  32.2 us (19%)
  local copies, waits for them, and re-layouts  8.45 us (5%)
    all_to_all x4, starting transfers between devices, swapped(): lax.all_to_all(array, INSIDE, split_axis=0, concat_axis=0, tiled=True)  41.1 us
    pallas_call x2, Pallas kernels, translate(): pl.pallas_call(functools.partial(translate_kernel, group=8), grid_spec=pl...  23.7 us
    ppermute x4, waiting for transfers between devices, across(): return lax.ppermute(array, axis, [(0, 1), (1, 0)])  17.2 us
    pallas_call x1, Pallas kernels, near_part(): pl.pallas_call(near_kernel, grid_spec=pltpu.PrefetchScalarGridSpec(num_sc...  15.7 us
    all_to_all x4, waiting for transfers between devices, swapped(): lax.all_to_all(array, INSIDE, split_axis=0, concat_axis=0, tiled=True)  14.8 us
    pallas_call x2, Pallas kernels, from_boxes(): pl.pallas_call(down_kernel, grid=(steps,), in_specs=[pl.BlockSpec((chips,...  10.4 us
    ppermute x4, starting transfers between devices, across(): return lax.ppermute(array, axis, [(0, 1), (1, 0)])  5.97 us
    pallas_call x1, Pallas kernels, far_part(): pl.pallas_call(far_kernel, grid_spec=pltpu.PrefetchScalarGridSpec(num_sca...  5.09 us
  transfers between devices with their start and end apart: 12, of which 5 were waited for; matrix products, arithmetic and copies ran while one was open for 3% of the time, Pallas kernels for 26%

profile of v2, /device:TPU:0, one launch (start us, length us, event | category | flops | bytes accessed | tf_op | source)
XLA Modules:
  0.0 164.8 jit_solution(15030613808218155904)
XLA Ops:
  0.0 4.8 %leaves.1 = (bf16[256,1024]{1,0:T(8,128)(2,1)}, bf16[256,1024]{1,0:T(8,128)(2,1)}) custom-call(s32[1]{0:T(128)} %bitcast.hi_ref, bf16[2,8,8192]{2,1,0:T(8,128)(2,1)} %own_ref.1, bf16[2,8192,128]{2,1,0:T(8,128)(2,1)} %bitcast.19), custom_call_target="tpu_custom_call" | custom-call | flops 1000000 | bytes 1000000 | tf_op jit(solution)/shard_map/leaves/pallas_call | solution.py:99
  4.8 4.6 %to_boxes.1 = (bf16[8,512,128]{2,1,0:T(8,128)(2,1)}, bf16[1024,2048]{1,0:T(8,128)(2,1)}) custom-call(bf16[256,1024]{1,0:T(8,128)(2,1)} %get-tuple-element.26.lhs_ref, bf16[64,1024]{1,0:T(8,128)(2,1)} %interp_ref.1, f32[8,1024]{1,0:T(8,128)} %angle_ref.1), custom_call_target="tpu_custom_call" | custom-call | flops 1000000 | bytes 1000000 | tf_op jit(solution)/shard_map/to_boxes/pallas_call | solution.py:152
  9.4 6.2 %all-to-all-start = ((bf16[8,512,128]{2,1,0:T(8,128)(2,1)}), bf16[8,512,128]{2,1,0:T(8,128)(2,1)S(1)}, u32[]{:S(2)}, u32[]{:S(2)}) async-start(bf16[8,512,128]{2,1,0:T(8,128)(2,1)} %get-tuple-element.27), calls=%async_computation | async-start | bytes 2097152 | tf_op jit(solution)/shard_map/all_to_all | solution.py:441
  15.6 2.6 %collective-permute-start = (bf16[256,1024]{1,0:T(8,128)(2,1)}, bf16[256,1024]{1,0:T(8,128)(2,1)S(1)}, u32[]{:S(2)}, u32[]{:S(2)}) collective-permute-start(bf16[256,1024]{1,0:T(8,128)(2,1)} %get-tuple-element.24), channel_id=1, source_target_pairs={{0,4},{4,0},{1,5},{5,1},{2,6},{6,2},{3,7},{7,3},{8,12},{12,8},{9,1... | collective-permute-start | bytes 1572872 | tf_op jit(solution)/shard_map/ppermute | solution.py:41
  21.9 16.6 %collective-permute-done.lhs_ref = bf16[256,1024]{1,0:T(8,128)(2,1)S(1)} collective-permute-done((bf16[256,1024]{1,0:T(8,128)(2,1)}, bf16[256,1024]{1,0:T(8,128)(2,1)S(1)}, u32[]{:S(2)}, u32[]{:S(2)}) %collective-permute-start) | collective-permute-done | bytes 524320 | tf_op jit(solution)/shard_map/ppermute | solution.py:41
  39.3 5.0 %to_boxes_again.1 = bf16[8,512,128]{2,1,0:T(8,128)(2,1)} custom-call(bf16[256,1024]{1,0:T(8,128)(2,1)} %copy-done.7, bf16[1024,2048]{1,0:T(8,128)(2,1)} %get-tuple-element.29.mat_ref), custom_call_target="tpu_custom_call" | custom-call | flops 1000000 | bytes 4000000000 | tf_op jit(solution)/shard_map/to_boxes_again/pallas_call | solution.py:178
  44.2 7.7 %all-to-all-start.1 = ((bf16[8,512,128]{2,1,0:T(8,128)(2,1)}), bf16[8,512,128]{2,1,0:T(8,128)(2,1)S(1)}, u32[]{:S(2)}, u32[]{:S(2)}) async-start(bf16[8,512,128]{2,1,0:T(8,128)(2,1)} %to_boxes_again.1), calls=%async_computation.1 | async-start | bytes 2097152 | tf_op jit(solution)/shard_map/all_to_all | solution.py:441
  51.9 14.2 %all-to-all-done.1 = bf16[8,512,128]{2,1,0:T(8,128)(2,1)S(1)} async-done(((bf16[8,512,128]{2,1,0:T(8,128)(2,1)}), bf16[8,512,128]{2,1,0:T(8,128)(2,1)S(1)}, u32[]{:S(2)}, u32[]{:S(2)}) %all-to-all-start.1) | async-done | bytes 1048608 | tf_op jit(solution)/shard_map/all_to_all | solution.py:441
  66.2 1.0 copy.16
  67.5 1.6 collective-permute-start.3
  69.0 1.3 collective-permute-start.6
  70.3 3.0 %collective-permute-start.5 = (bf16[2,8,8192]{2,1,0:T(8,128)(2,1)S(1)}, bf16[2,8,8192]{2,1,0:T(8,128)(2,1)S(1)}, u32[]{:S(2)}, u32[]{:S(2)}) collective-permute-start(bf16[2,8,8192]{2,1,0:T(8,128)(2,1)S(1)} %copy-done.5), channel_id=1, source_target_pairs={{0,1},{1,2},{2,3},{3,4},{4,5},{5,6},{6,7},{7,8},{8,9},{9,10},{10,1... | collective-permute-start | bytes 786440 | tf_op jit(solution)/shard_map/ppermute | solution.py:37
  73.5 0.9 select_maximum_fusion.oper_ref
  75.2 0.9 copy-done.4
  76.2 11.9 %translate.3 = bf16[256,16,128]{2,1,0:T(8,128)(2,1)} custom-call(s32[6144]{0:T(1024)} %select_n.93.list_ref, f32[2,320,128]{2,1,0:T(8,128)} %select_maximum_fusion.oper_ref, bf16[256,16,128]{2,1,0:T(8,128)(2,1)} %bitcast.22, bf16[256,16,128]{2,1,0:T(8,128)(2,1)} %copy-done.4, bf16[256,16,128]{2,1,0:T(8,128)(2,1)} %bitcast.25, ...), custom_call_target="tpu_custom_call" | custom-call | flops 1000000 | bytes 25000000 | tf_op jit(solution)/shard_map/translate/pallas_call | solution.py:246
  88.1 22.7 %all-to-all-start.3 = ((bf16[8,512,128]{2,1,0:T(8,128)(2,1)}), bf16[8,512,128]{2,1,0:T(8,128)(2,1)S(1)}, u32[]{:S(2)}, u32[]{:S(2)}) async-start(bf16[8,512,128]{2,1,0:T(8,128)(2,1)} %bitcast.29), calls=%async_computation.3 | async-start | bytes 2097152 | tf_op jit(solution)/shard_map/all_to_all | solution.py:441
  110.8 11.9 %translate.2 = bf16[256,16,128]{2,1,0:T(8,128)(2,1)} custom-call(s32[6144]{0:T(1024)} %select_n.91.list_ref, f32[2,320,128]{2,1,0:T(8,128)} %select_maximum_fusion.oper_ref, bf16[256,16,128]{2,1,0:T(8,128)(2,1)} %bitcast.23, bf16[256,16,128]{2,1,0:T(8,128)(2,1)} %copy-done.4, bf16[256,16,128]{2,1,0:T(8,128)(2,1)} %bitcast.26, ...), custom_call_target="tpu_custom_call" | custom-call | flops 1000000 | bytes 25000000 | tf_op jit(solution)/shard_map/translate/pallas_call | solution.py:246
  123.2 4.5 %all-to-all-start.2 = ((bf16[8,512,128]{2,1,0:T(8,128)(2,1)}), bf16[8,512,128]{2,1,0:T(8,128)(2,1)S(1)}, u32[]{:S(2)}, u32[]{:S(2)}) async-start(bf16[8,512,128]{2,1,0:T(8,128)(2,1)} %bitcast.28), calls=%async_computation.2 | async-start | bytes 2097152 | tf_op jit(solution)/shard_map/all_to_all | solution.py:441
  127.8 5.2 %from_boxes.3 = bf16[256,1024]{1,0:T(8,128)(2,1)} custom-call(bf16[8,512,128]{2,1,0:T(8,128)(2,1)} %copy-done.2, bf16[1024,2048]{1,0:T(8,128)(2,1)} %get-tuple-element.29.mat_ref), custom_call_target="tpu_custom_call" | custom-call | flops 1000000 | bytes 1000000 | tf_op jit(solution)/shard_map/from_boxes/pallas_call | solution.py:375
  133.0 3.4 %collective-permute-start.7 = (bf16[256,1024]{1,0:T(8,128)(2,1)}, bf16[256,1024]{1,0:T(8,128)(2,1)S(1)}, u32[]{:S(2)}, u32[]{:S(2)}) collective-permute-start(bf16[256,1024]{1,0:T(8,128)(2,1)} %from_boxes.3), channel_id=1, source_target_pairs={{0,4},{4,0},{1,5},{5,1},{2,6},{6,2},{3,7},{7,3},{8,12},{12,8},{9,1... | collective-permute-start | bytes 1572872 | tf_op jit(solution)/shard_map/ppermute | solution.py:41
  136.3 15.7 %near_part.1.near_ref = f32[2,8,8192]{2,1,0:T(8,128)} custom-call(s32[2048]{0:T(1024)} %reshape.37.idx_ref, bf16[2,8,8192]{2,1,0:T(8,128)(2,1)} %copy-done.9, bf16[2,8,8192]{2,1,0:T(8,128)(2,1)} %own_ref.1, bf16[2,8,8192]{2,1,0:T(8,128)(2,1)} %copy-done.8, bf16[2,8192,256]{2,1,0:T(8,128)(2,1)} %bitcast.27), custom_call_target="tpu_custom_call" | custom-call | flops 1000000 | bytes 1000000 | tf_op jit(solution)/shard_map/near_part/pallas_call | solution.py:330
  152.1 1.0 copy-done.3
  153.1 5.2 %from_boxes.2.own_ref = bf16[256,1024]{1,0:T(8,128)(2,1)} custom-call(bf16[8,512,128]{2,1,0:T(8,128)(2,1)} %copy-done.3, bf16[1024,2048]{1,0:T(8,128)(2,1)} %get-tuple-element.29.mat_ref), custom_call_target="tpu_custom_call" | custom-call | flops 1000000 | bytes 1000000 | tf_op jit(solution)/shard_map/from_boxes/pallas_call | solution.py:375
  159.7 5.1 %far_part.1 = f32[2,8,8192]{2,1,0:T(8,128)} custom-call(s32[1]{0:T(128)} %bitcast.hi_ref, bf16[256,1024]{1,0:T(8,128)(2,1)} %from_boxes.2.own_ref, bf16[256,1024]{1,0:T(8,128)(2,1)} %copy-done.6, bf16[2,8192,128]{2,1,0:T(8,128)(2,1)} %bitcast.20, f32[2,8,8192]{2,1,0:T(8,128)} %near_part.1.near_ref), custom_call_target="tpu_custom_call" | custom-call | flops 1000000 | bytes 1000000 | tf_op jit(solution)/shard_map/far_part/pallas_call | solution.py:425
  (55 shorter events, 7.7 us)
Async XLA Ops:
  0.0 18.2 %copy-start.12 = (s32[1024,12]{0,1:T(8,128)S(1)}, s32[1024,12]{0,1:T(8,128)}, u32[]{:S(2)}) copy-start(s32[1024,12]{0,1:T(8,128)} %param.18) | copy-start | bytes 147460
  0.0 18.5 %copy-start.11 = (s32[1024,12]{0,1:T(8,128)S(1)}, s32[1024,12]{0,1:T(8,128)}, u32[]{:S(2)}) copy-start(s32[1024,12]{0,1:T(8,128)} %param.19) | copy-start | bytes 147460
  0.0 19.2 %copy-start.13 = (s32[256,8]{0,1:T(8,128)S(1)}, s32[256,8]{0,1:T(8,128)}, u32[]{:S(2)}) copy-start(s32[256,8]{0,1:T(8,128)} %param.12) | copy-start | bytes 24580
  0.0 19.2 %copy-start.14 = (s32[256]{0:T(256)S(1)}, s32[256]{0:T(256)}, u32[]{:S(2)}) copy-start(s32[256]{0:T(256)} %param.13) | copy-start | bytes 3076
  9.4 34.8 %all-to-all-start = ((bf16[8,512,128]{2,1,0:T(8,128)(2,1)}), bf16[8,512,128]{2,1,0:T(8,128)(2,1)S(1)}, u32[]{:S(2)}, u32[]{:S(2)}) async-start(bf16[8,512,128]{2,1,0:T(8,128)(2,1)} %get-tuple-element.27), calls=%async_computation | async-start | bytes 2097152 | tf_op jit(solution)/shard_map/all_to_all | solution.py:441
  15.6 22.8 %collective-permute-start = (bf16[256,1024]{1,0:T(8,128)(2,1)}, bf16[256,1024]{1,0:T(8,128)(2,1)S(1)}, u32[]{:S(2)}, u32[]{:S(2)}) collective-permute-start(bf16[256,1024]{1,0:T(8,128)(2,1)} %get-tuple-element.24), channel_id=1, source_target_pairs={{0,4},{4,0},{1,5},{5,1},{2,6},{6,2},{3,7},{7,3},{8,12},{12,8},{9,1... | collective-permute-start | bytes 1572872 | tf_op jit(solution)/shard_map/ppermute | solution.py:41
  20.4 45.7 %copy-start.10 = (bf16[2,316,64]{1,2,0:T(8,128)(2,1)S(1)}, bf16[2,316,64]{1,2,0:T(8,128)(2,1)}, u32[]{:S(2)}) copy-start(bf16[2,316,64]{1,2,0:T(8,128)(2,1)} %param.17) | copy-start | bytes 242692
  20.4 48.6 %copy-start.5 = (bf16[2,8,8192]{2,1,0:T(8,128)(2,1)S(1)}, bf16[2,8,8192]{2,1,0:T(8,128)(2,1)}, u32[]{:S(2)}) copy-start(bf16[2,8,8192]{2,1,0:T(8,128)(2,1)} %own_ref.1) | copy-start | bytes 786436
  44.2 31.0 %copy-start = (bf16[8,512,128]{2,1,0:T(8,128)(2,1)}, bf16[8,512,128]{2,1,0:T(8,128)(2,1)S(1)}, u32[]{:S(2)}) copy-start(bf16[8,512,128]{2,1,0:T(8,128)(2,1)S(1)} %all-to-all-done) | copy-start | bytes 3145732
  44.2 21.9 %all-to-all-start.1 = ((bf16[8,512,128]{2,1,0:T(8,128)(2,1)}), bf16[8,512,128]{2,1,0:T(8,128)(2,1)S(1)}, u32[]{:S(2)}, u32[]{:S(2)}) async-start(bf16[8,512,128]{2,1,0:T(8,128)(2,1)} %to_boxes_again.1), calls=%async_computation.1 | async-start | bytes 2097152 | tf_op jit(solution)/shard_map/all_to_all | solution.py:441
  51.9 22.6 %collective-permute-start.1 = (bf16[256,16,128]{2,1,0:T(8,128)(2,1)S(1)}, bf16[256,16,128]{2,1,0:T(8,128)(2,1)S(1)}, u32[]{:S(2)}, u32[]{:S(2)}) collective-permute-start(bf16[256,16,128]{2,1,0:T(8,128)(2,1)S(1)} %bitcast.21), channel_id=1, source_target_pairs={{0,1},{1,0},{2,3},{3,2},{4,5},{5,4},{6,7},{7,6},{8,9},{9,8},{10,11... | collective-permute-start | bytes 3145736 | tf_op jit(solution)/shard_map/ppermute | solution.py:41
  66.1 9.1 %copy-start.1 = (bf16[8,512,128]{2,1,0:T(8,128)(2,1)}, bf16[8,512,128]{2,1,0:T(8,128)(2,1)S(1)}, u32[]{:S(2)}) copy-start(bf16[8,512,128]{2,1,0:T(8,128)(2,1)S(1)} %all-to-all-done.1) | copy-start | bytes 3145732
  66.1 9.1 %collective-permute-start.2 = (bf16[256,16,128]{2,1,0:T(8,128)(2,1)S(1)}, bf16[256,16,128]{2,1,0:T(8,128)(2,1)}, u32[]{:S(2)}, u32[]{:S(2)}) collective-permute-start(bf16[256,16,128]{2,1,0:T(8,128)(2,1)S(1)} %bitcast.24), channel_id=1, source_target_pairs={{0,1},{1,0},{2,3},{3,2},{4,5},{5,4},{6,7},{7,6},{8,9},{9,8},{10,11... | collective-permute-start | bytes 3145736 | tf_op jit(solution)/shard_map/ppermute | solution.py:41
  67.1 3.2 %collective-permute-start.4 = (bf16[2,316,64]{2,1,0:T(8,128)(2,1)}, bf16[2,316,64]{2,1,0:T(8,128)(2,1)S(1)}, u32[]{:S(2)}, u32[]{:S(2)}) collective-permute-start(bf16[2,316,64]{2,1,0:T(8,128)(2,1)} %copy.16), channel_id=1, source_target_pairs={{1,0},{0,1},{3,2},{2,3},{17,4},{16,5},{19,6},{18,7},{5,8},{4,9},{7... | collective-permute-start | bytes 242696 | tf_op jit(solution)/shard_map/ppermute | solution.py:478
  67.5 5.9 %collective-permute-start.3 = (bf16[2,316,64]{2,1,0:T(8,128)(2,1)}, bf16[2,316,64]{2,1,0:T(8,128)(2,1)S(1)}, u32[]{:S(2)}, u32[]{:S(2)}) collective-permute-start(bf16[2,316,64]{2,1,0:T(8,128)(2,1)} %copy.16), channel_id=1, source_target_pairs={{0,0},{1,1},{2,2},{3,3},{16,4},{17,5},{18,6},{19,7},{4,8},{5,9},{6... | collective-permute-start | bytes 242696 | tf_op jit(solution)/shard_map/ppermute | solution.py:478
  69.0 5.3 %collective-permute-start.6 = (bf16[2,8,8192]{2,1,0:T(8,128)(2,1)S(1)}, bf16[2,8,8192]{2,1,0:T(8,128)(2,1)S(1)}, u32[]{:S(2)}, u32[]{:S(2)}) collective-permute-start(bf16[2,8,8192]{2,1,0:T(8,128)(2,1)S(1)} %copy-done.5), channel_id=1, source_target_pairs={{1,0},{2,1},{3,2},{4,3},{5,4},{6,5},{7,6},{8,7},{9,8},{10,9},{11,1... | collective-permute-start | bytes 786440 | tf_op jit(solution)/shard_map/ppermute | solution.py:37
  70.3 4.2 %collective-permute-start.5 = (bf16[2,8,8192]{2,1,0:T(8,128)(2,1)S(1)}, bf16[2,8,8192]{2,1,0:T(8,128)(2,1)S(1)}, u32[]{:S(2)}, u32[]{:S(2)}) collective-permute-start(bf16[2,8,8192]{2,1,0:T(8,128)(2,1)S(1)} %copy-done.5), channel_id=1, source_target_pairs={{0,1},{1,2},{2,3},{3,4},{4,5},{5,6},{6,7},{7,8},{8,9},{9,10},{10,1... | collective-permute-start | bytes 786440 | tf_op jit(solution)/shard_map/ppermute | solution.py:37
  75.2 1.0 copy-start.4
  88.1 35.1 %all-to-all-start.3 = ((bf16[8,512,128]{2,1,0:T(8,128)(2,1)}), bf16[8,512,128]{2,1,0:T(8,128)(2,1)S(1)}, u32[]{:S(2)}, u32[]{:S(2)}) async-start(bf16[8,512,128]{2,1,0:T(8,128)(2,1)} %bitcast.29), calls=%async_computation.3 | async-start | bytes 2097152 | tf_op jit(solution)/shard_map/all_to_all | solution.py:441
  123.2 4.6 %copy-start.2 = (bf16[8,512,128]{2,1,0:T(8,128)(2,1)}, bf16[8,512,128]{2,1,0:T(8,128)(2,1)S(1)}, u32[]{:S(2)}) copy-start(bf16[8,512,128]{2,1,0:T(8,128)(2,1)S(1)} %all-to-all-done.3.got_ref) | copy-start | bytes 3145732
  123.2 28.9 %all-to-all-start.2 = ((bf16[8,512,128]{2,1,0:T(8,128)(2,1)}), bf16[8,512,128]{2,1,0:T(8,128)(2,1)S(1)}, u32[]{:S(2)}, u32[]{:S(2)}) async-start(bf16[8,512,128]{2,1,0:T(8,128)(2,1)} %bitcast.28), calls=%async_computation.2 | async-start | bytes 2097152 | tf_op jit(solution)/shard_map/all_to_all | solution.py:441
  133.0 25.9 %collective-permute-start.7 = (bf16[256,1024]{1,0:T(8,128)(2,1)}, bf16[256,1024]{1,0:T(8,128)(2,1)S(1)}, u32[]{:S(2)}, u32[]{:S(2)}) collective-permute-start(bf16[256,1024]{1,0:T(8,128)(2,1)} %from_boxes.3), channel_id=1, source_target_pairs={{0,4},{4,0},{1,5},{5,1},{2,6},{6,2},{3,7},{7,3},{8,12},{12,8},{9,1... | collective-permute-start | bytes 1572872 | tf_op jit(solution)/shard_map/ppermute | solution.py:41
  152.1 1.0 copy-start.3
  158.9 0.8 copy-start.6
  (3 other events, 2.2 us)

commit v3 on v2

--- a/solution.py
+++ b/solution.py
@@ -185,7 +185,7 @@
         out_specs=pl.BlockSpec((chips, 2 * rows, LANES), lambda s: (s, 0, 0)),
         out_shape=jax.ShapeDtypeStruct((CHIPS, 2 * rows, LANES), BF16),
         compiler_params=ROOM,
-        cost_estimate=cost(4000),
+        cost_estimate=cost(6),
         name="to_boxes_again",
     )(lhs, matrix)
 
@@ -535,8 +535,8 @@
     below = passed_along(late_currents, 1)
     above = passed_along(late_currents, -1)
     operators = operator_table(translation)
+    rows_partner, operators, below, above = lax.optimization_barrier((rows_partner, operators, below, above))
     parts = (rows_own, swapped_own, rows_partner, across(rows_partner, "core"))
-    parts, operators, below, above = lax.optimization_barrier((parts, operators, below, above))
 
     fields_partner = translate(lists[1], operators, parts)
     down_partner = from_boxes(from_owners(fields_partner, rows, samples), matrix)

time: 166 us -> 154 us (0.928)
  starting transfers between devices: 53.4 us -> 40.1 us
  waiting for transfers between devices: 32.2 us -> 34.1 us
    all_to_all x4, starting transfers between devices: 41.1 us -> 21.4 us  [swapped(): lax.all_to_all(array, INSIDE, split_axis=0, concat_axis=0, tiled=True)]
    ppermute x4, starting transfers between devices: 5.97 us -> 13 us  [across(): return lax.ppermute(array, axis, [(0, 1), (1, 0)])]
    ppermute x4, waiting for transfers between devices: 17.2 us -> 19.8 us  [across(): return lax.ppermute(array, axis, [(0, 1), (1, 0)])]
  transfers between devices with their start and end apart: 12 -> 12, of which waited for: 5 -> 5; matrix products, arithmetic and copies ran while one was open for 3% -> 3% of each run, Pallas kernels for 26% -> 28%
where the time goes in v3:
time: 154 us; the launch traced here: 153 us
  Pallas kernels  69.3 us (45%)
  starting transfers between devices  40.1 us (26%)
  waiting for transfers between devices  34.1 us (22%)
  local copies, waits for them, and re-layouts  7.67 us (5%)
    pallas_call x2, Pallas kernels, translate(): pl.pallas_call(functools.partial(translate_kernel, group=8), grid_spec=pl...  23.7 us
    all_to_all x4, starting transfers between devices, swapped(): lax.all_to_all(array, INSIDE, split_axis=0, concat_axis=0, tiled=True)  21.4 us
    ppermute x4, waiting for transfers between devices, across(): return lax.ppermute(array, axis, [(0, 1), (1, 0)])  19.8 us
    pallas_call x1, Pallas kernels, near_part(): pl.pallas_call(near_kernel, grid_spec=pltpu.PrefetchScalarGridSpec(num_sc...  15.8 us
    all_to_all x4, waiting for transfers between devices, swapped(): lax.all_to_all(array, INSIDE, split_axis=0, concat_axis=0, tiled=True)  14.3 us
    ppermute x4, starting transfers between devices, across(): return lax.ppermute(array, axis, [(0, 1), (1, 0)])  13 us
    pallas_call x2, Pallas kernels, from_boxes(): pl.pallas_call(down_kernel, grid=(steps,), in_specs=[pl.BlockSpec((chips,...  10.4 us
    pallas_call x1, Pallas kernels, far_part(): pl.pallas_call(far_kernel, grid_spec=pltpu.PrefetchScalarGridSpec(num_sca...  5.09 us
  transfers between devices with their start and end apart: 12, of which 5 were waited for; matrix products, arithmetic and copies ran while one was open for 3% of the time, Pallas kernels for 28%

profile of v3, /device:TPU:0, one launch (start us, length us, event | category | flops | bytes accessed | tf_op | source)
XLA Modules:
  0.0 152.7 jit_solution(3905179989715871186)
XLA Ops:
  0.0 4.8 %leaves.1 = (bf16[256,1024]{1,0:T(8,128)(2,1)}, bf16[256,1024]{1,0:T(8,128)(2,1)}) custom-call(s32[1]{0:T(128)} %bitcast.hi_ref, bf16[2,8,8192]{2,1,0:T(8,128)(2,1)} %own_ref.1, bf16[2,8192,128]{2,1,0:T(8,128)(2,1)} %bitcast.19), custom_call_target="tpu_custom_call" | custom-call | flops 1000000 | bytes 1000000 | tf_op jit(solution)/shard_map/leaves/pallas_call | solution.py:99
  4.8 4.6 %to_boxes.1 = (bf16[8,512,128]{2,1,0:T(8,128)(2,1)}, bf16[1024,2048]{1,0:T(8,128)(2,1)}) custom-call(bf16[256,1024]{1,0:T(8,128)(2,1)} %get-tuple-element.24.lhs_ref, bf16[64,1024]{1,0:T(8,128)(2,1)} %interp_ref.1, f32[8,1024]{1,0:T(8,128)} %angle_ref.1), custom_call_target="tpu_custom_call" | custom-call | flops 1000000 | bytes 1000000 | tf_op jit(solution)/shard_map/to_boxes/pallas_call | solution.py:152
  9.4 6.2 %all-to-all-start.1 = ((bf16[8,512,128]{2,1,0:T(8,128)(2,1)}), bf16[8,512,128]{2,1,0:T(8,128)(2,1)S(1)}, u32[]{:S(2)}, u32[]{:S(2)}) async-start(bf16[8,512,128]{2,1,0:T(8,128)(2,1)} %get-tuple-element.29), calls=%async_computation.1 | async-start | bytes 2097152 | tf_op jit(solution)/shard_map/all_to_all | solution.py:441
  15.6 2.6 %collective-permute-start = (bf16[256,1024]{1,0:T(8,128)(2,1)}, bf16[256,1024]{1,0:T(8,128)(2,1)S(1)}, u32[]{:S(2)}, u32[]{:S(2)}) collective-permute-start(bf16[256,1024]{1,0:T(8,128)(2,1)} %get-tuple-element.21), channel_id=1, source_target_pairs={{0,4},{4,0},{1,5},{5,1},{2,6},{6,2},{3,7},{7,3},{8,12},{12,8},{9,1... | collective-permute-start | bytes 1572872 | tf_op jit(solution)/shard_map/ppermute | solution.py:41
  21.9 16.6 %collective-permute-done.lhs_ref = bf16[256,1024]{1,0:T(8,128)(2,1)S(1)} collective-permute-done((bf16[256,1024]{1,0:T(8,128)(2,1)}, bf16[256,1024]{1,0:T(8,128)(2,1)S(1)}, u32[]{:S(2)}, u32[]{:S(2)}) %collective-permute-start) | collective-permute-done | bytes 524320 | tf_op jit(solution)/shard_map/ppermute | solution.py:41
  39.3 5.0 %to_boxes_again.1 = bf16[8,512,128]{2,1,0:T(8,128)(2,1)} custom-call(bf16[256,1024]{1,0:T(8,128)(2,1)} %copy-done.8, bf16[1024,2048]{1,0:T(8,128)(2,1)} %get-tuple-element.25.mat_ref), custom_call_target="tpu_custom_call" | custom-call | flops 1000000 | bytes 6000000 | tf_op jit(solution)/shard_map/to_boxes_again/pallas_call | solution.py:178
  44.2 7.7 %all-to-all-start = ((bf16[8,512,128]{2,1,0:T(8,128)(2,1)}), bf16[8,512,128]{2,1,0:T(8,128)(2,1)S(1)}, u32[]{:S(2)}, u32[]{:S(2)}) async-start(bf16[8,512,128]{2,1,0:T(8,128)(2,1)} %to_boxes_again.1), calls=%async_computation | async-start | bytes 2097152 | tf_op jit(solution)/shard_map/all_to_all | solution.py:441
  52.8 1.3 collective-permute-start.4
  54.1 3.8 %collective-permute-start.3 = (bf16[2,8,8192]{2,1,0:T(8,128)(2,1)S(1)}, bf16[2,8,8192]{2,1,0:T(8,128)(2,1)}, u32[]{:S(2)}, u32[]{:S(2)}) collective-permute-start(bf16[2,8,8192]{2,1,0:T(8,128)(2,1)S(1)} %copy-done.6), channel_id=1, source_target_pairs={{0,1},{1,2},{2,3},{3,4},{4,5},{5,6},{6,7},{7,8},{8,9},{9,10},{10,1... | collective-permute-start | bytes 786440 | tf_op jit(solution)/shard_map/ppermute | solution.py:37
  58.8 1.0 collective-permute-start.5
  60.6 10.4 %all-to-all-done = bf16[8,512,128]{2,1,0:T(8,128)(2,1)S(1)} async-done(((bf16[8,512,128]{2,1,0:T(8,128)(2,1)}), bf16[8,512,128]{2,1,0:T(8,128)(2,1)S(1)}, u32[]{:S(2)}, u32[]{:S(2)}) %all-to-all-start) | async-done | bytes 1048608 | tf_op jit(solution)/shard_map/all_to_all | solution.py:441
  71.0 6.9 %collective-permute-start.6 = (bf16[256,16,128]{2,1,0:T(8,128)(2,1)S(1)}, bf16[256,16,128]{2,1,0:T(8,128)(2,1)S(1)}, u32[]{:S(2)}, u32[]{:S(2)}) collective-permute-start(bf16[256,16,128]{2,1,0:T(8,128)(2,1)S(1)} %bitcast.24), channel_id=1, source_target_pairs={{0,1},{1,0},{2,3},{3,2},{4,5},{5,4},{6,7},{7,6},{8,9},{9,8},{10,11... | collective-permute-start | bytes 3145736 | tf_op jit(solution)/shard_map/ppermute | solution.py:41
  77.8 2.3 %collective-permute-done.6.four_ref = bf16[256,16,128]{2,1,0:T(8,128)(2,1)S(1)} collective-permute-done((bf16[256,16,128]{2,1,0:T(8,128)(2,1)S(1)}, bf16[256,16,128]{2,1,0:T(8,128)(2,1)S(1)}, u32[]{:S(2)}, u32[]{:S(2)}) %collective-permute-start.6) | collective-permute-done | bytes 1048608 | tf_op jit(solution)/shard_map/ppermute | solution.py:41
  81.1 11.9 %translate.3 = bf16[256,16,128]{2,1,0:T(8,128)(2,1)} custom-call(s32[6144]{0:T(1024)} %select_n.93.list_ref, f32[2,320,128]{2,1,0:T(8,128)} %select_maximum_fusion.oper_ref, bf16[256,16,128]{2,1,0:T(8,128)(2,1)} %bitcast.22, bf16[256,16,128]{2,1,0:T(8,128)(2,1)} %copy-done.4, bf16[256,16,128]{2,1,0:T(8,128)(2,1)} %bitcast.25, bf16[256,16,128]{2,1,0:T(8,128)(2,1)} %copy-done.5), custom_call_target="tpu_custom_call" | custom-call | flops 1000000 | bytes 25000000 | tf_op jit(solution)/shard_map/translate/pallas_call | solution.py:246
  93.0 3.9 %all-to-all-start.3 = ((bf16[8,512,128]{2,1,0:T(8,128)(2,1)}), bf16[8,512,128]{2,1,0:T(8,128)(2,1)S(1)}, u32[]{:S(2)}, u32[]{:S(2)}) async-start(bf16[8,512,128]{2,1,0:T(8,128)(2,1)} %bitcast.29), calls=%async_computation.3 | async-start | bytes 2097152 | tf_op jit(solution)/shard_map/all_to_all | solution.py:441
  96.9 11.9 %translate.2 = bf16[256,16,128]{2,1,0:T(8,128)(2,1)} custom-call(s32[6144]{0:T(1024)} %select_n.91.list_ref, f32[2,320,128]{2,1,0:T(8,128)} %select_maximum_fusion.oper_ref, bf16[256,16,128]{2,1,0:T(8,128)(2,1)} %bitcast.23, bf16[256,16,128]{2,1,0:T(8,128)(2,1)} %copy-done.4, bf16[256,16,128]{2,1,0:T(8,128)(2,1)} %bitcast.26, bf16[256,16,128]{2,1,0:T(8,128)(2,1)} %copy-done.5), custom_call_target="tpu_custom_call" | custom-call | flops 1000000 | bytes 25000000 | tf_op jit(solution)/shard_map/translate/pallas_call | solution.py:246
  108.8 3.9 %all-to-all-done.3.got_ref = bf16[8,512,128]{2,1,0:T(8,128)(2,1)S(1)} async-done(((bf16[8,512,128]{2,1,0:T(8,128)(2,1)}), bf16[8,512,128]{2,1,0:T(8,128)(2,1)S(1)}, u32[]{:S(2)}, u32[]{:S(2)}) %all-to-all-start.3) | async-done | bytes 1048608 | tf_op jit(solution)/shard_map/all_to_all | solution.py:441
  112.7 3.6 %all-to-all-start.2 = ((bf16[8,512,128]{2,1,0:T(8,128)(2,1)}), bf16[8,512,128]{2,1,0:T(8,128)(2,1)S(1)}, u32[]{:S(2)}, u32[]{:S(2)}) async-start(bf16[8,512,128]{2,1,0:T(8,128)(2,1)} %bitcast.28), calls=%async_computation.2 | async-start | bytes 2097152 | tf_op jit(solution)/shard_map/all_to_all | solution.py:441
  116.3 5.2 %from_boxes.3 = bf16[256,1024]{1,0:T(8,128)(2,1)} custom-call(bf16[8,512,128]{2,1,0:T(8,128)(2,1)} %copy-done.2, bf16[1024,2048]{1,0:T(8,128)(2,1)} %get-tuple-element.25.mat_ref), custom_call_target="tpu_custom_call" | custom-call | flops 1000000 | bytes 1000000 | tf_op jit(solution)/shard_map/from_boxes/pallas_call | solution.py:375
  121.4 2.5 %collective-permute-start.7 = (bf16[256,1024]{1,0:T(8,128)(2,1)}, bf16[256,1024]{1,0:T(8,128)(2,1)S(1)}, u32[]{:S(2)}, u32[]{:S(2)}) collective-permute-start(bf16[256,1024]{1,0:T(8,128)(2,1)} %from_boxes.3), channel_id=1, source_target_pairs={{0,4},{4,0},{1,5},{5,1},{2,6},{6,2},{3,7},{7,3},{8,12},{12,8},{9,1... | collective-permute-start | bytes 1572872 | tf_op jit(solution)/shard_map/ppermute | solution.py:41
  124.0 15.8 %near_part.1.near_ref = f32[2,8,8192]{2,1,0:T(8,128)} custom-call(s32[2048]{0:T(1024)} %reshape.37.idx_ref, bf16[2,8,8192]{2,1,0:T(8,128)(2,1)} %collective-permute-done.3.below_ref, bf16[2,8,8192]{2,1,0:T(8,128)(2,1)} %own_ref.1, bf16[2,8,8192]{2,1,0:T(8,128)(2,1)} %copy-done.9, bf16[2,8192,256]{2,1,0:T(8,128)(2,1)} %bitcast.27), custom_call_target="tpu_custom_call" | custom-call | flops 1000000 | bytes 1000000 | tf_op jit(solution)/shard_map/near_part/pallas_call | solution.py:330
  139.7 1.0 copy-done.3
  140.7 5.2 %from_boxes.2.own_ref = bf16[256,1024]{1,0:T(8,128)(2,1)} custom-call(bf16[8,512,128]{2,1,0:T(8,128)(2,1)} %copy-done.3, bf16[1024,2048]{1,0:T(8,128)(2,1)} %get-tuple-element.25.mat_ref), custom_call_target="tpu_custom_call" | custom-call | flops 1000000 | bytes 1000000 | tf_op jit(solution)/shard_map/from_boxes/pallas_call | solution.py:375
  147.6 5.1 %far_part.1 = f32[2,8,8192]{2,1,0:T(8,128)} custom-call(s32[1]{0:T(128)} %bitcast.hi_ref, bf16[256,1024]{1,0:T(8,128)(2,1)} %from_boxes.2.own_ref, bf16[256,1024]{1,0:T(8,128)(2,1)} %copy-done.7, bf16[2,8192,128]{2,1,0:T(8,128)(2,1)} %bitcast.20, f32[2,8,8192]{2,1,0:T(8,128)} %near_part.1.near_ref), custom_call_target="tpu_custom_call" | custom-call | flops 1000000 | bytes 1000000 | tf_op jit(solution)/shard_map/far_part/pallas_call | solution.py:425
  (55 shorter events, 9.6 us)
Async XLA Ops:
  0.0 18.2 %copy-start.12 = (s32[1024,12]{0,1:T(8,128)S(1)}, s32[1024,12]{0,1:T(8,128)}, u32[]{:S(2)}) copy-start(s32[1024,12]{0,1:T(8,128)} %param.18) | copy-start | bytes 147460
  0.0 18.5 %copy-start.11 = (s32[1024,12]{0,1:T(8,128)S(1)}, s32[1024,12]{0,1:T(8,128)}, u32[]{:S(2)}) copy-start(s32[1024,12]{0,1:T(8,128)} %param.19) | copy-start | bytes 147460
  0.0 19.2 %copy-start.13 = (s32[256,8]{0,1:T(8,128)S(1)}, s32[256,8]{0,1:T(8,128)}, u32[]{:S(2)}) copy-start(s32[256,8]{0,1:T(8,128)} %param.12) | copy-start | bytes 24580
  0.0 19.2 %copy-start.14 = (s32[256]{0:T(256)S(1)}, s32[256]{0:T(256)}, u32[]{:S(2)}) copy-start(s32[256]{0:T(256)} %param.13) | copy-start | bytes 3076
  9.4 34.8 %all-to-all-start.1 = ((bf16[8,512,128]{2,1,0:T(8,128)(2,1)}), bf16[8,512,128]{2,1,0:T(8,128)(2,1)S(1)}, u32[]{:S(2)}, u32[]{:S(2)}) async-start(bf16[8,512,128]{2,1,0:T(8,128)(2,1)} %get-tuple-element.29), calls=%async_computation.1 | async-start | bytes 2097152 | tf_op jit(solution)/shard_map/all_to_all | solution.py:441
  15.6 22.8 %collective-permute-start = (bf16[256,1024]{1,0:T(8,128)(2,1)}, bf16[256,1024]{1,0:T(8,128)(2,1)S(1)}, u32[]{:S(2)}, u32[]{:S(2)}) collective-permute-start(bf16[256,1024]{1,0:T(8,128)(2,1)} %get-tuple-element.21), channel_id=1, source_target_pairs={{0,4},{4,0},{1,5},{5,1},{2,6},{6,2},{3,7},{7,3},{8,12},{12,8},{9,1... | collective-permute-start | bytes 1572872 | tf_op jit(solution)/shard_map/ppermute | solution.py:41
  20.4 31.5 %copy-start.10 = (bf16[2,316,64]{1,2,0:T(8,128)(2,1)S(1)}, bf16[2,316,64]{1,2,0:T(8,128)(2,1)}, u32[]{:S(2)}) copy-start(bf16[2,316,64]{1,2,0:T(8,128)(2,1)} %param.17) | copy-start | bytes 242692
  20.4 32.4 %copy-start.6 = (bf16[2,8,8192]{2,1,0:T(8,128)(2,1)S(1)}, bf16[2,8,8192]{2,1,0:T(8,128)(2,1)}, u32[]{:S(2)}) copy-start(bf16[2,8,8192]{2,1,0:T(8,128)(2,1)} %own_ref.1) | copy-start | bytes 786436
  44.2 35.9 %copy-start = (bf16[8,512,128]{2,1,0:T(8,128)(2,1)}, bf16[8,512,128]{2,1,0:T(8,128)(2,1)S(1)}, u32[]{:S(2)}) copy-start(bf16[8,512,128]{2,1,0:T(8,128)(2,1)S(1)} %all-to-all-done.1) | copy-start | bytes 3145732
  44.2 26.7 %all-to-all-start = ((bf16[8,512,128]{2,1,0:T(8,128)(2,1)}), bf16[8,512,128]{2,1,0:T(8,128)(2,1)S(1)}, u32[]{:S(2)}, u32[]{:S(2)}) async-start(bf16[8,512,128]{2,1,0:T(8,128)(2,1)} %to_boxes_again.1), calls=%async_computation | async-start | bytes 2097152 | tf_op jit(solution)/shard_map/all_to_all | solution.py:441
  52.1 5.8 %collective-permute-start.2 = (bf16[2,316,64]{2,1,0:T(8,128)(2,1)S(1)}, bf16[2,316,64]{2,1,0:T(8,128)(2,1)S(1)}, u32[]{:S(2)}, u32[]{:S(2)}) collective-permute-start(bf16[2,316,64]{2,1,0:T(8,128)(2,1)S(1)} %copy.16), channel_id=1, source_target_pairs={{1,0},{0,1},{3,2},{2,3},{17,4},{16,5},{19,6},{18,7},{5,8},{4,9},{7... | collective-permute-start | bytes 242696 | tf_op jit(solution)/shard_map/ppermute | solution.py:478
  52.1 5.8 %collective-permute-start.1 = (bf16[2,316,64]{2,1,0:T(8,128)(2,1)S(1)}, bf16[2,316,64]{2,1,0:T(8,128)(2,1)S(1)}, u32[]{:S(2)}, u32[]{:S(2)}) collective-permute-start(bf16[2,316,64]{2,1,0:T(8,128)(2,1)S(1)} %copy.16), channel_id=1, source_target_pairs={{0,0},{1,1},{2,2},{3,3},{16,4},{17,5},{18,6},{19,7},{4,8},{5,9},{6... | collective-permute-start | bytes 242696 | tf_op jit(solution)/shard_map/ppermute | solution.py:478
  52.8 7.0 %collective-permute-start.4 = (bf16[2,8,8192]{2,1,0:T(8,128)(2,1)S(1)}, bf16[2,8,8192]{2,1,0:T(8,128)(2,1)S(1)}, u32[]{:S(2)}, u32[]{:S(2)}) collective-permute-start(bf16[2,8,8192]{2,1,0:T(8,128)(2,1)S(1)} %copy-done.6), channel_id=1, source_target_pairs={{1,0},{2,1},{3,2},{4,3},{5,4},{6,5},{7,6},{8,7},{9,8},{10,9},{11,1... | collective-permute-start | bytes 786440 | tf_op jit(solution)/shard_map/ppermute | solution.py:37
  54.1 6.4 %collective-permute-start.3 = (bf16[2,8,8192]{2,1,0:T(8,128)(2,1)S(1)}, bf16[2,8,8192]{2,1,0:T(8,128)(2,1)}, u32[]{:S(2)}, u32[]{:S(2)}) collective-permute-start(bf16[2,8,8192]{2,1,0:T(8,128)(2,1)S(1)} %copy-done.6), channel_id=1, source_target_pairs={{0,1},{1,2},{2,3},{3,4},{4,5},{5,6},{6,7},{7,8},{8,9},{9,10},{10,1... | collective-permute-start | bytes 786440 | tf_op jit(solution)/shard_map/ppermute | solution.py:37
  58.8 19.0 %collective-permute-start.5 = (bf16[256,16,128]{2,1,0:T(8,128)(2,1)S(1)}, bf16[256,16,128]{2,1,0:T(8,128)(2,1)S(1)}, u32[]{:S(2)}, u32[]{:S(2)}) collective-permute-start(bf16[256,16,128]{2,1,0:T(8,128)(2,1)S(1)} %bitcast.21), channel_id=1, source_target_pairs={{0,1},{1,0},{2,3},{3,2},{4,5},{5,4},{6,7},{7,6},{8,9},{9,8},{10,11... | collective-permute-start | bytes 3145736 | tf_op jit(solution)/shard_map/ppermute | solution.py:41
  71.0 9.2 %copy-start.1 = (bf16[8,512,128]{2,1,0:T(8,128)(2,1)}, bf16[8,512,128]{2,1,0:T(8,128)(2,1)S(1)}, u32[]{:S(2)}) copy-start(bf16[8,512,128]{2,1,0:T(8,128)(2,1)S(1)} %all-to-all-done) | copy-start | bytes 3145732
  71.0 9.1 %collective-permute-start.6 = (bf16[256,16,128]{2,1,0:T(8,128)(2,1)S(1)}, bf16[256,16,128]{2,1,0:T(8,128)(2,1)S(1)}, u32[]{:S(2)}, u32[]{:S(2)}) collective-permute-start(bf16[256,16,128]{2,1,0:T(8,128)(2,1)S(1)} %bitcast.24), channel_id=1, source_target_pairs={{0,1},{1,0},{2,3},{3,2},{4,5},{5,4},{6,7},{7,6},{8,9},{9,8},{10,11... | collective-permute-start | bytes 3145736 | tf_op jit(solution)/shard_map/ppermute | solution.py:41
  77.8 2.3 %copy-start.4 = (bf16[256,16,128]{2,1,0:T(8,128)(2,1)}, bf16[256,16,128]{2,1,0:T(8,128)(2,1)S(1)}, u32[]{:S(2)}) copy-start(bf16[256,16,128]{2,1,0:T(8,128)(2,1)S(1)} %collective-permute-done.5.two_ref) | copy-start | bytes 3145732
  80.1 1.0 copy-start.5
  93.0 19.7 %all-to-all-start.3 = ((bf16[8,512,128]{2,1,0:T(8,128)(2,1)}), bf16[8,512,128]{2,1,0:T(8,128)(2,1)S(1)}, u32[]{:S(2)}, u32[]{:S(2)}) async-start(bf16[8,512,128]{2,1,0:T(8,128)(2,1)} %bitcast.29), calls=%async_computation.3 | async-start | bytes 2097152 | tf_op jit(solution)/shard_map/all_to_all | solution.py:441
  112.7 3.6 %copy-start.2 = (bf16[8,512,128]{2,1,0:T(8,128)(2,1)}, bf16[8,512,128]{2,1,0:T(8,128)(2,1)S(1)}, u32[]{:S(2)}) copy-start(bf16[8,512,128]{2,1,0:T(8,128)(2,1)S(1)} %all-to-all-done.3.got_ref) | copy-start | bytes 3145732
  112.7 27.0 %all-to-all-start.2 = ((bf16[8,512,128]{2,1,0:T(8,128)(2,1)}), bf16[8,512,128]{2,1,0:T(8,128)(2,1)S(1)}, u32[]{:S(2)}, u32[]{:S(2)}) async-start(bf16[8,512,128]{2,1,0:T(8,128)(2,1)} %bitcast.28), calls=%async_computation.2 | async-start | bytes 2097152 | tf_op jit(solution)/shard_map/all_to_all | solution.py:441
  121.4 25.4 %collective-permute-start.7 = (bf16[256,1024]{1,0:T(8,128)(2,1)}, bf16[256,1024]{1,0:T(8,128)(2,1)S(1)}, u32[]{:S(2)}, u32[]{:S(2)}) collective-permute-start(bf16[256,1024]{1,0:T(8,128)(2,1)} %from_boxes.3), channel_id=1, source_target_pairs={{0,4},{4,0},{1,5},{5,1},{2,6},{6,2},{3,7},{7,3},{8,12},{12,8},{9,1... | collective-permute-start | bytes 1572872 | tf_op jit(solution)/shard_map/ppermute | solution.py:41
  139.7 1.0 copy-start.3
  (3 other events, 2.3 us)

commit v4 on v3

--- a/solution.py
+++ b/solution.py
@@ -25,6 +25,7 @@
 F32 = jnp.float32
 BF16 = jnp.bfloat16
 ROOM = pltpu.CompilerParams(vmem_limit_bytes=58 * 2**20)
+LESS = pltpu.CompilerParams(vmem_limit_bytes=28 * 2**20)
 
 
 def cost(megabytes):
@@ -184,7 +185,7 @@
         ],
         out_specs=pl.BlockSpec((chips, 2 * rows, LANES), lambda s: (s, 0, 0)),
         out_shape=jax.ShapeDtypeStruct((CHIPS, 2 * rows, LANES), BF16),
-        compiler_params=ROOM,
+        compiler_params=LESS,
         cost_estimate=cost(6),
         name="to_boxes_again",
     )(lhs, matrix)
@@ -257,7 +258,7 @@
             ],
         ),
         out_shape=jax.ShapeDtypeStruct((targets, 2 * R, LANES), BF16),
-        compiler_params=ROOM,
+        compiler_params=LESS,
         cost_estimate=cost(25),
         name="translate",
     )(lists, operators, *parts)
@@ -382,7 +383,7 @@
         out_specs=pl.BlockSpec((rows, DEPTH), lambda s: (0, 0)),
         out_shape=jax.ShapeDtypeStruct((rows, DEPTH), BF16),
         scratch_shapes=[pltpu.VMEM((rows, DEPTH), F32)],
-        compiler_params=ROOM,
+        compiler_params=LESS,
         cost_estimate=cost(1),
         name="from_boxes",
     )(received, matrix)
@@ -431,7 +432,7 @@
             out_specs=wave,
         ),
         out_shape=jax.ShapeDtypeStruct((2, R, width), F32),
-        compiler_params=ROOM,
+        compiler_params=LESS,
         cost_estimate=cost(1),
         name="far_part",
     )(hi, own, other, radiation, near_field)
@@ -522,20 +523,17 @@
     index = jnp.where(live, near_list - first, 3 * clusters).reshape(-1)
     lists = target_lists(trans_box, trans_off, hi, core)
 
+    below = passed_along(currents, 1)
+    above = passed_along(currents, -1)
+    operators = operator_table(translation)
     leaf_own, leaf_other = leaves(side, currents, radiation)
     leaf_partner = across(leaf_other, "hi")
+    leaf_own, below, above, operators = lax.optimization_barrier((leaf_own, below, above, operators))
     boxes_own, matrix = to_boxes(leaf_own, interp, shift_angle)
     rows_own = to_owners(boxes_own, samples)
     swapped_own = across(rows_own, "core")
-
-    leaf_partner, lists, index, late_currents, translation = lax.optimization_barrier(
-        (leaf_partner, lists, index, currents, translation)
-    )
+    leaf_partner, lists, index = lax.optimization_barrier((leaf_partner, lists, index))
     rows_partner = to_owners(to_boxes_again(leaf_partner, matrix), samples)
-    below = passed_along(late_currents, 1)
-    above = passed_along(late_currents, -1)
-    operators = operator_table(translation)
-    rows_partner, operators, below, above = lax.optimization_barrier((rows_partner, operators, below, above))
     parts = (rows_own, swapped_own, rows_partner, across(rows_partner, "core"))
 
     fields_partner = translate(lists[1], operators, parts)

time: 154 us -> 154 us (level)
  Pallas kernels: 69.3 us -> 54.5 us
  waiting for transfers between devices: 34.1 us -> 44.4 us
  local copies, waits for them, and re-layouts: 7.67 us -> 13.1 us
    all_to_all x4, starting transfers between devices: 21.4 us -> 29.2 us  [swapped(): lax.all_to_all(array, INSIDE, split_axis=0, concat_axis=0, tiled=True)]
    unnamed x32 -> x37, local copies, waits for them, and re-layouts: 4.62 us -> 11.4 us
    ppermute x4, starting transfers between devices: 13 us -> 6.9 us  [across(): return lax.ppermute(array, axis, [(0, 1), (1, 0)])]
    ppermute x4, waiting for transfers between devices: 19.8 us -> 25.8 us  [across(): return lax.ppermute(array, axis, [(0, 1), (1, 0)])]
    pallas_call x2, Pallas kernels: 23.7 us -> 17.9 us  [translate(): pl.pallas_call(functools.partial(translate_kernel, group=8), grid_spec=pl...]
    pallas_call x2, Pallas kernels: 10.4 us -> 5.18 us  [from_boxes(): pl.pallas_call(down_kernel, grid=(steps,), in_specs=[pl.BlockSpec((chips,...]
    all_to_all x4, waiting for transfers between devices: 14.3 us -> 18.6 us  [swapped(): lax.all_to_all(array, INSIDE, split_axis=0, concat_axis=0, tiled=True)]
    pallas_call x1, Pallas kernels: 5.09 us -> 3.07 us  [far_part(): pl.pallas_call(far_kernel, grid_spec=pltpu.PrefetchScalarGridSpec(num_sca...]
  transfers between devices with their start and end apart: 12 -> 12, of which waited for: 5 -> 5; matrix products, arithmetic and copies ran while one was open for 3% -> 2% of each run, Pallas kernels for 28% -> 25%
where the time goes in v4:
time: 154 us; the launch traced here: 153 us
  Pallas kernels  54.5 us (35%)
  waiting for transfers between devices  44.4 us (29%)
  starting transfers between devices  40.5 us (26%)
  local copies, waits for them, and re-layouts  13.1 us (9%)
    all_to_all x4, starting transfers between devices, swapped(): lax.all_to_all(array, INSIDE, split_axis=0, concat_axis=0, tiled=True)  29.2 us
    ppermute x4, waiting for transfers between devices, across(): return lax.ppermute(array, axis, [(0, 1), (1, 0)])  25.8 us
    all_to_all x4, waiting for transfers between devices, swapped(): lax.all_to_all(array, INSIDE, split_axis=0, concat_axis=0, tiled=True)  18.6 us
    pallas_call x2, Pallas kernels, translate(): pl.pallas_call(functools.partial(translate_kernel, group=8), grid_spec=pl...  17.9 us
    pallas_call x1, Pallas kernels, near_part(): pl.pallas_call(near_kernel, grid_spec=pltpu.PrefetchScalarGridSpec(num_sc...  15.8 us
    unnamed x37, local copies, waits for them, and re-layouts  11.4 us
    ppermute x4, starting transfers between devices, across(): return lax.ppermute(array, axis, [(0, 1), (1, 0)])  6.9 us
    pallas_call x2, Pallas kernels, from_boxes(): pl.pallas_call(down_kernel, grid=(steps,), in_specs=[pl.BlockSpec((chips,...  5.18 us
  transfers between devices with their start and end apart: 12, of which 5 were waited for; matrix products, arithmetic and copies ran while one was open for 2% of the time, Pallas kernels for 25%

profile of v4, /device:TPU:0, one launch (start us, length us, event | category | flops | bytes accessed | tf_op | source)
XLA Modules:
  0.0 153.3 jit_solution(14526339158843732519)
XLA Ops:
  2.2 2.0 %collective-permute-start.1 = (bf16[2,8,8192]{2,1,0:T(8,128)(2,1)}, bf16[2,8,8192]{2,1,0:T(8,128)(2,1)S(1)}, u32[]{:S(2)}, u32[]{:S(2)}) collective-permute-start(bf16[2,8,8192]{2,1,0:T(8,128)(2,1)} %own_ref.1), channel_id=1, source_target_pairs={{0,1},{1,2},{2,3},{3,4},{4,5},{5,6},{6,7},{7,8},{8,9},{9,10},{10,1... | collective-permute-start | bytes 786440 | tf_op jit(solution)/shard_map/ppermute | solution.py:38
  5.5 4.8 %leaves.1 = (bf16[256,1024]{1,0:T(8,128)(2,1)}, bf16[256,1024]{1,0:T(8,128)(2,1)}) custom-call(s32[1]{0:T(128)} %bitcast.hi_ref, bf16[2,8,8192]{2,1,0:T(8,128)(2,1)} %own_ref.1, bf16[2,8192,128]{2,1,0:T(8,128)(2,1)} %bitcast.19), custom_call_target="tpu_custom_call" | custom-call | flops 1000000 | bytes 1000000 | tf_op jit(solution)/shard_map/leaves/pallas_call | solution.py:100
  10.6 4.8 %to_boxes.1 = (bf16[8,512,128]{2,1,0:T(8,128)(2,1)}, bf16[1024,2048]{1,0:T(8,128)(2,1)}) custom-call(bf16[256,1024]{1,0:T(8,128)(2,1)} %get-tuple-element.23.lhs_ref, bf16[64,1024]{1,0:T(8,128)(2,1)} %interp_ref.1, f32[8,1024]{1,0:T(8,128)} %angle_ref.1), custom_call_target="tpu_custom_call" | custom-call | flops 1000000 | bytes 1000000 | tf_op jit(solution)/shard_map/to_boxes/pallas_call | solution.py:153
  15.4 18.2 %all-to-all-start = ((bf16[8,512,128]{2,1,0:T(8,128)(2,1)}), bf16[8,512,128]{2,1,0:T(8,128)(2,1)S(1)}, u32[]{:S(2)}, u32[]{:S(2)}) async-start(bf16[8,512,128]{2,1,0:T(8,128)(2,1)} %get-tuple-element.24), calls=%async_computation | async-start | bytes 2097152 | tf_op jit(solution)/shard_map/all_to_all | solution.py:442
  33.6 3.6 %collective-permute-start = (bf16[256,1024]{1,0:T(8,128)(2,1)S(1)}, bf16[256,1024]{1,0:T(8,128)(2,1)S(1)}, u32[]{:S(2)}, u32[]{:S(2)}) collective-permute-start(bf16[256,1024]{1,0:T(8,128)(2,1)S(1)} %copy-done.16), channel_id=1, source_target_pairs={{0,4},{4,0},{1,5},{5,1},{2,6},{6,2},{3,7},{7,3},{8,12},{12,8},{9,1... | collective-permute-start | bytes 1572872 | tf_op jit(solution)/shard_map/ppermute | solution.py:42
  39.7 21.1 %collective-permute-done.lhs_ref = bf16[256,1024]{1,0:T(8,128)(2,1)S(1)} collective-permute-done((bf16[256,1024]{1,0:T(8,128)(2,1)S(1)}, bf16[256,1024]{1,0:T(8,128)(2,1)S(1)}, u32[]{:S(2)}, u32[]{:S(2)}) %collective-permute-start) | collective-permute-done | bytes 524320 | tf_op jit(solution)/shard_map/ppermute | solution.py:42
  60.7 2.2 %copy-done = bf16[1024,2048]{1,0:T(8,128)(2,1)S(1)} copy-done((bf16[1024,2048]{1,0:T(8,128)(2,1)S(1)}, bf16[1024,2048]{1,0:T(8,128)(2,1)}, u32[]{:S(2)}) %copy-start) | copy-done | bytes 4194328
  62.9 3.0 %to_boxes_again.1 = bf16[8,512,128]{2,1,0:T(8,128)(2,1)} custom-call(bf16[256,1024]{1,0:T(8,128)(2,1)S(1)} %collective-permute-done.lhs_ref, bf16[1024,2048]{1,0:T(8,128)(2,1)S(1)} %copy-done), custom_call_target="tpu_custom_call" | custom-call | flops 1000000 | bytes 6000000 | tf_op jit(solution)/shard_map/to_boxes_again/pallas_call | solution.py:179
  65.9 3.9 %all-to-all-start.1 = ((bf16[8,512,128]{2,1,0:T(8,128)(2,1)}), bf16[8,512,128]{2,1,0:T(8,128)(2,1)S(1)}, u32[]{:S(2)}, u32[]{:S(2)}) async-start(bf16[8,512,128]{2,1,0:T(8,128)(2,1)} %to_boxes_again.1), calls=%async_computation.1 | async-start | bytes 2097152 | tf_op jit(solution)/shard_map/all_to_all | solution.py:442
  69.8 14.5 %all-to-all-done.1 = bf16[8,512,128]{2,1,0:T(8,128)(2,1)S(1)} async-done(((bf16[8,512,128]{2,1,0:T(8,128)(2,1)}), bf16[8,512,128]{2,1,0:T(8,128)(2,1)S(1)}, u32[]{:S(2)}, u32[]{:S(2)}) %all-to-all-start.1) | async-done | bytes 1048608 | tf_op jit(solution)/shard_map/all_to_all | solution.py:442
  84.3 2.6 %collective-permute-done.6.four_ref = bf16[256,16,128]{2,1,0:T(8,128)(2,1)S(1)} collective-permute-done((bf16[256,16,128]{2,1,0:T(8,128)(2,1)S(1)}, bf16[256,16,128]{2,1,0:T(8,128)(2,1)S(1)}, u32[]{:S(2)}, u32[]{:S(2)}) %collective-permute-start.6) | collective-permute-done | bytes 1048608 | tf_op jit(solution)/shard_map/ppermute | solution.py:42
  87.0 8.5 %translate.3 = bf16[256,16,128]{2,1,0:T(8,128)(2,1)S(1)} custom-call(s32[6144]{0:T(1024)S(1)} %select_n.93.list_ref, f32[2,320,128]{2,1,0:T(8,128)S(1)} %select_maximum_fusion.oper_ref, bf16[256,16,128]{2,1,0:T(8,128)(2,1)S(1)} %bitcast.22, bf16[256,16,128]{2,1,0:T(8,128)(2,1)S(1)} %collective-permute-done.5.two_ref, bf16[256,16,128]{2,1,0:T(8,128)(2,1)S(1)} %bitcast.25, ...), custom_call_target="tpu_custom_call" | custom-call | flops 1000000 | bytes 25000000 | tf_op jit(solution)/shard_map/translate/pallas_call | solution.py:247
  96.5 3.6 %all-to-all-start.3 = ((bf16[8,512,128]{2,1,0:T(8,128)(2,1)}), bf16[8,512,128]{2,1,0:T(8,128)(2,1)S(1)}, u32[]{:S(2)}, u32[]{:S(2)}) async-start(bf16[8,512,128]{2,1,0:T(8,128)(2,1)} %bitcast.27), calls=%async_computation.3 | async-start | bytes 2097152 | tf_op jit(solution)/shard_map/all_to_all | solution.py:442
  102.5 9.4 %translate.2 = bf16[256,16,128]{2,1,0:T(8,128)(2,1)} custom-call(s32[6144]{0:T(1024)S(1)} %select_n.91.list_ref, f32[2,320,128]{2,1,0:T(8,128)S(1)} %select_maximum_fusion.oper_ref, bf16[256,16,128]{2,1,0:T(8,128)(2,1)S(1)} %bitcast.23, bf16[256,16,128]{2,1,0:T(8,128)(2,1)S(1)} %copy-done.6, bf16[256,16,128]{2,1,0:T(8,128)(2,1)S(1)} %bitcast.26, ...), custom_call_target="tpu_custom_call" | custom-call | flops 1000000 | bytes 25000000 | tf_op jit(solution)/shard_map/translate/pallas_call | solution.py:247
  111.9 4.1 %all-to-all-done.3.got_ref = bf16[8,512,128]{2,1,0:T(8,128)(2,1)S(1)} async-done(((bf16[8,512,128]{2,1,0:T(8,128)(2,1)}), bf16[8,512,128]{2,1,0:T(8,128)(2,1)S(1)}, u32[]{:S(2)}, u32[]{:S(2)}) %all-to-all-start.3) | async-done | bytes 1048608 | tf_op jit(solution)/shard_map/all_to_all | solution.py:442
  115.9 3.6 %all-to-all-start.2 = ((bf16[8,512,128]{2,1,0:T(8,128)(2,1)}), bf16[8,512,128]{2,1,0:T(8,128)(2,1)S(1)}, u32[]{:S(2)}, u32[]{:S(2)}) async-start(bf16[8,512,128]{2,1,0:T(8,128)(2,1)} %bitcast.5), calls=%async_computation.2 | async-start | bytes 2097152 | tf_op jit(solution)/shard_map/all_to_all | solution.py:442
  119.5 2.2 %copy-done.1 = bf16[1024,2048]{1,0:T(8,128)(2,1)S(1)} copy-done((bf16[1024,2048]{1,0:T(8,128)(2,1)S(1)}, bf16[1024,2048]{1,0:T(8,128)(2,1)}, u32[]{:S(2)}) %copy-start.1) | copy-done | bytes 4194328
  121.7 2.6 %from_boxes.3 = bf16[256,1024]{1,0:T(8,128)(2,1)S(1)} custom-call(bf16[8,512,128]{2,1,0:T(8,128)(2,1)S(1)} %all-to-all-done.3.got_ref, bf16[1024,2048]{1,0:T(8,128)(2,1)S(1)} %copy-done.1), custom_call_target="tpu_custom_call" | custom-call | flops 1000000 | bytes 1000000 | tf_op jit(solution)/shard_map/from_boxes/pallas_call | solution.py:376
  124.3 3.2 %collective-permute-start.7 = (bf16[256,1024]{1,0:T(8,128)(2,1)S(1)}, bf16[256,1024]{1,0:T(8,128)(2,1)S(1)}, u32[]{:S(2)}, u32[]{:S(2)}) collective-permute-start(bf16[256,1024]{1,0:T(8,128)(2,1)S(1)} %from_boxes.3), channel_id=1, source_target_pairs={{0,4},{4,0},{1,5},{5,1},{2,6},{6,2},{3,7},{7,3},{8,12},{12,8},{9,1... | collective-permute-start | bytes 1572872 | tf_op jit(solution)/shard_map/ppermute | solution.py:42
  127.5 15.8 %near_part.1.near_ref = f32[2,8,8192]{2,1,0:T(8,128)} custom-call(s32[2048]{0:T(1024)} %reshape.37.idx_ref, bf16[2,8,8192]{2,1,0:T(8,128)(2,1)} %copy-done.10, bf16[2,8,8192]{2,1,0:T(8,128)(2,1)} %own_ref.1, bf16[2,8,8192]{2,1,0:T(8,128)(2,1)} %copy-done.11, bf16[2,8192,256]{2,1,0:T(8,128)(2,1)} %bitcast.28), custom_call_target="tpu_custom_call" | custom-call | flops 1000000 | bytes 1000000 | tf_op jit(solution)/shard_map/near_part/pallas_call | solution.py:331
  143.3 2.2 %copy-done.2 = bf16[1024,2048]{1,0:T(8,128)(2,1)S(1)} copy-done((bf16[1024,2048]{1,0:T(8,128)(2,1)S(1)}, bf16[1024,2048]{1,0:T(8,128)(2,1)}, u32[]{:S(2)}) %copy-start.2) | copy-done | bytes 4194328
  145.5 2.6 %from_boxes.2.own_ref = bf16[256,1024]{1,0:T(8,128)(2,1)S(1)} custom-call(bf16[8,512,128]{2,1,0:T(8,128)(2,1)S(1)} %all-to-all-done.2.got_ref, bf16[1024,2048]{1,0:T(8,128)(2,1)S(1)} %copy-done.2), custom_call_target="tpu_custom_call" | custom-call | flops 1000000 | bytes 1000000 | tf_op jit(solution)/shard_map/from_boxes/pallas_call | solution.py:376
  148.1 2.1 %collective-permute-done.7.other_ref = bf16[256,1024]{1,0:T(8,128)(2,1)S(1)} collective-permute-done((bf16[256,1024]{1,0:T(8,128)(2,1)S(1)}, bf16[256,1024]{1,0:T(8,128)(2,1)S(1)}, u32[]{:S(2)}, u32[]{:S(2)}) %collective-permute-start.7) | collective-permute-done | bytes 524320 | tf_op jit(solution)/shard_map/ppermute | solution.py:42
  150.2 3.1 %far_part.1 = f32[2,8,8192]{2,1,0:T(8,128)} custom-call(s32[1]{0:T(128)} %bitcast.hi_ref, bf16[256,1024]{1,0:T(8,128)(2,1)S(1)} %from_boxes.2.own_ref, bf16[256,1024]{1,0:T(8,128)(2,1)S(1)} %collective-permute-done.7.other_ref, bf16[2,8192,128]{2,1,0:T(8,128)(2,1)S(1)} %bitcast.20, f32[2,8,8192]{2,1,0:T(8,128)S(1)} %copy-done.9), custom_call_target="tpu_custom_call" | custom-call | flops 1000000 | bytes 1000000 | tf_op jit(solution)/shard_map/far_part/pallas_call | solution.py:426
  (59 shorter events, 9.5 us)
Async XLA Ops:
  1.1 9.3 %collective-permute-start.4 = (bf16[2,316,64]{2,1,0:T(8,128)(2,1)S(1)}, bf16[2,316,64]{2,1,0:T(8,128)(2,1)S(1)}, u32[]{:S(2)}, u32[]{:S(2)}) collective-permute-start(bf16[2,316,64]{2,1,0:T(8,128)(2,1)S(1)} %copy.16), channel_id=1, source_target_pairs={{1,0},{0,1},{3,2},{2,3},{17,4},{16,5},{19,6},{18,7},{5,8},{4,9},{7... | collective-permute-start | bytes 242696 | tf_op jit(solution)/shard_map/ppermute | solution.py:479
  1.6 8.8 %collective-permute-start.3 = (bf16[2,316,64]{2,1,0:T(8,128)(2,1)S(1)}, bf16[2,316,64]{2,1,0:T(8,128)(2,1)S(1)}, u32[]{:S(2)}, u32[]{:S(2)}) collective-permute-start(bf16[2,316,64]{2,1,0:T(8,128)(2,1)S(1)} %copy.16), channel_id=1, source_target_pairs={{0,0},{1,1},{2,2},{3,3},{16,4},{17,5},{18,6},{19,7},{4,8},{5,9},{6... | collective-permute-start | bytes 242696 | tf_op jit(solution)/shard_map/ppermute | solution.py:479
  2.2 8.4 %collective-permute-start.1 = (bf16[2,8,8192]{2,1,0:T(8,128)(2,1)}, bf16[2,8,8192]{2,1,0:T(8,128)(2,1)S(1)}, u32[]{:S(2)}, u32[]{:S(2)}) collective-permute-start(bf16[2,8,8192]{2,1,0:T(8,128)(2,1)} %own_ref.1), channel_id=1, source_target_pairs={{0,1},{1,2},{2,3},{3,4},{4,5},{5,6},{6,7},{7,8},{8,9},{9,10},{10,1... | collective-permute-start | bytes 786440 | tf_op jit(solution)/shard_map/ppermute | solution.py:38
  4.2 6.4 %collective-permute-start.2 = (bf16[2,8,8192]{2,1,0:T(8,128)(2,1)}, bf16[2,8,8192]{2,1,0:T(8,128)(2,1)S(1)}, u32[]{:S(2)}, u32[]{:S(2)}) collective-permute-start(bf16[2,8,8192]{2,1,0:T(8,128)(2,1)} %own_ref.1), channel_id=1, source_target_pairs={{1,0},{2,1},{3,2},{4,3},{5,4},{6,5},{7,6},{8,7},{9,8},{10,9},{11,1... | collective-permute-start | bytes 786440 | tf_op jit(solution)/shard_map/ppermute | solution.py:38
  5.5 31.8 %copy-start.13 = (s32[1024,12]{0,1:T(8,128)S(1)}, s32[1024,12]{0,1:T(8,128)}, u32[]{:S(2)}) copy-start(s32[1024,12]{0,1:T(8,128)} %param.18) | copy-start | bytes 147460
  5.5 32.0 %copy-start.12 = (s32[1024,12]{0,1:T(8,128)S(1)}, s32[1024,12]{0,1:T(8,128)}, u32[]{:S(2)}) copy-start(s32[1024,12]{0,1:T(8,128)} %param.19) | copy-start | bytes 147460
  10.3 23.3 %copy-start.16 = (bf16[256,1024]{1,0:T(8,128)(2,1)S(1)}, bf16[256,1024]{1,0:T(8,128)(2,1)}, u32[]{:S(2)}) copy-start(bf16[256,1024]{1,0:T(8,128)(2,1)} %get-tuple-element.19) | copy-start | bytes 1572868
  10.3 27.9 %copy-start.14 = (s32[256,8]{0,1:T(8,128)S(1)}, s32[256,8]{0,1:T(8,128)}, u32[]{:S(2)}) copy-start(s32[256,8]{0,1:T(8,128)} %param.12) | copy-start | bytes 24580
  10.3 27.9 %copy-start.15 = (s32[256]{0:T(256)S(1)}, s32[256]{0:T(256)}, u32[]{:S(2)}) copy-start(s32[256]{0:T(256)} %param.13) | copy-start | bytes 3076
  10.6 4.8 %copy-start.10 = (bf16[2,8,8192]{2,1,0:T(8,128)(2,1)}, bf16[2,8,8192]{2,1,0:T(8,128)(2,1)S(1)}, u32[]{:S(2)}) copy-start(bf16[2,8,8192]{2,1,0:T(8,128)(2,1)S(1)} %collective-permute-done.1.below_ref) | copy-start | bytes 786436
  10.6 4.8 %copy-start.11 = (bf16[2,8,8192]{2,1,0:T(8,128)(2,1)}, bf16[2,8,8192]{2,1,0:T(8,128)(2,1)S(1)}, u32[]{:S(2)}) copy-start(bf16[2,8,8192]{2,1,0:T(8,128)(2,1)S(1)} %collective-permute-done.2.above_ref) | copy-start | bytes 786436
  15.4 50.5 %all-to-all-start = ((bf16[8,512,128]{2,1,0:T(8,128)(2,1)}), bf16[8,512,128]{2,1,0:T(8,128)(2,1)S(1)}, u32[]{:S(2)}, u32[]{:S(2)}) async-start(bf16[8,512,128]{2,1,0:T(8,128)(2,1)} %get-tuple-element.24), calls=%async_computation | async-start | bytes 2097152 | tf_op jit(solution)/shard_map/all_to_all | solution.py:442
  33.6 27.1 %collective-permute-start = (bf16[256,1024]{1,0:T(8,128)(2,1)S(1)}, bf16[256,1024]{1,0:T(8,128)(2,1)S(1)}, u32[]{:S(2)}, u32[]{:S(2)}) collective-permute-start(bf16[256,1024]{1,0:T(8,128)(2,1)S(1)} %copy-done.16), channel_id=1, source_target_pairs={{0,4},{4,0},{1,5},{5,1},{2,6},{6,2},{3,7},{7,3},{8,12},{12,8},{9,1... | collective-permute-start | bytes 1572872 | tf_op jit(solution)/shard_map/ppermute | solution.py:42
  65.9 18.4 %all-to-all-start.1 = ((bf16[8,512,128]{2,1,0:T(8,128)(2,1)}), bf16[8,512,128]{2,1,0:T(8,128)(2,1)S(1)}, u32[]{:S(2)}, u32[]{:S(2)}) async-start(bf16[8,512,128]{2,1,0:T(8,128)(2,1)} %to_boxes_again.1), calls=%async_computation.1 | async-start | bytes 2097152 | tf_op jit(solution)/shard_map/all_to_all | solution.py:442
  69.8 14.5 %collective-permute-start.5 = (bf16[256,16,128]{2,1,0:T(8,128)(2,1)S(1)}, bf16[256,16,128]{2,1,0:T(8,128)(2,1)S(1)}, u32[]{:S(2)}, u32[]{:S(2)}) collective-permute-start(bf16[256,16,128]{2,1,0:T(8,128)(2,1)S(1)} %bitcast.21), channel_id=1, source_target_pairs={{0,1},{1,0},{2,3},{3,2},{4,5},{5,4},{6,7},{7,6},{8,9},{9,8},{10,11... | collective-permute-start | bytes 3145736 | tf_op jit(solution)/shard_map/ppermute | solution.py:42
  84.3 2.7 %collective-permute-start.6 = (bf16[256,16,128]{2,1,0:T(8,128)(2,1)S(1)}, bf16[256,16,128]{2,1,0:T(8,128)(2,1)S(1)}, u32[]{:S(2)}, u32[]{:S(2)}) collective-permute-start(bf16[256,16,128]{2,1,0:T(8,128)(2,1)S(1)} %bitcast.24), channel_id=1, source_target_pairs={{0,1},{1,0},{2,3},{3,2},{4,5},{5,4},{6,7},{7,6},{8,9},{9,8},{10,11... | collective-permute-start | bytes 3145736 | tf_op jit(solution)/shard_map/ppermute | solution.py:42
  84.3 12.1 %copy-start.5 = (bf16[256,16,128]{2,1,0:T(8,128)(2,1)}, bf16[256,16,128]{2,1,0:T(8,128)(2,1)S(1)}, u32[]{:S(2)}) copy-start(bf16[256,16,128]{2,1,0:T(8,128)(2,1)S(1)} %collective-permute-done.5.two_ref) | copy-start | bytes 3145732
  87.0 8.5 %copy-start.7 = (bf16[256,16,128]{2,1,0:T(8,128)(2,1)}, bf16[256,16,128]{2,1,0:T(8,128)(2,1)S(1)}, u32[]{:S(2)}) copy-start(bf16[256,16,128]{2,1,0:T(8,128)(2,1)S(1)} %collective-permute-done.6.four_ref) | copy-start | bytes 3145732
  96.5 19.5 %all-to-all-start.3 = ((bf16[8,512,128]{2,1,0:T(8,128)(2,1)}), bf16[8,512,128]{2,1,0:T(8,128)(2,1)S(1)}, u32[]{:S(2)}, u32[]{:S(2)}) async-start(bf16[8,512,128]{2,1,0:T(8,128)(2,1)} %bitcast.27), calls=%async_computation.3 | async-start | bytes 2097152 | tf_op jit(solution)/shard_map/all_to_all | solution.py:442
  115.9 27.4 %all-to-all-start.2 = ((bf16[8,512,128]{2,1,0:T(8,128)(2,1)}), bf16[8,512,128]{2,1,0:T(8,128)(2,1)S(1)}, u32[]{:S(2)}, u32[]{:S(2)}) async-start(bf16[8,512,128]{2,1,0:T(8,128)(2,1)} %bitcast.5), calls=%async_computation.2 | async-start | bytes 2097152 | tf_op jit(solution)/shard_map/all_to_all | solution.py:442
  124.3 25.9 %collective-permute-start.7 = (bf16[256,1024]{1,0:T(8,128)(2,1)S(1)}, bf16[256,1024]{1,0:T(8,128)(2,1)S(1)}, u32[]{:S(2)}, u32[]{:S(2)}) collective-permute-start(bf16[256,1024]{1,0:T(8,128)(2,1)S(1)} %from_boxes.3), channel_id=1, source_target_pairs={{0,4},{4,0},{1,5},{5,1},{2,6},{6,2},{3,7},{7,3},{8,12},{12,8},{9,1... | collective-permute-start | bytes 1572872 | tf_op jit(solution)/shard_map/ppermute | solution.py:42
  143.3 2.2 %copy-start.2 = (bf16[1024,2048]{1,0:T(8,128)(2,1)S(1)}, bf16[1024,2048]{1,0:T(8,128)(2,1)}, u32[]{:S(2)}) copy-start(bf16[1024,2048]{1,0:T(8,128)(2,1)} %get-tuple-element.26.mat_ref) | copy-start | bytes 12582916
  145.5 4.7 %copy-start.3 = (bf16[2,256,32,128]{3,2,1,0:T(8,128)(2,1)S(1)}, bf16[2,256,32,128]{3,2,1,0:T(8,128)(2,1)}, u32[]{:S(2)}) copy-start(bf16[2,256,32,128]{3,2,1,0:T(8,128)(2,1)} %param.14) | copy-start | bytes 12582916
  145.5 4.7 %copy-start.9 = (f32[2,8,8192]{2,1,0:T(8,128)S(1)}, f32[2,8,8192]{2,1,0:T(8,128)}, u32[]{:S(2)}) copy-start(f32[2,8,8192]{2,1,0:T(8,128)} %near_part.1.near_ref) | copy-start | bytes 1572868
  (5 other events, 7.8 us)

commit v5 on v4

--- a/solution.py
+++ b/solution.py
@@ -32,10 +32,13 @@
     return pl.CostEstimate(flops=10**6, bytes_accessed=megabytes * 10**6, transcendentals=0)
 
 
-def passed_along(array, by):
+def neighbours(array):
     size = lax.axis_size(ALL)
-    pairs = [(i, i + by) for i in range(size) if 0 <= i + by < size]
-    return lax.ppermute(array, ALL, pairs)
+    pairs = [(i, i + 1) for i in range(1, size - 1, 2)] + [(i + 1, i) for i in range(1, size - 1, 2)]
+    outside = lax.ppermute(array, ALL, pairs)
+    inside = across(array, "core")
+    first = lax.axis_index("core") == 0
+    return jnp.where(first, outside, inside), jnp.where(first, inside, outside)
 
 
 def across(array, axis):
@@ -467,18 +470,18 @@
 def operator_table(translation):
     groups, mids = lax.axis_size("grp"), lax.axis_size("mid")
     core = lax.axis_index("core")
-    got = []
-    for turned in range(2):
-        pairs = [
-            (((h * groups + g) * mids + m) * 2 + (c ^ turned), ((g * 2 + h) * mids + m) * 2 + c)
-            for g in range(groups)
-            for h in range(2)
-            for m in range(mids)
-            for c in range(2)
-        ]
-        got.append(lax.ppermute(translation, ALL, pairs).astype(F32))
-    low = jnp.where(core == 0, got[0], got[1])
-    high = jnp.where(core == 0, got[1], got[0])
+    pairs = [
+        (((h * groups + g) * mids + m) * 2 + c, ((g * 2 + h) * mids + m) * 2 + c)
+        for g in range(groups)
+        for h in range(2)
+        for m in range(mids)
+        for c in range(2)
+    ]
+    mine = lax.ppermute(translation, ALL, pairs)
+    other = across(mine, "core").astype(F32)
+    mine = mine.astype(F32)
+    low = jnp.where(core == 0, mine, other)
+    high = jnp.where(core == 0, other, mine)
     operator = padded(jnp.concatenate([low, high], axis=2))
     return jnp.pad(operator, ((0, 0), (0, -operator.shape[1] % R), (0, 0)))
 
@@ -523,16 +526,16 @@
     index = jnp.where(live, near_list - first, 3 * clusters).reshape(-1)
     lists = target_lists(trans_box, trans_off, hi, core)
 
-    below = passed_along(currents, 1)
-    above = passed_along(currents, -1)
-    operators = operator_table(translation)
     leaf_own, leaf_other = leaves(side, currents, radiation)
     leaf_partner = across(leaf_other, "hi")
-    leaf_own, below, above, operators = lax.optimization_barrier((leaf_own, below, above, operators))
     boxes_own, matrix = to_boxes(leaf_own, interp, shift_angle)
     rows_own = to_owners(boxes_own, samples)
     swapped_own = across(rows_own, "core")
-    leaf_partner, lists, index = lax.optimization_barrier((leaf_partner, lists, index))
+    operators = operator_table(translation)
+    below, above = neighbours(currents)
+    leaf_partner, lists, index, operators, below, above = lax.optimization_barrier(
+        (leaf_partner, lists, index, operators, below, above)
+    )
     rows_partner = to_owners(to_boxes_again(leaf_partner, matrix), samples)
     parts = (rows_own, swapped_own, rows_partner, across(rows_partner, "core"))
 

time: 154 us -> 142 us (0.922)
  starting transfers between devices: 40.5 us -> 28.1 us
    all_to_all x4, starting transfers between devices: 29.2 us -> 15.5 us  [swapped(): lax.all_to_all(array, INSIDE, split_axis=0, concat_axis=0, tiled=True)]
    ppermute x4 -> x6, waiting for transfers between devices: 25.8 us -> 21.4 us  [across(): return lax.ppermute(array, axis, [(0, 1), (1, 0)])]
    ppermute x4 -> x6, starting transfers between devices: 6.9 us -> 11.1 us  [across(): return lax.ppermute(array, axis, [(0, 1), (1, 0)])]
    all_to_all x4, waiting for transfers between devices: 18.6 us -> 22.6 us  [swapped(): lax.all_to_all(array, INSIDE, split_axis=0, concat_axis=0, tiled=True)]
    ppermute x4 -> x2, starting transfers between devices: 4.43 us -> 1.47 us  [the longest x1 0.8 us: neighbours(): outside = lax.ppermute(array, ALL, pairs)]
    unnamed x37 -> x31, local copies, waits for them, and re-layouts: 11.4 us -> 11.4 us
  transfers between devices with their start and end apart: 12 -> 12, of which waited for: 5 -> 7; matrix products, arithmetic and copies ran while one was open for 2% -> 3% of each run, Pallas kernels for 25% -> 30%
where the time goes in v5:
time: 142 us; the launch traced here: 141 us
  Pallas kernels  54.3 us (38%)
  waiting for transfers between devices  43.9 us (31%)
  starting transfers between devices  28.1 us (20%)
  local copies, waits for them, and re-layouts  13.1 us (9%)
    all_to_all x4, waiting for transfers between devices, swapped(): lax.all_to_all(array, INSIDE, split_axis=0, concat_axis=0, tiled=True)  22.6 us
    ppermute x6, waiting for transfers between devices, across(): return lax.ppermute(array, axis, [(0, 1), (1, 0)])  21.4 us
    pallas_call x2, Pallas kernels, translate(): pl.pallas_call(functools.partial(translate_kernel, group=8), grid_spec=pl...  17.9 us
    pallas_call x1, Pallas kernels, near_part(): pl.pallas_call(near_kernel, grid_spec=pltpu.PrefetchScalarGridSpec(num_sc...  15.8 us
    all_to_all x4, starting transfers between devices, swapped(): lax.all_to_all(array, INSIDE, split_axis=0, concat_axis=0, tiled=True)  15.5 us
    unnamed x31, local copies, waits for them, and re-layouts  11.4 us
    ppermute x6, starting transfers between devices, across(): return lax.ppermute(array, axis, [(0, 1), (1, 0)])  11.1 us
    pallas_call x2, Pallas kernels, from_boxes(): pl.pallas_call(down_kernel, grid=(steps,), in_specs=[pl.BlockSpec((chips,...  5.18 us
  transfers between devices with their start and end apart: 12, of which 7 were waited for; matrix products, arithmetic and copies ran while one was open for 3% of the time, Pallas kernels for 30%

profile of v5, /device:TPU:0, one launch (start us, length us, event | category | flops | bytes accessed | tf_op | source)
XLA Modules:
  0.0 141.0 jit_solution(15767612205928953657)
XLA Ops:
  0.8 4.4 %collective-permute-start.4 = (bf16[2,8,8192]{2,1,0:T(8,128)(2,1)}, bf16[2,8,8192]{2,1,0:T(8,128)(2,1)S(1)}, u32[]{:S(2)}, u32[]{:S(2)}) collective-permute-start(bf16[2,8,8192]{2,1,0:T(8,128)(2,1)} %own_ref.1), channel_id=1, source_target_pairs={{0,1},{1,0},{2,3},{3,2},{4,5},{5,4},{6,7},{7,6},{8,9},{9,8},{10,11... | collective-permute-start | bytes 786440 | tf_op jit(solution)/shard_map/ppermute | solution.py:45
  7.0 4.8 %leaves.1 = (bf16[256,1024]{1,0:T(8,128)(2,1)}, bf16[256,1024]{1,0:T(8,128)(2,1)}) custom-call(s32[1]{0:T(128)} %bitcast.hi_ref, bf16[2,8,8192]{2,1,0:T(8,128)(2,1)} %own_ref.1, bf16[2,8192,128]{2,1,0:T(8,128)(2,1)} %bitcast.19), custom_call_target="tpu_custom_call" | custom-call | flops 1000000 | bytes 1000000 | tf_op jit(solution)/shard_map/leaves/pallas_call | solution.py:103
  11.8 6.5 %collective-permute-start = (bf16[256,1024]{1,0:T(8,128)(2,1)}, bf16[256,1024]{1,0:T(8,128)(2,1)S(1)}, u32[]{:S(2)}, u32[]{:S(2)}) collective-permute-start(bf16[256,1024]{1,0:T(8,128)(2,1)} %get-tuple-element.18), channel_id=1, source_target_pairs={{0,4},{4,0},{1,5},{5,1},{2,6},{6,2},{3,7},{7,3},{8,12},{12,8},{9,1... | collective-permute-start | bytes 1572872 | tf_op jit(solution)/shard_map/ppermute | solution.py:45
  18.2 4.6 %to_boxes.1 = (bf16[8,512,128]{2,1,0:T(8,128)(2,1)}, bf16[1024,2048]{1,0:T(8,128)(2,1)}) custom-call(bf16[256,1024]{1,0:T(8,128)(2,1)} %get-tuple-element.21.lhs_ref, bf16[64,1024]{1,0:T(8,128)(2,1)} %interp_ref.1, f32[8,1024]{1,0:T(8,128)} %angle_ref.1), custom_call_target="tpu_custom_call" | custom-call | flops 1000000 | bytes 1000000 | tf_op jit(solution)/shard_map/to_boxes/pallas_call | solution.py:156
  22.8 3.6 %all-to-all-start = ((bf16[8,512,128]{2,1,0:T(8,128)(2,1)}), bf16[8,512,128]{2,1,0:T(8,128)(2,1)S(1)}, u32[]{:S(2)}, u32[]{:S(2)}) async-start(bf16[8,512,128]{2,1,0:T(8,128)(2,1)} %get-tuple-element.22), calls=%async_computation | async-start | bytes 2097152 | tf_op jit(solution)/shard_map/all_to_all | solution.py:445
  30.3 13.7 %collective-permute-done.lhs_ref = bf16[256,1024]{1,0:T(8,128)(2,1)S(1)} collective-permute-done((bf16[256,1024]{1,0:T(8,128)(2,1)}, bf16[256,1024]{1,0:T(8,128)(2,1)S(1)}, u32[]{:S(2)}, u32[]{:S(2)}) %collective-permute-start) | collective-permute-done | bytes 524320 | tf_op jit(solution)/shard_map/ppermute | solution.py:45
  44.0 2.2 %copy-done = bf16[1024,2048]{1,0:T(8,128)(2,1)S(1)} copy-done((bf16[1024,2048]{1,0:T(8,128)(2,1)S(1)}, bf16[1024,2048]{1,0:T(8,128)(2,1)}, u32[]{:S(2)}) %copy-start) | copy-done | bytes 4194328
  46.2 3.0 %to_boxes_again.1 = bf16[8,512,128]{2,1,0:T(8,128)(2,1)} custom-call(bf16[256,1024]{1,0:T(8,128)(2,1)S(1)} %collective-permute-done.lhs_ref, bf16[1024,2048]{1,0:T(8,128)(2,1)S(1)} %copy-done), custom_call_target="tpu_custom_call" | custom-call | flops 1000000 | bytes 6000000 | tf_op jit(solution)/shard_map/to_boxes_again/pallas_call | solution.py:182
  49.2 3.4 %all-to-all-done = bf16[8,512,128]{2,1,0:T(8,128)(2,1)S(1)} async-done(((bf16[8,512,128]{2,1,0:T(8,128)(2,1)}), bf16[8,512,128]{2,1,0:T(8,128)(2,1)S(1)}, u32[]{:S(2)}, u32[]{:S(2)}) %all-to-all-start) | async-done | bytes 1048608 | tf_op jit(solution)/shard_map/all_to_all | solution.py:445
  52.7 4.9 %all-to-all-start.1 = ((bf16[8,512,128]{2,1,0:T(8,128)(2,1)}), bf16[8,512,128]{2,1,0:T(8,128)(2,1)S(1)}, u32[]{:S(2)}, u32[]{:S(2)}) async-start(bf16[8,512,128]{2,1,0:T(8,128)(2,1)} %to_boxes_again.1), calls=%async_computation.1 | async-start | bytes 2097152 | tf_op jit(solution)/shard_map/all_to_all | solution.py:445
  57.5 15.1 %all-to-all-done.1 = bf16[8,512,128]{2,1,0:T(8,128)(2,1)S(1)} async-done(((bf16[8,512,128]{2,1,0:T(8,128)(2,1)}), bf16[8,512,128]{2,1,0:T(8,128)(2,1)S(1)}, u32[]{:S(2)}, u32[]{:S(2)}) %all-to-all-start.1) | async-done | bytes 1048608 | tf_op jit(solution)/shard_map/all_to_all | solution.py:445
  72.6 2.6 %collective-permute-done.6.four_ref = bf16[256,16,128]{2,1,0:T(8,128)(2,1)S(1)} collective-permute-done((bf16[256,16,128]{2,1,0:T(8,128)(2,1)S(1)}, bf16[256,16,128]{2,1,0:T(8,128)(2,1)S(1)}, u32[]{:S(2)}, u32[]{:S(2)}) %collective-permute-start.6) | collective-permute-done | bytes 1048608 | tf_op jit(solution)/shard_map/ppermute | solution.py:45
  75.3 8.5 %translate.3 = bf16[256,16,128]{2,1,0:T(8,128)(2,1)S(1)} custom-call(s32[6144]{0:T(1024)S(1)} %select_n.105.list_ref, f32[2,320,128]{2,1,0:T(8,128)S(1)} %select_maximum_fusion.oper_ref, bf16[256,16,128]{2,1,0:T(8,128)(2,1)S(1)} %bitcast.22, bf16[256,16,128]{2,1,0:T(8,128)(2,1)S(1)} %collective-permute-done.5.two_ref, bf16[256,16,128]{2,1,0:T(8,128)(2,1)S(1)} %bitcast.25, ...), custom_call_target="tpu_custom_call" | custom-call | flops 1000000 | bytes 25000000 | tf_op jit(solution)/shard_map/translate/pallas_call | solution.py:250
  84.8 3.6 %all-to-all-start.3 = ((bf16[8,512,128]{2,1,0:T(8,128)(2,1)}), bf16[8,512,128]{2,1,0:T(8,128)(2,1)S(1)}, u32[]{:S(2)}, u32[]{:S(2)}) async-start(bf16[8,512,128]{2,1,0:T(8,128)(2,1)} %bitcast.27), calls=%async_computation.3 | async-start | bytes 2097152 | tf_op jit(solution)/shard_map/all_to_all | solution.py:445
  90.8 9.4 %translate.2 = bf16[256,16,128]{2,1,0:T(8,128)(2,1)} custom-call(s32[6144]{0:T(1024)S(1)} %select_n.103.list_ref, f32[2,320,128]{2,1,0:T(8,128)S(1)} %select_maximum_fusion.oper_ref, bf16[256,16,128]{2,1,0:T(8,128)(2,1)S(1)} %bitcast.23, bf16[256,16,128]{2,1,0:T(8,128)(2,1)S(1)} %copy-done.6, bf16[256,16,128]{2,1,0:T(8,128)(2,1)S(1)} %bitcast.26, ...), custom_call_target="tpu_custom_call" | custom-call | flops 1000000 | bytes 25000000 | tf_op jit(solution)/shard_map/translate/pallas_call | solution.py:250
  100.2 4.1 %all-to-all-done.3.got_ref = bf16[8,512,128]{2,1,0:T(8,128)(2,1)S(1)} async-done(((bf16[8,512,128]{2,1,0:T(8,128)(2,1)}), bf16[8,512,128]{2,1,0:T(8,128)(2,1)S(1)}, u32[]{:S(2)}, u32[]{:S(2)}) %all-to-all-start.3) | async-done | bytes 1048608 | tf_op jit(solution)/shard_map/all_to_all | solution.py:445
  104.2 3.6 %all-to-all-start.2 = ((bf16[8,512,128]{2,1,0:T(8,128)(2,1)}), bf16[8,512,128]{2,1,0:T(8,128)(2,1)S(1)}, u32[]{:S(2)}, u32[]{:S(2)}) async-start(bf16[8,512,128]{2,1,0:T(8,128)(2,1)} %bitcast.5), calls=%async_computation.2 | async-start | bytes 2097152 | tf_op jit(solution)/shard_map/all_to_all | solution.py:445
  107.8 2.2 %copy-done.1 = bf16[1024,2048]{1,0:T(8,128)(2,1)S(1)} copy-done((bf16[1024,2048]{1,0:T(8,128)(2,1)S(1)}, bf16[1024,2048]{1,0:T(8,128)(2,1)}, u32[]{:S(2)}) %copy-start.1) | copy-done | bytes 4194328
  110.0 2.6 %from_boxes.3 = bf16[256,1024]{1,0:T(8,128)(2,1)S(1)} custom-call(bf16[8,512,128]{2,1,0:T(8,128)(2,1)S(1)} %all-to-all-done.3.got_ref, bf16[1024,2048]{1,0:T(8,128)(2,1)S(1)} %copy-done.1), custom_call_target="tpu_custom_call" | custom-call | flops 1000000 | bytes 1000000 | tf_op jit(solution)/shard_map/from_boxes/pallas_call | solution.py:379
  112.7 15.8 %near_part.1.near_ref = f32[2,8,8192]{2,1,0:T(8,128)} custom-call(s32[2048]{0:T(1024)} %reshape.37.idx_ref, bf16[2,8,8192]{2,1,0:T(8,128)(2,1)} %get-tuple-element.29.below_ref, bf16[2,8,8192]{2,1,0:T(8,128)(2,1)} %own_ref.1, bf16[2,8,8192]{2,1,0:T(8,128)(2,1)} %get-tuple-element.30.above_ref, bf16[2,8192,256]{2,1,0:T(8,128)(2,1)} %bitcast.28), custom_call_target="tpu_custom_call" | custom-call | flops 1000000 | bytes 1000000 | tf_op jit(solution)/shard_map/near_part/pallas_call | solution.py:334
  128.4 2.2 %copy-done.2 = bf16[1024,2048]{1,0:T(8,128)(2,1)S(1)} copy-done((bf16[1024,2048]{1,0:T(8,128)(2,1)S(1)}, bf16[1024,2048]{1,0:T(8,128)(2,1)}, u32[]{:S(2)}) %copy-start.2) | copy-done | bytes 4194328
  130.6 2.6 %from_boxes.2.own_ref = bf16[256,1024]{1,0:T(8,128)(2,1)S(1)} custom-call(bf16[8,512,128]{2,1,0:T(8,128)(2,1)S(1)} %all-to-all-done.2.got_ref, bf16[1024,2048]{1,0:T(8,128)(2,1)S(1)} %copy-done.2), custom_call_target="tpu_custom_call" | custom-call | flops 1000000 | bytes 1000000 | tf_op jit(solution)/shard_map/from_boxes/pallas_call | solution.py:379
  133.2 4.7 %collective-permute-done.7.other_ref = bf16[256,1024]{1,0:T(8,128)(2,1)S(1)} collective-permute-done((bf16[256,1024]{1,0:T(8,128)(2,1)S(1)}, bf16[256,1024]{1,0:T(8,128)(2,1)S(1)}, u32[]{:S(2)}, u32[]{:S(2)}) %collective-permute-start.7) | collective-permute-done | bytes 524320 | tf_op jit(solution)/shard_map/ppermute | solution.py:45
  138.0 3.1 %far_part.1 = f32[2,8,8192]{2,1,0:T(8,128)} custom-call(s32[1]{0:T(128)} %bitcast.hi_ref, bf16[256,1024]{1,0:T(8,128)(2,1)S(1)} %from_boxes.2.own_ref, bf16[256,1024]{1,0:T(8,128)(2,1)S(1)} %collective-permute-done.7.other_ref, bf16[2,8192,128]{2,1,0:T(8,128)(2,1)S(1)} %bitcast.20, f32[2,8,8192]{2,1,0:T(8,128)S(1)} %copy-done.9), custom_call_target="tpu_custom_call" | custom-call | flops 1000000 | bytes 1000000 | tf_op jit(solution)/shard_map/far_part/pallas_call | solution.py:429
  (54 shorter events, 9.8 us)
Async XLA Ops:
  0.0 26.4 %copy-start.11 = (s32[1024,12]{0,1:T(8,128)S(1)}, s32[1024,12]{0,1:T(8,128)}, u32[]{:S(2)}) copy-start(s32[1024,12]{0,1:T(8,128)} %param.18) | copy-start | bytes 147460
  0.0 26.7 %copy-start.10 = (s32[1024,12]{0,1:T(8,128)S(1)}, s32[1024,12]{0,1:T(8,128)}, u32[]{:S(2)}) copy-start(s32[1024,12]{0,1:T(8,128)} %param.19) | copy-start | bytes 147460
  0.0 29.4 %collective-permute-start.3 = (bf16[2,8,8192]{2,1,0:T(8,128)(2,1)}, bf16[2,8,8192]{2,1,0:T(8,128)(2,1)S(1)}, u32[]{:S(2)}, u32[]{:S(2)}) collective-permute-start(bf16[2,8,8192]{2,1,0:T(8,128)(2,1)} %own_ref.1), channel_id=1, source_target_pairs={{1,2},{3,4},{5,6},{7,8},{9,10},{11,12},{13,14},{15,16},{17,18},{19... | collective-permute-start | bytes 786440 | tf_op jit(solution)/shard_map/ppermute | solution.py:38
  0.8 28.6 %collective-permute-start.4 = (bf16[2,8,8192]{2,1,0:T(8,128)(2,1)}, bf16[2,8,8192]{2,1,0:T(8,128)(2,1)S(1)}, u32[]{:S(2)}, u32[]{:S(2)}) collective-permute-start(bf16[2,8,8192]{2,1,0:T(8,128)(2,1)} %own_ref.1), channel_id=1, source_target_pairs={{0,1},{1,0},{2,3},{3,2},{4,5},{5,4},{6,7},{7,6},{8,9},{9,8},{10,11... | collective-permute-start | bytes 786440 | tf_op jit(solution)/shard_map/ppermute | solution.py:45
  6.3 21.5 %collective-permute-start.1 = (bf16[2,316,64]{2,1,0:T(8,128)(2,1)S(1)}, bf16[2,316,64]{2,1,0:T(8,128)(2,1)S(1)}, u32[]{:S(2)}, u32[]{:S(2)}) collective-permute-start(bf16[2,316,64]{2,1,0:T(8,128)(2,1)S(1)} %copy.15), channel_id=1, source_target_pairs={{0,0},{1,1},{2,2},{3,3},{16,4},{17,5},{18,6},{19,7},{4,8},{5,9},{6... | collective-permute-start | bytes 242696 | tf_op jit(solution)/shard_map/ppermute | solution.py:480
  11.8 16.1 %copy-start.12 = (s32[256,8]{0,1:T(8,128)S(1)}, s32[256,8]{0,1:T(8,128)}, u32[]{:S(2)}) copy-start(s32[256,8]{0,1:T(8,128)} %param.12) | copy-start | bytes 24580
  11.8 16.1 %copy-start.13 = (s32[256]{0:T(256)S(1)}, s32[256]{0:T(256)}, u32[]{:S(2)}) copy-start(s32[256]{0:T(256)} %param.13) | copy-start | bytes 3076
  11.8 32.3 %collective-permute-start = (bf16[256,1024]{1,0:T(8,128)(2,1)}, bf16[256,1024]{1,0:T(8,128)(2,1)S(1)}, u32[]{:S(2)}, u32[]{:S(2)}) collective-permute-start(bf16[256,1024]{1,0:T(8,128)(2,1)} %get-tuple-element.18), channel_id=1, source_target_pairs={{0,4},{4,0},{1,5},{5,1},{2,6},{6,2},{3,7},{7,3},{8,12},{12,8},{9,1... | collective-permute-start | bytes 1572872 | tf_op jit(solution)/shard_map/ppermute | solution.py:45
  22.8 29.8 %all-to-all-start = ((bf16[8,512,128]{2,1,0:T(8,128)(2,1)}), bf16[8,512,128]{2,1,0:T(8,128)(2,1)S(1)}, u32[]{:S(2)}, u32[]{:S(2)}) async-start(bf16[8,512,128]{2,1,0:T(8,128)(2,1)} %get-tuple-element.22), calls=%async_computation | async-start | bytes 2097152 | tf_op jit(solution)/shard_map/all_to_all | solution.py:445
  27.8 1.5 %collective-permute-start.2 = (bf16[2,316,64]{2,1,0:T(8,128)(2,1)S(1)}, bf16[2,316,64]{2,1,0:T(8,128)(2,1)S(1)}, u32[]{:S(2)}, u32[]{:S(2)}) collective-permute-start(bf16[2,316,64]{2,1,0:T(8,128)(2,1)S(1)} %collective-permute-done.1), channel_id=1, source_target_pairs={{0,1},{1,0},{2,3},{3,2},{4,5},{5,4},{6,7},{7,6},{8,9},{9,8},{10,11... | collective-permute-start | bytes 242696 | tf_op jit(solution)/shard_map/ppermute | solution.py:45
  44.0 2.2 %copy-start = (bf16[1024,2048]{1,0:T(8,128)(2,1)S(1)}, bf16[1024,2048]{1,0:T(8,128)(2,1)}, u32[]{:S(2)}) copy-start(bf16[1024,2048]{1,0:T(8,128)(2,1)} %get-tuple-element.24.mat_ref) | copy-start | bytes 12582916
  52.7 19.9 %all-to-all-start.1 = ((bf16[8,512,128]{2,1,0:T(8,128)(2,1)}), bf16[8,512,128]{2,1,0:T(8,128)(2,1)S(1)}, u32[]{:S(2)}, u32[]{:S(2)}) async-start(bf16[8,512,128]{2,1,0:T(8,128)(2,1)} %to_boxes_again.1), calls=%async_computation.1 | async-start | bytes 2097152 | tf_op jit(solution)/shard_map/all_to_all | solution.py:445
  57.5 15.1 %collective-permute-start.5 = (bf16[256,16,128]{2,1,0:T(8,128)(2,1)S(1)}, bf16[256,16,128]{2,1,0:T(8,128)(2,1)S(1)}, u32[]{:S(2)}, u32[]{:S(2)}) collective-permute-start(bf16[256,16,128]{2,1,0:T(8,128)(2,1)S(1)} %bitcast.21), channel_id=1, source_target_pairs={{0,1},{1,0},{2,3},{3,2},{4,5},{5,4},{6,7},{7,6},{8,9},{9,8},{10,11... | collective-permute-start | bytes 3145736 | tf_op jit(solution)/shard_map/ppermute | solution.py:45
  72.6 2.7 %collective-permute-start.6 = (bf16[256,16,128]{2,1,0:T(8,128)(2,1)S(1)}, bf16[256,16,128]{2,1,0:T(8,128)(2,1)S(1)}, u32[]{:S(2)}, u32[]{:S(2)}) collective-permute-start(bf16[256,16,128]{2,1,0:T(8,128)(2,1)S(1)} %bitcast.24), channel_id=1, source_target_pairs={{0,1},{1,0},{2,3},{3,2},{4,5},{5,4},{6,7},{7,6},{8,9},{9,8},{10,11... | collective-permute-start | bytes 3145736 | tf_op jit(solution)/shard_map/ppermute | solution.py:45
  72.6 12.1 %copy-start.5 = (bf16[256,16,128]{2,1,0:T(8,128)(2,1)}, bf16[256,16,128]{2,1,0:T(8,128)(2,1)S(1)}, u32[]{:S(2)}) copy-start(bf16[256,16,128]{2,1,0:T(8,128)(2,1)S(1)} %collective-permute-done.5.two_ref) | copy-start | bytes 3145732
  75.3 8.5 %copy-start.7 = (bf16[256,16,128]{2,1,0:T(8,128)(2,1)}, bf16[256,16,128]{2,1,0:T(8,128)(2,1)S(1)}, u32[]{:S(2)}) copy-start(bf16[256,16,128]{2,1,0:T(8,128)(2,1)S(1)} %collective-permute-done.6.four_ref) | copy-start | bytes 3145732
  84.8 19.5 %all-to-all-start.3 = ((bf16[8,512,128]{2,1,0:T(8,128)(2,1)}), bf16[8,512,128]{2,1,0:T(8,128)(2,1)S(1)}, u32[]{:S(2)}, u32[]{:S(2)}) async-start(bf16[8,512,128]{2,1,0:T(8,128)(2,1)} %bitcast.27), calls=%async_computation.3 | async-start | bytes 2097152 | tf_op jit(solution)/shard_map/all_to_all | solution.py:445
  88.3 1.2 copy-start.6
  104.2 24.2 %all-to-all-start.2 = ((bf16[8,512,128]{2,1,0:T(8,128)(2,1)}), bf16[8,512,128]{2,1,0:T(8,128)(2,1)S(1)}, u32[]{:S(2)}, u32[]{:S(2)}) async-start(bf16[8,512,128]{2,1,0:T(8,128)(2,1)} %bitcast.5), calls=%async_computation.2 | async-start | bytes 2097152 | tf_op jit(solution)/shard_map/all_to_all | solution.py:445
  107.8 2.2 %copy-start.1 = (bf16[1024,2048]{1,0:T(8,128)(2,1)S(1)}, bf16[1024,2048]{1,0:T(8,128)(2,1)}, u32[]{:S(2)}) copy-start(bf16[1024,2048]{1,0:T(8,128)(2,1)} %get-tuple-element.24.mat_ref) | copy-start | bytes 12582916
  112.6 25.4 %collective-permute-start.7 = (bf16[256,1024]{1,0:T(8,128)(2,1)S(1)}, bf16[256,1024]{1,0:T(8,128)(2,1)S(1)}, u32[]{:S(2)}, u32[]{:S(2)}) collective-permute-start(bf16[256,1024]{1,0:T(8,128)(2,1)S(1)} %from_boxes.3), channel_id=1, source_target_pairs={{0,4},{4,0},{1,5},{5,1},{2,6},{6,2},{3,7},{7,3},{8,12},{12,8},{9,1... | collective-permute-start | bytes 1572872 | tf_op jit(solution)/shard_map/ppermute | solution.py:45
  128.4 2.2 %copy-start.2 = (bf16[1024,2048]{1,0:T(8,128)(2,1)S(1)}, bf16[1024,2048]{1,0:T(8,128)(2,1)}, u32[]{:S(2)}) copy-start(bf16[1024,2048]{1,0:T(8,128)(2,1)} %get-tuple-element.24.mat_ref) | copy-start | bytes 12582916
  130.6 7.4 %copy-start.3 = (bf16[2,256,32,128]{3,2,1,0:T(8,128)(2,1)S(1)}, bf16[2,256,32,128]{3,2,1,0:T(8,128)(2,1)}, u32[]{:S(2)}) copy-start(bf16[2,256,32,128]{3,2,1,0:T(8,128)(2,1)} %param.14) | copy-start | bytes 12582916
  130.6 7.4 %copy-start.9 = (f32[2,8,8192]{2,1,0:T(8,128)S(1)}, f32[2,8,8192]{2,1,0:T(8,128)}, u32[]{:S(2)}) copy-start(f32[2,8,8192]{2,1,0:T(8,128)} %near_part.1.near_ref) | copy-start | bytes 1572868
  (2 other events, 2.2 us)

commit v6 on v5

--- a/solution.py
+++ b/solution.py
@@ -32,13 +32,10 @@
     return pl.CostEstimate(flops=10**6, bytes_accessed=megabytes * 10**6, transcendentals=0)
 
 
-def neighbours(array):
+def next_chip(array):
     size = lax.axis_size(ALL)
     pairs = [(i, i + 1) for i in range(1, size - 1, 2)] + [(i + 1, i) for i in range(1, size - 1, 2)]
-    outside = lax.ppermute(array, ALL, pairs)
-    inside = across(array, "core")
-    first = lax.axis_index("core") == 0
-    return jnp.where(first, outside, inside), jnp.where(first, inside, outside)
+    return lax.ppermute(array, ALL, pairs)
 
 
 def across(array, axis):
@@ -260,7 +257,7 @@
                 pltpu.SemaphoreType.DMA((4,)),
             ],
         ),
-        out_shape=jax.ShapeDtypeStruct((targets, 2 * R, LANES), BF16),
+        out_shape=pltpu.HBM((targets, 2 * R, LANES), BF16),
         compiler_params=LESS,
         cost_estimate=cost(25),
         name="translate",
@@ -477,12 +474,12 @@
         for m in range(mids)
         for c in range(2)
     ]
-    mine = lax.ppermute(translation, ALL, pairs)
+    mine = lax.ppermute(jnp.swapaxes(translation, 1, 2), ALL, pairs)
     other = across(mine, "core").astype(F32)
     mine = mine.astype(F32)
     low = jnp.where(core == 0, mine, other)
     high = jnp.where(core == 0, other, mine)
-    operator = padded(jnp.concatenate([low, high], axis=2))
+    operator = padded(jnp.swapaxes(jnp.concatenate([low, high], axis=1), 1, 2))
     return jnp.pad(operator, ((0, 0), (0, -operator.shape[1] % R), (0, 0)))
 
 
@@ -532,16 +529,20 @@
     rows_own = to_owners(boxes_own, samples)
     swapped_own = across(rows_own, "core")
     operators = operator_table(translation)
-    below, above = neighbours(currents)
-    leaf_partner, lists, index, operators, below, above = lax.optimization_barrier(
-        (leaf_partner, lists, index, operators, below, above)
+    inside = across(currents, "core")
+    leaf_partner, lists, index, operators, inside = lax.optimization_barrier(
+        (leaf_partner, lists, index, operators, inside)
     )
     rows_partner = to_owners(to_boxes_again(leaf_partner, matrix), samples)
     parts = (rows_own, swapped_own, rows_partner, across(rows_partner, "core"))
 
     fields_partner = translate(lists[1], operators, parts)
+    fields_partner, late_currents = lax.optimization_barrier((fields_partner, currents))
+    outside = next_chip(late_currents)
+    fields_own = translate(lists[0], operators, parts)
+    fields_own, outside = lax.optimization_barrier((fields_own, outside))
     down_partner = from_boxes(from_owners(fields_partner, rows, samples), matrix)
-    fields_own = translate(lists[0], operators, parts)
+    below, above = jnp.where(core == 0, outside, inside), jnp.where(core == 0, inside, outside)
     down_partner, index = lax.optimization_barrier((down_partner, index))
     down_other = across(down_partner, "hi")
     near_field = near_part(index, below, currents, above, near_blocks)

time: 142 us -> 152 us (1.070)
  waiting for transfers between devices: 43.9 us -> 50 us
  starting transfers between devices: 28.1 us -> 30.9 us
    ppermute x6, waiting for transfers between devices: 21.4 us -> 32 us  [across(): return lax.ppermute(array, axis, [(0, 1), (1, 0)])]
    all_to_all x4, starting transfers between devices: 15.5 us -> 22.2 us  [swapped(): lax.all_to_all(array, INSIDE, split_axis=0, concat_axis=0, tiled=True)]
    all_to_all x4, waiting for transfers between devices: 22.6 us -> 18 us  [swapped(): lax.all_to_all(array, INSIDE, split_axis=0, concat_axis=0, tiled=True)]
    ppermute x6, starting transfers between devices: 11.1 us -> 6.62 us  [across(): return lax.ppermute(array, axis, [(0, 1), (1, 0)])]
    unnamed x31 -> x33, local copies, waits for them, and re-layouts: 11.4 us -> 10.5 us
  transfers between devices with their start and end apart: 12 -> 12, of which waited for: 7 -> 6; matrix products, arithmetic and copies ran while one was open for 3% -> 3% of each run, Pallas kernels for 30% -> 22%
where the time goes in v6:
time: 152 us; the launch traced here: 151 us
  Pallas kernels  55.3 us (36%)
  waiting for transfers between devices  50 us (33%)
  starting transfers between devices  30.9 us (20%)
  local copies, waits for them, and re-layouts  12.2 us (8%)
  other arithmetic  2.38 us (2%)
    ppermute x6, waiting for transfers between devices, across(): return lax.ppermute(array, axis, [(0, 1), (1, 0)])  32 us
    all_to_all x4, starting transfers between devices, swapped(): lax.all_to_all(array, INSIDE, split_axis=0, concat_axis=0, tiled=True)  22.2 us
    pallas_call x2, Pallas kernels, translate(): pl.pallas_call(functools.partial(translate_kernel, group=8), grid_spec=pl...  18.8 us
    all_to_all x4, waiting for transfers between devices, swapped(): lax.all_to_all(array, INSIDE, split_axis=0, concat_axis=0, tiled=True)  18 us
    pallas_call x1, Pallas kernels, near_part(): pl.pallas_call(near_kernel, grid_spec=pltpu.PrefetchScalarGridSpec(num_sc...  15.8 us
    unnamed x33, local copies, waits for them, and re-layouts  10.5 us
    ppermute x6, starting transfers between devices, across(): return lax.ppermute(array, axis, [(0, 1), (1, 0)])  6.62 us
    pallas_call x2, Pallas kernels, from_boxes(): pl.pallas_call(down_kernel, grid=(steps,), in_specs=[pl.BlockSpec((chips,...  5.19 us
  transfers between devices with their start and end apart: 12, of which 6 were waited for; matrix products, arithmetic and copies ran while one was open for 3% of the time, Pallas kernels for 22%

profile of v6, /device:TPU:0, one launch (start us, length us, event | category | flops | bytes accessed | tf_op | source)
XLA Modules:
  0.0 151.0 jit_solution(12252391180571404017)
XLA Ops:
  0.0 4.8 %leaves.1 = (bf16[256,1024]{1,0:T(8,128)(2,1)}, bf16[256,1024]{1,0:T(8,128)(2,1)}) custom-call(s32[1]{0:T(128)} %bitcast.hi_ref, bf16[2,8,8192]{2,1,0:T(8,128)(2,1)} %own_ref.1, bf16[2,8192,128]{2,1,0:T(8,128)(2,1)} %bitcast.22), custom_call_target="tpu_custom_call" | custom-call | flops 1000000 | bytes 1000000 | tf_op jit(solution)/shard_map/leaves/pallas_call | solution.py:100
  4.9 4.6 %to_boxes.1 = (bf16[8,512,128]{2,1,0:T(8,128)(2,1)}, bf16[1024,2048]{1,0:T(8,128)(2,1)}) custom-call(bf16[256,1024]{1,0:T(8,128)(2,1)} %get-tuple-element.24.lhs_ref, bf16[64,1024]{1,0:T(8,128)(2,1)} %interp_ref.1, f32[8,1024]{1,0:T(8,128)} %angle_ref.1), custom_call_target="tpu_custom_call" | custom-call | flops 1000000 | bytes 1000000 | tf_op jit(solution)/shard_map/to_boxes/pallas_call | solution.py:153
  9.5 6.2 %all-to-all-start = ((bf16[8,512,128]{2,1,0:T(8,128)(2,1)}), bf16[8,512,128]{2,1,0:T(8,128)(2,1)S(1)}, u32[]{:S(2)}, u32[]{:S(2)}) async-start(bf16[8,512,128]{2,1,0:T(8,128)(2,1)} %get-tuple-element.25), calls=%async_computation | async-start | bytes 2097152 | tf_op jit(solution)/shard_map/all_to_all | solution.py:442
  16.6 5.6 %collective-permute-start = (bf16[256,1024]{1,0:T(8,128)(2,1)}, bf16[256,1024]{1,0:T(8,128)(2,1)S(1)}, u32[]{:S(2)}, u32[]{:S(2)}) collective-permute-start(bf16[256,1024]{1,0:T(8,128)(2,1)} %get-tuple-element.21), channel_id=1, source_target_pairs={{0,4},{4,0},{1,5},{5,1},{2,6},{6,2},{3,7},{7,3},{8,12},{12,8},{9,1... | collective-permute-start | bytes 1572872 | tf_op jit(solution)/shard_map/ppermute | solution.py:42
  25.3 27.5 %collective-permute-done.lhs_ref = bf16[256,1024]{1,0:T(8,128)(2,1)S(1)} collective-permute-done((bf16[256,1024]{1,0:T(8,128)(2,1)}, bf16[256,1024]{1,0:T(8,128)(2,1)S(1)}, u32[]{:S(2)}, u32[]{:S(2)}) %collective-permute-start) | collective-permute-done | bytes 524320 | tf_op jit(solution)/shard_map/ppermute | solution.py:42
  52.7 2.2 %copy-done = bf16[1024,2048]{1,0:T(8,128)(2,1)S(1)} copy-done((bf16[1024,2048]{1,0:T(8,128)(2,1)S(1)}, bf16[1024,2048]{1,0:T(8,128)(2,1)}, u32[]{:S(2)}) %copy-start) | copy-done | bytes 4194328
  54.9 3.0 %to_boxes_again.1 = bf16[8,512,128]{2,1,0:T(8,128)(2,1)} custom-call(bf16[256,1024]{1,0:T(8,128)(2,1)S(1)} %collective-permute-done.lhs_ref, bf16[1024,2048]{1,0:T(8,128)(2,1)S(1)} %copy-done), custom_call_target="tpu_custom_call" | custom-call | flops 1000000 | bytes 6000000 | tf_op jit(solution)/shard_map/to_boxes_again/pallas_call | solution.py:179
  58.0 3.6 %all-to-all-start.1 = ((bf16[8,512,128]{2,1,0:T(8,128)(2,1)}), bf16[8,512,128]{2,1,0:T(8,128)(2,1)S(1)}, u32[]{:S(2)}, u32[]{:S(2)}) async-start(bf16[8,512,128]{2,1,0:T(8,128)(2,1)} %to_boxes_again.1), calls=%async_computation.1 | async-start | bytes 2097152 | tf_op jit(solution)/shard_map/all_to_all | solution.py:442
  61.6 15.4 %all-to-all-done.1 = bf16[8,512,128]{2,1,0:T(8,128)(2,1)S(1)} async-done(((bf16[8,512,128]{2,1,0:T(8,128)(2,1)}), bf16[8,512,128]{2,1,0:T(8,128)(2,1)S(1)}, u32[]{:S(2)}, u32[]{:S(2)}) %all-to-all-start.1) | async-done | bytes 1048608 | tf_op jit(solution)/shard_map/all_to_all | solution.py:442
  77.0 2.6 %collective-permute-done.5.four_ref = bf16[256,16,128]{2,1,0:T(8,128)(2,1)S(1)} collective-permute-done((bf16[256,16,128]{2,1,0:T(8,128)(2,1)S(1)}, bf16[256,16,128]{2,1,0:T(8,128)(2,1)S(1)}, u32[]{:S(2)}, u32[]{:S(2)}) %collective-permute-start.5) | collective-permute-done | bytes 1048608 | tf_op jit(solution)/shard_map/ppermute | solution.py:42
  79.7 9.4 %translate.3 = bf16[256,16,128]{2,1,0:T(8,128)(2,1)} custom-call(s32[6144]{0:T(1024)S(1)} %select_n.105.list_ref, f32[2,320,128]{2,1,0:T(8,128)S(1)} %pad.4.oper_ref, bf16[256,16,128]{2,1,0:T(8,128)(2,1)S(1)} %bitcast.25, bf16[256,16,128]{2,1,0:T(8,128)(2,1)S(1)} %collective-permute-done.4.two_ref, bf16[256,16,128]{2,1,0:T(8,128)(2,1)S(1)} %bitcast.28, ...), custom_call_target="tpu_custom_call" | custom-call | flops 1000000 | bytes 25000000 | tf_op jit(solution)/shard_map/translate/pallas_call | solution.py:247
  90.0 3.6 %all-to-all-start.3 = ((bf16[8,512,128]{2,1,0:T(8,128)(2,1)}), bf16[8,512,128]{2,1,0:T(8,128)(2,1)S(1)}, u32[]{:S(2)}, u32[]{:S(2)}) async-start(bf16[8,512,128]{2,1,0:T(8,128)(2,1)} %bitcast.32), calls=%async_computation.3 | async-start | bytes 2097152 | tf_op jit(solution)/shard_map/all_to_all | solution.py:442
  93.6 1.4 collective-permute-start.6
  97.5 9.4 %translate.2 = bf16[256,16,128]{2,1,0:T(8,128)(2,1)} custom-call(s32[6144]{0:T(1024)S(1)} %select_n.103.list_ref, f32[2,320,128]{2,1,0:T(8,128)S(1)} %pad.4.oper_ref, bf16[256,16,128]{2,1,0:T(8,128)(2,1)S(1)} %bitcast.26, bf16[256,16,128]{2,1,0:T(8,128)(2,1)S(1)} %copy-done.5, bf16[256,16,128]{2,1,0:T(8,128)(2,1)S(1)} %bitcast.29, ...), custom_call_target="tpu_custom_call" | custom-call | flops 1000000 | bytes 25000000 | tf_op jit(solution)/shard_map/translate/pallas_call | solution.py:247
  106.9 2.6 %all-to-all-done.3.got_ref = bf16[8,512,128]{2,1,0:T(8,128)(2,1)S(1)} async-done(((bf16[8,512,128]{2,1,0:T(8,128)(2,1)}), bf16[8,512,128]{2,1,0:T(8,128)(2,1)S(1)}, u32[]{:S(2)}, u32[]{:S(2)}) %all-to-all-start.3) | async-done | bytes 1048608 | tf_op jit(solution)/shard_map/all_to_all | solution.py:442
  109.5 8.8 %all-to-all-start.2 = ((bf16[8,512,128]{2,1,0:T(8,128)(2,1)}), bf16[8,512,128]{2,1,0:T(8,128)(2,1)S(1)}, u32[]{:S(2)}, u32[]{:S(2)}) async-start(bf16[8,512,128]{2,1,0:T(8,128)(2,1)} %bitcast.31), calls=%async_computation.2 | async-start | bytes 2097152 | tf_op jit(solution)/shard_map/all_to_all | solution.py:442
  118.3 2.2 %copy-done.1 = bf16[1024,2048]{1,0:T(8,128)(2,1)S(1)} copy-done((bf16[1024,2048]{1,0:T(8,128)(2,1)S(1)}, bf16[1024,2048]{1,0:T(8,128)(2,1)}, u32[]{:S(2)}) %copy-start.1) | copy-done | bytes 4194328
  120.5 2.6 %from_boxes.3 = bf16[256,1024]{1,0:T(8,128)(2,1)S(1)} custom-call(bf16[8,512,128]{2,1,0:T(8,128)(2,1)S(1)} %all-to-all-done.3.got_ref, bf16[1024,2048]{1,0:T(8,128)(2,1)S(1)} %copy-done.1), custom_call_target="tpu_custom_call" | custom-call | flops 1000000 | bytes 1000000 | tf_op jit(solution)/shard_map/from_boxes/pallas_call | solution.py:376
  123.9 1.9 %broadcast_select_fusion = (bf16[2,8,8192]{2,1,0:T(8,128)(2,1)}, bf16[2,8,8192]{2,1,0:T(8,128)(2,1)}) fusion(bf16[2,8,8192]{2,1,0:T(8,128)(2,1)} %collective-permute-done.3, bf16[2,8,8192]{2,1,0:T(8,128)(2,1)} %collective-permute-done.6, pred[]{:T(512)S(6)} %eq.17), kind=kLoop, calls=%fused_computation.4 | loop fusion | flops 262144 | bytes 1048577 | tf_op jit(solution)/shard_map/jit(_where)/select_n | solution.py:545
  125.8 15.8 %near_part.1.near_ref = f32[2,8,8192]{2,1,0:T(8,128)} custom-call(s32[2048]{0:T(1024)} %reshape.37.idx_ref, bf16[2,8,8192]{2,1,0:T(8,128)(2,1)} %get-tuple-element.38.below_ref, bf16[2,8,8192]{2,1,0:T(8,128)(2,1)} %own_ref.1, bf16[2,8,8192]{2,1,0:T(8,128)(2,1)} %get-tuple-element.37.above_ref, bf16[2,8192,256]{2,1,0:T(8,128)(2,1)} %bitcast.30), custom_call_target="tpu_custom_call" | custom-call | flops 1000000 | bytes 1000000 | tf_op jit(solution)/shard_map/near_part/pallas_call | solution.py:331
  141.5 2.2 %copy-done.2 = bf16[1024,2048]{1,0:T(8,128)(2,1)S(1)} copy-done((bf16[1024,2048]{1,0:T(8,128)(2,1)S(1)}, bf16[1024,2048]{1,0:T(8,128)(2,1)}, u32[]{:S(2)}) %copy-start.2) | copy-done | bytes 4194328
  143.7 2.6 %from_boxes.2.own_ref = bf16[256,1024]{1,0:T(8,128)(2,1)S(1)} custom-call(bf16[8,512,128]{2,1,0:T(8,128)(2,1)S(1)} %all-to-all-done.2.got_ref, bf16[1024,2048]{1,0:T(8,128)(2,1)S(1)} %copy-done.2), custom_call_target="tpu_custom_call" | custom-call | flops 1000000 | bytes 1000000 | tf_op jit(solution)/shard_map/from_boxes/pallas_call | solution.py:376
  146.3 1.6 %collective-permute-done.7.other_ref = bf16[256,1024]{1,0:T(8,128)(2,1)S(1)} collective-permute-done((bf16[256,1024]{1,0:T(8,128)(2,1)S(1)}, bf16[256,1024]{1,0:T(8,128)(2,1)S(1)}, u32[]{:S(2)}, u32[]{:S(2)}) %collective-permute-start.7) | collective-permute-done | bytes 524320 | tf_op jit(solution)/shard_map/ppermute | solution.py:42
  147.9 3.1 %far_part.1 = f32[2,8,8192]{2,1,0:T(8,128)} custom-call(s32[1]{0:T(128)} %bitcast.hi_ref, bf16[256,1024]{1,0:T(8,128)(2,1)S(1)} %from_boxes.2.own_ref, bf16[256,1024]{1,0:T(8,128)(2,1)S(1)} %collective-permute-done.7.other_ref, bf16[2,8192,128]{2,1,0:T(8,128)(2,1)S(1)} %bitcast.23, f32[2,8,8192]{2,1,0:T(8,128)S(1)} %copy-done.8), custom_call_target="tpu_custom_call" | custom-call | flops 1000000 | bytes 1000000 | tf_op jit(solution)/shard_map/far_part/pallas_call | solution.py:426
  (57 shorter events, 8.1 us)
Async XLA Ops:
  0.0 15.7 %copy-start.9 = (bf16[2,8,8192]{2,1,0:T(8,128)(2,1)S(1)}, bf16[2,8,8192]{2,1,0:T(8,128)(2,1)}, u32[]{:S(2)}) copy-start(bf16[2,8,8192]{2,1,0:T(8,128)(2,1)} %own_ref.1) | copy-start | bytes 786436
  0.0 15.8 %copy-start.10 = (bf16[2,316,64]{1,2,0:T(8,128)(2,1)S(1)}, bf16[2,316,64]{1,2,0:T(8,128)(2,1)}, u32[]{:S(2)}) copy-start(bf16[2,316,64]{1,2,0:T(8,128)(2,1)} %param.17) | copy-start | bytes 242692
  0.0 22.2 %copy-start.12 = (s32[1024,12]{0,1:T(8,128)S(1)}, s32[1024,12]{0,1:T(8,128)}, u32[]{:S(2)}) copy-start(s32[1024,12]{0,1:T(8,128)} %param.18) | copy-start | bytes 147460
  0.0 22.5 %copy-start.11 = (s32[1024,12]{0,1:T(8,128)S(1)}, s32[1024,12]{0,1:T(8,128)}, u32[]{:S(2)}) copy-start(s32[1024,12]{0,1:T(8,128)} %param.19) | copy-start | bytes 147460
  4.8 18.8 %copy-start.13 = (s32[256,8]{0,1:T(8,128)S(1)}, s32[256,8]{0,1:T(8,128)}, u32[]{:S(2)}) copy-start(s32[256,8]{0,1:T(8,128)} %param.12) | copy-start | bytes 24580
  4.8 18.8 %copy-start.14 = (s32[256]{0:T(256)S(1)}, s32[256]{0:T(256)}, u32[]{:S(2)}) copy-start(s32[256]{0:T(256)} %param.13) | copy-start | bytes 3076
  9.5 48.5 %all-to-all-start = ((bf16[8,512,128]{2,1,0:T(8,128)(2,1)}), bf16[8,512,128]{2,1,0:T(8,128)(2,1)S(1)}, u32[]{:S(2)}, u32[]{:S(2)}) async-start(bf16[8,512,128]{2,1,0:T(8,128)(2,1)} %get-tuple-element.25), calls=%async_computation | async-start | bytes 2097152 | tf_op jit(solution)/shard_map/all_to_all | solution.py:442
  15.7 9.6 %collective-permute-start.3 = (bf16[2,8,8192]{2,1,0:T(8,128)(2,1)S(1)}, bf16[2,8,8192]{2,1,0:T(8,128)(2,1)}, u32[]{:S(2)}, u32[]{:S(2)}) collective-permute-start(bf16[2,8,8192]{2,1,0:T(8,128)(2,1)S(1)} %copy-done.9), channel_id=1, source_target_pairs={{0,1},{1,0},{2,3},{3,2},{4,5},{5,4},{6,7},{7,6},{8,9},{9,8},{10,11... | collective-permute-start | bytes 786440 | tf_op jit(solution)/shard_map/ppermute | solution.py:42
  15.9 7.6 %collective-permute-start.1 = (bf16[2,64,316]{1,2,0:T(8,128)(2,1)S(1)}, bf16[2,64,316]{1,2,0:T(8,128)(2,1)S(1)}, u32[]{:S(2)}, u32[]{:S(2)}) collective-permute-start(bf16[2,64,316]{1,2,0:T(8,128)(2,1)S(1)} %bitcast.33), channel_id=1, source_target_pairs={{0,0},{1,1},{2,2},{3,3},{16,4},{17,5},{18,6},{19,7},{4,8},{5,9},{6... | collective-permute-start | bytes 242696 | tf_op jit(solution)/shard_map/ppermute | solution.py:477
  16.6 36.1 %collective-permute-start = (bf16[256,1024]{1,0:T(8,128)(2,1)}, bf16[256,1024]{1,0:T(8,128)(2,1)S(1)}, u32[]{:S(2)}, u32[]{:S(2)}) collective-permute-start(bf16[256,1024]{1,0:T(8,128)(2,1)} %get-tuple-element.21), channel_id=1, source_target_pairs={{0,4},{4,0},{1,5},{5,1},{2,6},{6,2},{3,7},{7,3},{8,12},{12,8},{9,1... | collective-permute-start | bytes 1572872 | tf_op jit(solution)/shard_map/ppermute | solution.py:42
  23.6 1.5 collective-permute-start.2
  52.7 2.2 %copy-start = (bf16[1024,2048]{1,0:T(8,128)(2,1)S(1)}, bf16[1024,2048]{1,0:T(8,128)(2,1)}, u32[]{:S(2)}) copy-start(bf16[1024,2048]{1,0:T(8,128)(2,1)} %get-tuple-element.27.mat_ref) | copy-start | bytes 12582916
  58.0 19.1 %all-to-all-start.1 = ((bf16[8,512,128]{2,1,0:T(8,128)(2,1)}), bf16[8,512,128]{2,1,0:T(8,128)(2,1)S(1)}, u32[]{:S(2)}, u32[]{:S(2)}) async-start(bf16[8,512,128]{2,1,0:T(8,128)(2,1)} %to_boxes_again.1), calls=%async_computation.1 | async-start | bytes 2097152 | tf_op jit(solution)/shard_map/all_to_all | solution.py:442
  61.5 15.5 %collective-permute-start.4 = (bf16[256,16,128]{2,1,0:T(8,128)(2,1)S(1)}, bf16[256,16,128]{2,1,0:T(8,128)(2,1)S(1)}, u32[]{:S(2)}, u32[]{:S(2)}) collective-permute-start(bf16[256,16,128]{2,1,0:T(8,128)(2,1)S(1)} %bitcast.24), channel_id=1, source_target_pairs={{0,1},{1,0},{2,3},{3,2},{4,5},{5,4},{6,7},{7,6},{8,9},{9,8},{10,11... | collective-permute-start | bytes 3145736 | tf_op jit(solution)/shard_map/ppermute | solution.py:42
  77.0 2.7 %collective-permute-start.5 = (bf16[256,16,128]{2,1,0:T(8,128)(2,1)S(1)}, bf16[256,16,128]{2,1,0:T(8,128)(2,1)S(1)}, u32[]{:S(2)}, u32[]{:S(2)}) collective-permute-start(bf16[256,16,128]{2,1,0:T(8,128)(2,1)S(1)} %bitcast.27), channel_id=1, source_target_pairs={{0,1},{1,0},{2,3},{3,2},{4,5},{5,4},{6,7},{7,6},{8,9},{9,8},{10,11... | collective-permute-start | bytes 3145736 | tf_op jit(solution)/shard_map/ppermute | solution.py:42
  77.0 13.0 %copy-start.4 = (bf16[256,16,128]{2,1,0:T(8,128)(2,1)}, bf16[256,16,128]{2,1,0:T(8,128)(2,1)S(1)}, u32[]{:S(2)}) copy-start(bf16[256,16,128]{2,1,0:T(8,128)(2,1)S(1)} %collective-permute-done.4.two_ref) | copy-start | bytes 3145732
  90.0 19.5 %all-to-all-start.3 = ((bf16[8,512,128]{2,1,0:T(8,128)(2,1)}), bf16[8,512,128]{2,1,0:T(8,128)(2,1)S(1)}, u32[]{:S(2)}, u32[]{:S(2)}) async-start(bf16[8,512,128]{2,1,0:T(8,128)(2,1)} %bitcast.32), calls=%async_computation.3 | async-start | bytes 2097152 | tf_op jit(solution)/shard_map/all_to_all | solution.py:442
  93.6 13.3 %collective-permute-start.6 = (bf16[2,8,8192]{2,1,0:T(8,128)(2,1)}, bf16[2,8,8192]{2,1,0:T(8,128)(2,1)}, u32[]{:S(2)}, u32[]{:S(2)}) collective-permute-start(bf16[2,8,8192]{2,1,0:T(8,128)(2,1)} %own_ref.1), channel_id=1, source_target_pairs={{1,2},{3,4},{5,6},{7,8},{9,10},{11,12},{13,14},{15,16},{17,18},{19... | collective-permute-start | bytes 786440 | tf_op jit(solution)/shard_map/ppermute | solution.py:38
  109.5 32.0 %all-to-all-start.2 = ((bf16[8,512,128]{2,1,0:T(8,128)(2,1)}), bf16[8,512,128]{2,1,0:T(8,128)(2,1)S(1)}, u32[]{:S(2)}, u32[]{:S(2)}) async-start(bf16[8,512,128]{2,1,0:T(8,128)(2,1)} %bitcast.31), calls=%async_computation.2 | async-start | bytes 2097152 | tf_op jit(solution)/shard_map/all_to_all | solution.py:442
  118.3 2.2 %copy-start.1 = (bf16[1024,2048]{1,0:T(8,128)(2,1)S(1)}, bf16[1024,2048]{1,0:T(8,128)(2,1)}, u32[]{:S(2)}) copy-start(bf16[1024,2048]{1,0:T(8,128)(2,1)} %get-tuple-element.27.mat_ref) | copy-start | bytes 12582916
  123.1 24.8 %collective-permute-start.7 = (bf16[256,1024]{1,0:T(8,128)(2,1)S(1)}, bf16[256,1024]{1,0:T(8,128)(2,1)S(1)}, u32[]{:S(2)}, u32[]{:S(2)}) collective-permute-start(bf16[256,1024]{1,0:T(8,128)(2,1)S(1)} %from_boxes.3), channel_id=1, source_target_pairs={{0,4},{4,0},{1,5},{5,1},{2,6},{6,2},{3,7},{7,3},{8,12},{12,8},{9,1... | collective-permute-start | bytes 1572872 | tf_op jit(solution)/shard_map/ppermute | solution.py:42
  141.5 2.2 %copy-start.2 = (bf16[1024,2048]{1,0:T(8,128)(2,1)S(1)}, bf16[1024,2048]{1,0:T(8,128)(2,1)}, u32[]{:S(2)}) copy-start(bf16[1024,2048]{1,0:T(8,128)(2,1)} %get-tuple-element.27.mat_ref) | copy-start | bytes 12582916
  143.7 4.2 %copy-start.3 = (bf16[2,256,32,128]{3,2,1,0:T(8,128)(2,1)S(1)}, bf16[2,256,32,128]{3,2,1,0:T(8,128)(2,1)}, u32[]{:S(2)}) copy-start(bf16[2,256,32,128]{3,2,1,0:T(8,128)(2,1)} %param.14) | copy-start | bytes 12582916
  143.7 4.2 %copy-start.8 = (f32[2,8,8192]{2,1,0:T(8,128)S(1)}, f32[2,8,8192]{2,1,0:T(8,128)}, u32[]{:S(2)}) copy-start(f32[2,8,8192]{2,1,0:T(8,128)} %near_part.1.near_ref) | copy-start | bytes 1572868
  (3 other events, 3.4 us)

commit v7 on v5

--- a/solution.py
+++ b/solution.py
@@ -96,7 +96,7 @@
 def leaves(hi, currents, radiation):
     width = currents.shape[2]
     rows = width // WIDE * R
-    steps = 4
+    steps = 8
     per_step = width // steps
     shape = jax.ShapeDtypeStruct((rows, DEPTH), BF16)
     spec = pl.BlockSpec((rows // steps, DEPTH), lambda s, *_: (s, 0))
@@ -477,12 +477,12 @@
         for m in range(mids)
         for c in range(2)
     ]
-    mine = lax.ppermute(translation, ALL, pairs)
+    mine = lax.ppermute(jnp.swapaxes(translation, 1, 2), ALL, pairs)
     other = across(mine, "core").astype(F32)
     mine = mine.astype(F32)
     low = jnp.where(core == 0, mine, other)
     high = jnp.where(core == 0, other, mine)
-    operator = padded(jnp.concatenate([low, high], axis=2))
+    operator = padded(jnp.swapaxes(jnp.concatenate([low, high], axis=1), 1, 2))
     return jnp.pad(operator, ((0, 0), (0, -operator.shape[1] % R), (0, 0)))
 
 

time: 142 us -> 143 us (level)
  Pallas kernels: 54.3 us -> 56.5 us
    ppermute x6, waiting for transfers between devices: 21.4 us -> 19.1 us  [across(): return lax.ppermute(array, axis, [(0, 1), (1, 0)])]
    pallas_call x1, Pallas kernels: 4.77 us -> 7.01 us  [leaves(): pl.pallas_call(leaf_kernel, grid_spec=pltpu.PrefetchScalarGridSpec(num_sc...]
    all_to_all x4, waiting for transfers between devices: 22.6 us -> 24.6 us  [swapped(): lax.all_to_all(array, INSIDE, split_axis=0, concat_axis=0, tiled=True)]
  transfers between devices with their start and end apart: 12 -> 12, of which waited for: 7 -> 7; matrix products, arithmetic and copies ran while one was open for 3% -> 3% of each run, Pallas kernels for 30% -> 32%
where the time goes in v7:
time: 143 us; the launch traced here: 142 us
  Pallas kernels  56.5 us (40%)
  waiting for transfers between devices  43.7 us (31%)
  starting transfers between devices  26.8 us (19%)
  local copies, waits for them, and re-layouts  13.1 us (9%)
    all_to_all x4, waiting for transfers between devices, swapped(): lax.all_to_all(array, INSIDE, split_axis=0, concat_axis=0, tiled=True)  24.6 us
    ppermute x6, waiting for transfers between devices, across(): return lax.ppermute(array, axis, [(0, 1), (1, 0)])  19.1 us
    pallas_call x2, Pallas kernels, translate(): pl.pallas_call(functools.partial(translate_kernel, group=8), grid_spec=pl...  17.9 us
    pallas_call x1, Pallas kernels, near_part(): pl.pallas_call(near_kernel, grid_spec=pltpu.PrefetchScalarGridSpec(num_sc...  15.8 us
    all_to_all x4, starting transfers between devices, swapped(): lax.all_to_all(array, INSIDE, split_axis=0, concat_axis=0, tiled=True)  14.2 us
    unnamed x31, local copies, waits for them, and re-layouts  11.4 us
    ppermute x6, starting transfers between devices, across(): return lax.ppermute(array, axis, [(0, 1), (1, 0)])  11.1 us
    pallas_call x1, Pallas kernels, leaves(): pl.pallas_call(leaf_kernel, grid_spec=pltpu.PrefetchScalarGridSpec(num_sc...  7.01 us
  transfers between devices with their start and end apart: 12, of which 7 were waited for; matrix products, arithmetic and copies ran while one was open for 3% of the time, Pallas kernels for 32%

profile of v7, /device:TPU:0, one launch (start us, length us, event | category | flops | bytes accessed | tf_op | source)
XLA Modules:
  0.0 141.8 jit_solution(5158196918682592293)
XLA Ops:
  0.8 4.4 %collective-permute-start.4 = (bf16[2,8,8192]{2,1,0:T(8,128)(2,1)}, bf16[2,8,8192]{2,1,0:T(8,128)(2,1)S(1)}, u32[]{:S(2)}, u32[]{:S(2)}) collective-permute-start(bf16[2,8,8192]{2,1,0:T(8,128)(2,1)} %own_ref.1), channel_id=1, source_target_pairs={{0,1},{1,0},{2,3},{3,2},{4,5},{5,4},{6,7},{7,6},{8,9},{9,8},{10,11... | collective-permute-start | bytes 786440 | tf_op jit(solution)/shard_map/ppermute | solution.py:45
  7.0 7.0 %leaves.1 = (bf16[256,1024]{1,0:T(8,128)(2,1)}, bf16[256,1024]{1,0:T(8,128)(2,1)}) custom-call(s32[1]{0:T(128)} %bitcast.hi_ref, bf16[2,8,8192]{2,1,0:T(8,128)(2,1)} %own_ref.1, bf16[2,8192,128]{2,1,0:T(8,128)(2,1)} %bitcast.22), custom_call_target="tpu_custom_call" | custom-call | flops 1000000 | bytes 1000000 | tf_op jit(solution)/shard_map/leaves/pallas_call | solution.py:103
  14.0 6.5 %collective-permute-start = (bf16[256,1024]{1,0:T(8,128)(2,1)}, bf16[256,1024]{1,0:T(8,128)(2,1)S(1)}, u32[]{:S(2)}, u32[]{:S(2)}) collective-permute-start(bf16[256,1024]{1,0:T(8,128)(2,1)} %get-tuple-element.18), channel_id=1, source_target_pairs={{0,4},{4,0},{1,5},{5,1},{2,6},{6,2},{3,7},{7,3},{8,12},{12,8},{9,1... | collective-permute-start | bytes 1572872 | tf_op jit(solution)/shard_map/ppermute | solution.py:45
  20.5 4.6 %to_boxes.1 = (bf16[8,512,128]{2,1,0:T(8,128)(2,1)}, bf16[1024,2048]{1,0:T(8,128)(2,1)}) custom-call(bf16[256,1024]{1,0:T(8,128)(2,1)} %get-tuple-element.21.lhs_ref, bf16[64,1024]{1,0:T(8,128)(2,1)} %interp_ref.1, f32[8,1024]{1,0:T(8,128)} %angle_ref.1), custom_call_target="tpu_custom_call" | custom-call | flops 1000000 | bytes 1000000 | tf_op jit(solution)/shard_map/to_boxes/pallas_call | solution.py:156
  25.1 3.6 %all-to-all-start = ((bf16[8,512,128]{2,1,0:T(8,128)(2,1)}), bf16[8,512,128]{2,1,0:T(8,128)(2,1)S(1)}, u32[]{:S(2)}, u32[]{:S(2)}) async-start(bf16[8,512,128]{2,1,0:T(8,128)(2,1)} %get-tuple-element.22), calls=%async_computation | async-start | bytes 2097152 | tf_op jit(solution)/shard_map/all_to_all | solution.py:445
  32.6 11.4 %collective-permute-done.lhs_ref = bf16[256,1024]{1,0:T(8,128)(2,1)S(1)} collective-permute-done((bf16[256,1024]{1,0:T(8,128)(2,1)}, bf16[256,1024]{1,0:T(8,128)(2,1)S(1)}, u32[]{:S(2)}, u32[]{:S(2)}) %collective-permute-start) | collective-permute-done | bytes 524320 | tf_op jit(solution)/shard_map/ppermute | solution.py:45
  44.0 2.2 %copy-done = bf16[1024,2048]{1,0:T(8,128)(2,1)S(1)} copy-done((bf16[1024,2048]{1,0:T(8,128)(2,1)S(1)}, bf16[1024,2048]{1,0:T(8,128)(2,1)}, u32[]{:S(2)}) %copy-start) | copy-done | bytes 4194328
  46.2 3.0 %to_boxes_again.1 = bf16[8,512,128]{2,1,0:T(8,128)(2,1)} custom-call(bf16[256,1024]{1,0:T(8,128)(2,1)S(1)} %collective-permute-done.lhs_ref, bf16[1024,2048]{1,0:T(8,128)(2,1)S(1)} %copy-done), custom_call_target="tpu_custom_call" | custom-call | flops 1000000 | bytes 6000000 | tf_op jit(solution)/shard_map/to_boxes_again/pallas_call | solution.py:182
  49.2 5.7 %all-to-all-done = bf16[8,512,128]{2,1,0:T(8,128)(2,1)S(1)} async-done(((bf16[8,512,128]{2,1,0:T(8,128)(2,1)}), bf16[8,512,128]{2,1,0:T(8,128)(2,1)S(1)}, u32[]{:S(2)}, u32[]{:S(2)}) %all-to-all-start) | async-done | bytes 1048608 | tf_op jit(solution)/shard_map/all_to_all | solution.py:445
  54.9 3.6 %all-to-all-start.1 = ((bf16[8,512,128]{2,1,0:T(8,128)(2,1)}), bf16[8,512,128]{2,1,0:T(8,128)(2,1)S(1)}, u32[]{:S(2)}, u32[]{:S(2)}) async-start(bf16[8,512,128]{2,1,0:T(8,128)(2,1)} %to_boxes_again.1), calls=%async_computation.1 | async-start | bytes 2097152 | tf_op jit(solution)/shard_map/all_to_all | solution.py:445
  58.6 14.9 %all-to-all-done.1 = bf16[8,512,128]{2,1,0:T(8,128)(2,1)S(1)} async-done(((bf16[8,512,128]{2,1,0:T(8,128)(2,1)}), bf16[8,512,128]{2,1,0:T(8,128)(2,1)S(1)}, u32[]{:S(2)}, u32[]{:S(2)}) %all-to-all-start.1) | async-done | bytes 1048608 | tf_op jit(solution)/shard_map/all_to_all | solution.py:445
  73.4 2.6 %collective-permute-done.6.four_ref = bf16[256,16,128]{2,1,0:T(8,128)(2,1)S(1)} collective-permute-done((bf16[256,16,128]{2,1,0:T(8,128)(2,1)S(1)}, bf16[256,16,128]{2,1,0:T(8,128)(2,1)S(1)}, u32[]{:S(2)}, u32[]{:S(2)}) %collective-permute-start.6) | collective-permute-done | bytes 1048608 | tf_op jit(solution)/shard_map/ppermute | solution.py:45
  76.1 8.5 %translate.3 = bf16[256,16,128]{2,1,0:T(8,128)(2,1)S(1)} custom-call(s32[6144]{0:T(1024)S(1)} %select_n.105.list_ref, f32[2,320,128]{2,1,0:T(8,128)S(1)} %pad.4.oper_ref, bf16[256,16,128]{2,1,0:T(8,128)(2,1)S(1)} %bitcast.25, bf16[256,16,128]{2,1,0:T(8,128)(2,1)S(1)} %collective-permute-done.5.two_ref, bf16[256,16,128]{2,1,0:T(8,128)(2,1)S(1)} %bitcast.28, ...), custom_call_target="tpu_custom_call" | custom-call | flops 1000000 | bytes 25000000 | tf_op jit(solution)/shard_map/translate/pallas_call | solution.py:250
  85.6 3.6 %all-to-all-start.3 = ((bf16[8,512,128]{2,1,0:T(8,128)(2,1)}), bf16[8,512,128]{2,1,0:T(8,128)(2,1)S(1)}, u32[]{:S(2)}, u32[]{:S(2)}) async-start(bf16[8,512,128]{2,1,0:T(8,128)(2,1)} %bitcast.30), calls=%async_computation.3 | async-start | bytes 2097152 | tf_op jit(solution)/shard_map/all_to_all | solution.py:445
  91.6 9.4 %translate.2 = bf16[256,16,128]{2,1,0:T(8,128)(2,1)} custom-call(s32[6144]{0:T(1024)S(1)} %select_n.103.list_ref, f32[2,320,128]{2,1,0:T(8,128)S(1)} %pad.4.oper_ref, bf16[256,16,128]{2,1,0:T(8,128)(2,1)S(1)} %bitcast.26, bf16[256,16,128]{2,1,0:T(8,128)(2,1)S(1)} %copy-done.6, bf16[256,16,128]{2,1,0:T(8,128)(2,1)S(1)} %bitcast.29, ...), custom_call_target="tpu_custom_call" | custom-call | flops 1000000 | bytes 25000000 | tf_op jit(solution)/shard_map/translate/pallas_call | solution.py:250
  101.0 4.1 %all-to-all-done.3.got_ref = bf16[8,512,128]{2,1,0:T(8,128)(2,1)S(1)} async-done(((bf16[8,512,128]{2,1,0:T(8,128)(2,1)}), bf16[8,512,128]{2,1,0:T(8,128)(2,1)S(1)}, u32[]{:S(2)}, u32[]{:S(2)}) %all-to-all-start.3) | async-done | bytes 1048608 | tf_op jit(solution)/shard_map/all_to_all | solution.py:445
  105.0 3.6 %all-to-all-start.2 = ((bf16[8,512,128]{2,1,0:T(8,128)(2,1)}), bf16[8,512,128]{2,1,0:T(8,128)(2,1)S(1)}, u32[]{:S(2)}, u32[]{:S(2)}) async-start(bf16[8,512,128]{2,1,0:T(8,128)(2,1)} %bitcast.7), calls=%async_computation.2 | async-start | bytes 2097152 | tf_op jit(solution)/shard_map/all_to_all | solution.py:445
  108.6 2.2 %copy-done.1 = bf16[1024,2048]{1,0:T(8,128)(2,1)S(1)} copy-done((bf16[1024,2048]{1,0:T(8,128)(2,1)S(1)}, bf16[1024,2048]{1,0:T(8,128)(2,1)}, u32[]{:S(2)}) %copy-start.1) | copy-done | bytes 4194328
  110.8 2.6 %from_boxes.3 = bf16[256,1024]{1,0:T(8,128)(2,1)S(1)} custom-call(bf16[8,512,128]{2,1,0:T(8,128)(2,1)S(1)} %all-to-all-done.3.got_ref, bf16[1024,2048]{1,0:T(8,128)(2,1)S(1)} %copy-done.1), custom_call_target="tpu_custom_call" | custom-call | flops 1000000 | bytes 1000000 | tf_op jit(solution)/shard_map/from_boxes/pallas_call | solution.py:379
  113.5 15.8 %near_part.1.near_ref = f32[2,8,8192]{2,1,0:T(8,128)} custom-call(s32[2048]{0:T(1024)} %reshape.37.idx_ref, bf16[2,8,8192]{2,1,0:T(8,128)(2,1)} %get-tuple-element.29.below_ref, bf16[2,8,8192]{2,1,0:T(8,128)(2,1)} %own_ref.1, bf16[2,8,8192]{2,1,0:T(8,128)(2,1)} %get-tuple-element.30.above_ref, bf16[2,8192,256]{2,1,0:T(8,128)(2,1)} %bitcast.31), custom_call_target="tpu_custom_call" | custom-call | flops 1000000 | bytes 1000000 | tf_op jit(solution)/shard_map/near_part/pallas_call | solution.py:334
  129.2 2.2 %copy-done.2 = bf16[1024,2048]{1,0:T(8,128)(2,1)S(1)} copy-done((bf16[1024,2048]{1,0:T(8,128)(2,1)S(1)}, bf16[1024,2048]{1,0:T(8,128)(2,1)}, u32[]{:S(2)}) %copy-start.2) | copy-done | bytes 4194328
  131.4 2.6 %from_boxes.2.own_ref = bf16[256,1024]{1,0:T(8,128)(2,1)S(1)} custom-call(bf16[8,512,128]{2,1,0:T(8,128)(2,1)S(1)} %all-to-all-done.2.got_ref, bf16[1024,2048]{1,0:T(8,128)(2,1)S(1)} %copy-done.2), custom_call_target="tpu_custom_call" | custom-call | flops 1000000 | bytes 1000000 | tf_op jit(solution)/shard_map/from_boxes/pallas_call | solution.py:379
  134.0 4.7 %collective-permute-done.7.other_ref = bf16[256,1024]{1,0:T(8,128)(2,1)S(1)} collective-permute-done((bf16[256,1024]{1,0:T(8,128)(2,1)S(1)}, bf16[256,1024]{1,0:T(8,128)(2,1)S(1)}, u32[]{:S(2)}, u32[]{:S(2)}) %collective-permute-start.7) | collective-permute-done | bytes 524320 | tf_op jit(solution)/shard_map/ppermute | solution.py:45
  138.8 3.1 %far_part.1 = f32[2,8,8192]{2,1,0:T(8,128)} custom-call(s32[1]{0:T(128)} %bitcast.hi_ref, bf16[256,1024]{1,0:T(8,128)(2,1)S(1)} %from_boxes.2.own_ref, bf16[256,1024]{1,0:T(8,128)(2,1)S(1)} %collective-permute-done.7.other_ref, bf16[2,8192,128]{2,1,0:T(8,128)(2,1)S(1)} %bitcast.23, f32[2,8,8192]{2,1,0:T(8,128)S(1)} %copy-done.9), custom_call_target="tpu_custom_call" | custom-call | flops 1000000 | bytes 1000000 | tf_op jit(solution)/shard_map/far_part/pallas_call | solution.py:429
  (55 shorter events, 9.9 us)
Async XLA Ops:
  0.0 28.7 %copy-start.11 = (s32[1024,12]{0,1:T(8,128)S(1)}, s32[1024,12]{0,1:T(8,128)}, u32[]{:S(2)}) copy-start(s32[1024,12]{0,1:T(8,128)} %param.18) | copy-start | bytes 147460
  0.0 28.9 %copy-start.10 = (s32[1024,12]{0,1:T(8,128)S(1)}, s32[1024,12]{0,1:T(8,128)}, u32[]{:S(2)}) copy-start(s32[1024,12]{0,1:T(8,128)} %param.19) | copy-start | bytes 147460
  0.0 31.7 %collective-permute-start.3 = (bf16[2,8,8192]{2,1,0:T(8,128)(2,1)}, bf16[2,8,8192]{2,1,0:T(8,128)(2,1)S(1)}, u32[]{:S(2)}, u32[]{:S(2)}) collective-permute-start(bf16[2,8,8192]{2,1,0:T(8,128)(2,1)} %own_ref.1), channel_id=1, source_target_pairs={{1,2},{3,4},{5,6},{7,8},{9,10},{11,12},{13,14},{15,16},{17,18},{19... | collective-permute-start | bytes 786440 | tf_op jit(solution)/shard_map/ppermute | solution.py:38
  0.8 30.9 %collective-permute-start.4 = (bf16[2,8,8192]{2,1,0:T(8,128)(2,1)}, bf16[2,8,8192]{2,1,0:T(8,128)(2,1)S(1)}, u32[]{:S(2)}, u32[]{:S(2)}) collective-permute-start(bf16[2,8,8192]{2,1,0:T(8,128)(2,1)} %own_ref.1), channel_id=1, source_target_pairs={{0,1},{1,0},{2,3},{3,2},{4,5},{5,4},{6,7},{7,6},{8,9},{9,8},{10,11... | collective-permute-start | bytes 786440 | tf_op jit(solution)/shard_map/ppermute | solution.py:45
  6.3 23.7 %collective-permute-start.1 = (bf16[2,64,316]{1,2,0:T(8,128)(2,1)S(1)}, bf16[2,64,316]{1,2,0:T(8,128)(2,1)S(1)}, u32[]{:S(2)}, u32[]{:S(2)}) collective-permute-start(bf16[2,64,316]{1,2,0:T(8,128)(2,1)S(1)} %bitcast.32), channel_id=1, source_target_pairs={{0,0},{1,1},{2,2},{3,3},{16,4},{17,5},{18,6},{19,7},{4,8},{5,9},{6... | collective-permute-start | bytes 242696 | tf_op jit(solution)/shard_map/ppermute | solution.py:480
  14.0 16.1 %copy-start.12 = (s32[256,8]{0,1:T(8,128)S(1)}, s32[256,8]{0,1:T(8,128)}, u32[]{:S(2)}) copy-start(s32[256,8]{0,1:T(8,128)} %param.12) | copy-start | bytes 24580
  14.0 16.1 %copy-start.13 = (s32[256]{0:T(256)S(1)}, s32[256]{0:T(256)}, u32[]{:S(2)}) copy-start(s32[256]{0:T(256)} %param.13) | copy-start | bytes 3076
  14.0 30.0 %collective-permute-start = (bf16[256,1024]{1,0:T(8,128)(2,1)}, bf16[256,1024]{1,0:T(8,128)(2,1)S(1)}, u32[]{:S(2)}, u32[]{:S(2)}) collective-permute-start(bf16[256,1024]{1,0:T(8,128)(2,1)} %get-tuple-element.18), channel_id=1, source_target_pairs={{0,4},{4,0},{1,5},{5,1},{2,6},{6,2},{3,7},{7,3},{8,12},{12,8},{9,1... | collective-permute-start | bytes 1572872 | tf_op jit(solution)/shard_map/ppermute | solution.py:45
  25.1 29.8 %all-to-all-start = ((bf16[8,512,128]{2,1,0:T(8,128)(2,1)}), bf16[8,512,128]{2,1,0:T(8,128)(2,1)S(1)}, u32[]{:S(2)}, u32[]{:S(2)}) async-start(bf16[8,512,128]{2,1,0:T(8,128)(2,1)} %get-tuple-element.22), calls=%async_computation | async-start | bytes 2097152 | tf_op jit(solution)/shard_map/all_to_all | solution.py:445
  30.0 1.5 %collective-permute-start.2 = (bf16[2,64,316]{1,2,0:T(8,128)(2,1)S(1)}, bf16[2,64,316]{1,2,0:T(8,128)(2,1)S(1)}, u32[]{:S(2)}, u32[]{:S(2)}) collective-permute-start(bf16[2,64,316]{1,2,0:T(8,128)(2,1)S(1)} %collective-permute-done.1), channel_id=1, source_target_pairs={{0,1},{1,0},{2,3},{3,2},{4,5},{5,4},{6,7},{7,6},{8,9},{9,8},{10,11... | collective-permute-start | bytes 242696 | tf_op jit(solution)/shard_map/ppermute | solution.py:45
  44.0 2.2 %copy-start = (bf16[1024,2048]{1,0:T(8,128)(2,1)S(1)}, bf16[1024,2048]{1,0:T(8,128)(2,1)}, u32[]{:S(2)}) copy-start(bf16[1024,2048]{1,0:T(8,128)(2,1)} %get-tuple-element.24.mat_ref) | copy-start | bytes 12582916
  54.9 18.5 %all-to-all-start.1 = ((bf16[8,512,128]{2,1,0:T(8,128)(2,1)}), bf16[8,512,128]{2,1,0:T(8,128)(2,1)S(1)}, u32[]{:S(2)}, u32[]{:S(2)}) async-start(bf16[8,512,128]{2,1,0:T(8,128)(2,1)} %to_boxes_again.1), calls=%async_computation.1 | async-start | bytes 2097152 | tf_op jit(solution)/shard_map/all_to_all | solution.py:445
  58.5 15.0 %collective-permute-start.5 = (bf16[256,16,128]{2,1,0:T(8,128)(2,1)S(1)}, bf16[256,16,128]{2,1,0:T(8,128)(2,1)S(1)}, u32[]{:S(2)}, u32[]{:S(2)}) collective-permute-start(bf16[256,16,128]{2,1,0:T(8,128)(2,1)S(1)} %bitcast.24), channel_id=1, source_target_pairs={{0,1},{1,0},{2,3},{3,2},{4,5},{5,4},{6,7},{7,6},{8,9},{9,8},{10,11... | collective-permute-start | bytes 3145736 | tf_op jit(solution)/shard_map/ppermute | solution.py:45
  73.4 2.7 %collective-permute-start.6 = (bf16[256,16,128]{2,1,0:T(8,128)(2,1)S(1)}, bf16[256,16,128]{2,1,0:T(8,128)(2,1)S(1)}, u32[]{:S(2)}, u32[]{:S(2)}) collective-permute-start(bf16[256,16,128]{2,1,0:T(8,128)(2,1)S(1)} %bitcast.27), channel_id=1, source_target_pairs={{0,1},{1,0},{2,3},{3,2},{4,5},{5,4},{6,7},{7,6},{8,9},{9,8},{10,11... | collective-permute-start | bytes 3145736 | tf_op jit(solution)/shard_map/ppermute | solution.py:45
  73.4 12.1 %copy-start.5 = (bf16[256,16,128]{2,1,0:T(8,128)(2,1)}, bf16[256,16,128]{2,1,0:T(8,128)(2,1)S(1)}, u32[]{:S(2)}) copy-start(bf16[256,16,128]{2,1,0:T(8,128)(2,1)S(1)} %collective-permute-done.5.two_ref) | copy-start | bytes 3145732
  76.1 8.5 %copy-start.7 = (bf16[256,16,128]{2,1,0:T(8,128)(2,1)}, bf16[256,16,128]{2,1,0:T(8,128)(2,1)S(1)}, u32[]{:S(2)}) copy-start(bf16[256,16,128]{2,1,0:T(8,128)(2,1)S(1)} %collective-permute-done.6.four_ref) | copy-start | bytes 3145732
  85.6 19.5 %all-to-all-start.3 = ((bf16[8,512,128]{2,1,0:T(8,128)(2,1)}), bf16[8,512,128]{2,1,0:T(8,128)(2,1)S(1)}, u32[]{:S(2)}, u32[]{:S(2)}) async-start(bf16[8,512,128]{2,1,0:T(8,128)(2,1)} %bitcast.30), calls=%async_computation.3 | async-start | bytes 2097152 | tf_op jit(solution)/shard_map/all_to_all | solution.py:445
  89.1 1.2 copy-start.6
  105.0 24.2 %all-to-all-start.2 = ((bf16[8,512,128]{2,1,0:T(8,128)(2,1)}), bf16[8,512,128]{2,1,0:T(8,128)(2,1)S(1)}, u32[]{:S(2)}, u32[]{:S(2)}) async-start(bf16[8,512,128]{2,1,0:T(8,128)(2,1)} %bitcast.7), calls=%async_computation.2 | async-start | bytes 2097152 | tf_op jit(solution)/shard_map/all_to_all | solution.py:445
  108.6 2.2 %copy-start.1 = (bf16[1024,2048]{1,0:T(8,128)(2,1)S(1)}, bf16[1024,2048]{1,0:T(8,128)(2,1)}, u32[]{:S(2)}) copy-start(bf16[1024,2048]{1,0:T(8,128)(2,1)} %get-tuple-element.24.mat_ref) | copy-start | bytes 12582916
  113.4 25.4 %collective-permute-start.7 = (bf16[256,1024]{1,0:T(8,128)(2,1)S(1)}, bf16[256,1024]{1,0:T(8,128)(2,1)S(1)}, u32[]{:S(2)}, u32[]{:S(2)}) collective-permute-start(bf16[256,1024]{1,0:T(8,128)(2,1)S(1)} %from_boxes.3), channel_id=1, source_target_pairs={{0,4},{4,0},{1,5},{5,1},{2,6},{6,2},{3,7},{7,3},{8,12},{12,8},{9,1... | collective-permute-start | bytes 1572872 | tf_op jit(solution)/shard_map/ppermute | solution.py:45
  129.2 2.2 %copy-start.2 = (bf16[1024,2048]{1,0:T(8,128)(2,1)S(1)}, bf16[1024,2048]{1,0:T(8,128)(2,1)}, u32[]{:S(2)}) copy-start(bf16[1024,2048]{1,0:T(8,128)(2,1)} %get-tuple-element.24.mat_ref) | copy-start | bytes 12582916
  131.4 7.4 %copy-start.3 = (bf16[2,256,32,128]{3,2,1,0:T(8,128)(2,1)S(1)}, bf16[2,256,32,128]{3,2,1,0:T(8,128)(2,1)}, u32[]{:S(2)}) copy-start(bf16[2,256,32,128]{3,2,1,0:T(8,128)(2,1)} %param.14) | copy-start | bytes 12582916
  131.4 7.4 %copy-start.9 = (f32[2,8,8192]{2,1,0:T(8,128)S(1)}, f32[2,8,8192]{2,1,0:T(8,128)}, u32[]{:S(2)}) copy-start(f32[2,8,8192]{2,1,0:T(8,128)} %near_part.1.near_ref) | copy-start | bytes 1572868
  (2 other events, 2.2 us)

commit v8 on v7

--- a/solution.py
+++ b/solution.py
@@ -96,7 +96,7 @@
 def leaves(hi, currents, radiation):
     width = currents.shape[2]
     rows = width // WIDE * R
-    steps = 8
+    steps = 2
     per_step = width // steps
     shape = jax.ShapeDtypeStruct((rows, DEPTH), BF16)
     spec = pl.BlockSpec((rows // steps, DEPTH), lambda s, *_: (s, 0))
@@ -151,7 +151,7 @@
 
 def to_boxes(lhs, interp, angle):
     rows = lhs.shape[0]
-    steps = 4
+    steps = 2
     chips = CHIPS // steps
     return pl.pallas_call(
         up_kernel,
@@ -177,7 +177,7 @@
 
 def to_boxes_again(lhs, matrix):
     rows = lhs.shape[0]
-    steps = 4
+    steps = 2
     chips = CHIPS // steps
     return pl.pallas_call(
         again_kernel,
@@ -244,7 +244,7 @@
 def translate(lists, operators, parts):
     targets = lists.shape[0] // (2 * IL)
     boxes = parts[0].shape[0]
-    steps = 2
+    steps = 1
     per_step = targets // steps
     anywhere = pl.BlockSpec(memory_space=pl.ANY)
     return pl.pallas_call(
@@ -328,7 +328,7 @@
 
 def near_part(index, below, own, above, blocks):
     width = own.shape[2]
-    steps = 8
+    steps = 4
     per_step = width // steps
     whole = pl.BlockSpec((2, R, width), lambda s, *_: (0, 0, 0))
     return pl.pallas_call(
@@ -374,7 +374,7 @@
 
 def from_boxes(received, matrix):
     rows = received.shape[1] // 2
-    steps = 4
+    steps = 2
     chips = CHIPS // steps
     return pl.pallas_call(
         down_kernel,
@@ -422,7 +422,7 @@
 def far_part(hi, own, other, radiation, near_field):
     width = near_field.shape[2]
     rows = own.shape[0]
-    steps = 4
+    steps = 2
     per_step = width // steps
     field = pl.BlockSpec((rows // steps, DEPTH), lambda s, *_: (s, 0))
     wave = pl.BlockSpec((2, R, per_step), lambda s, *_: (0, 0, s))

time: 143 us -> 140 us (0.979)
  Pallas kernels: 56.5 us -> 49.5 us
  waiting for transfers between devices: 43.7 us -> 47.1 us
    ppermute x6, waiting for transfers between devices: 19.1 us -> 23.3 us  [across(): return lax.ppermute(array, axis, [(0, 1), (1, 0)])]
    pallas_call x1, Pallas kernels: 7.01 us -> 3.67 us  [leaves(): pl.pallas_call(leaf_kernel, grid_spec=pltpu.PrefetchScalarGridSpec(num_sc...]
  transfers between devices with their start and end apart: 12 -> 12, of which waited for: 7 -> 8; matrix products, arithmetic and copies ran while one was open for 3% -> 3% of each run, Pallas kernels for 32% -> 28%
where the time goes in v8:
time: 140 us; the launch traced here: 139 us
  Pallas kernels  49.5 us (35%)
  waiting for transfers between devices  47.1 us (34%)
  starting transfers between devices  28 us (20%)
  local copies, waits for them, and re-layouts  13.1 us (9%)
    all_to_all x4, waiting for transfers between devices, swapped(): lax.all_to_all(array, INSIDE, split_axis=0, concat_axis=0, tiled=True)  23.8 us
    ppermute x6, waiting for transfers between devices, across(): return lax.ppermute(array, axis, [(0, 1), (1, 0)])  23.3 us
    pallas_call x2, Pallas kernels, translate(): pl.pallas_call(functools.partial(translate_kernel, group=8), grid_spec=pl...  17.8 us
    all_to_all x4, starting transfers between devices, swapped(): lax.all_to_all(array, INSIDE, split_axis=0, concat_axis=0, tiled=True)  15.5 us
    pallas_call x1, Pallas kernels, near_part(): pl.pallas_call(near_kernel, grid_spec=pltpu.PrefetchScalarGridSpec(num_sc...  14.7 us
    unnamed x31, local copies, waits for them, and re-layouts  11.4 us
    ppermute x6, starting transfers between devices, across(): return lax.ppermute(array, axis, [(0, 1), (1, 0)])  11.1 us
    pallas_call x1, Pallas kernels, to_boxes(): pl.pallas_call(up_kernel, grid=(steps,), in_specs=[pl.BlockSpec((rows, DE...  4.19 us
  transfers between devices with their start and end apart: 12, of which 8 were waited for; matrix products, arithmetic and copies ran while one was open for 3% of the time, Pallas kernels for 28%

profile of v8, /device:TPU:0, one launch (start us, length us, event | category | flops | bytes accessed | tf_op | source)
XLA Modules:
  0.0 139.4 jit_solution(9647608520625760809)
XLA Ops:
  0.8 4.4 %collective-permute-start.4 = (bf16[2,8,8192]{2,1,0:T(8,128)(2,1)}, bf16[2,8,8192]{2,1,0:T(8,128)(2,1)S(1)}, u32[]{:S(2)}, u32[]{:S(2)}) collective-permute-start(bf16[2,8,8192]{2,1,0:T(8,128)(2,1)} %own_ref.1), channel_id=1, source_target_pairs={{0,1},{1,0},{2,3},{3,2},{4,5},{5,4},{6,7},{7,6},{8,9},{9,8},{10,11... | collective-permute-start | bytes 786440 | tf_op jit(solution)/shard_map/ppermute | solution.py:45
  7.0 3.7 %leaves.1 = (bf16[256,1024]{1,0:T(8,128)(2,1)}, bf16[256,1024]{1,0:T(8,128)(2,1)}) custom-call(s32[1]{0:T(128)} %bitcast.hi_ref, bf16[2,8,8192]{2,1,0:T(8,128)(2,1)} %own_ref.1, bf16[2,8192,128]{2,1,0:T(8,128)(2,1)} %bitcast.22), custom_call_target="tpu_custom_call" | custom-call | flops 1000000 | bytes 1000000 | tf_op jit(solution)/shard_map/leaves/pallas_call | solution.py:103
  10.7 6.5 %collective-permute-start = (bf16[256,1024]{1,0:T(8,128)(2,1)}, bf16[256,1024]{1,0:T(8,128)(2,1)S(1)}, u32[]{:S(2)}, u32[]{:S(2)}) collective-permute-start(bf16[256,1024]{1,0:T(8,128)(2,1)} %get-tuple-element.18), channel_id=1, source_target_pairs={{0,4},{4,0},{1,5},{5,1},{2,6},{6,2},{3,7},{7,3},{8,12},{12,8},{9,1... | collective-permute-start | bytes 1572872 | tf_op jit(solution)/shard_map/ppermute | solution.py:45
  17.1 4.2 %to_boxes.1 = (bf16[8,512,128]{2,1,0:T(8,128)(2,1)}, bf16[1024,2048]{1,0:T(8,128)(2,1)}) custom-call(bf16[256,1024]{1,0:T(8,128)(2,1)} %get-tuple-element.21.lhs_ref, bf16[64,1024]{1,0:T(8,128)(2,1)} %interp_ref.1, f32[8,1024]{1,0:T(8,128)} %angle_ref.1), custom_call_target="tpu_custom_call" | custom-call | flops 1000000 | bytes 1000000 | tf_op jit(solution)/shard_map/to_boxes/pallas_call | solution.py:156
  21.3 3.6 %all-to-all-start = ((bf16[8,512,128]{2,1,0:T(8,128)(2,1)}), bf16[8,512,128]{2,1,0:T(8,128)(2,1)S(1)}, u32[]{:S(2)}, u32[]{:S(2)}) async-start(bf16[8,512,128]{2,1,0:T(8,128)(2,1)} %get-tuple-element.22), calls=%async_computation | async-start | bytes 2097152 | tf_op jit(solution)/shard_map/all_to_all | solution.py:445
  28.9 15.2 %collective-permute-done.lhs_ref = bf16[256,1024]{1,0:T(8,128)(2,1)S(1)} collective-permute-done((bf16[256,1024]{1,0:T(8,128)(2,1)}, bf16[256,1024]{1,0:T(8,128)(2,1)S(1)}, u32[]{:S(2)}, u32[]{:S(2)}) %collective-permute-start) | collective-permute-done | bytes 524320 | tf_op jit(solution)/shard_map/ppermute | solution.py:45
  44.0 2.2 %copy-done = bf16[1024,2048]{1,0:T(8,128)(2,1)S(1)} copy-done((bf16[1024,2048]{1,0:T(8,128)(2,1)S(1)}, bf16[1024,2048]{1,0:T(8,128)(2,1)}, u32[]{:S(2)}) %copy-start) | copy-done | bytes 4194328
  46.2 2.5 %to_boxes_again.1 = bf16[8,512,128]{2,1,0:T(8,128)(2,1)} custom-call(bf16[256,1024]{1,0:T(8,128)(2,1)S(1)} %collective-permute-done.lhs_ref, bf16[1024,2048]{1,0:T(8,128)(2,1)S(1)} %copy-done), custom_call_target="tpu_custom_call" | custom-call | flops 1000000 | bytes 6000000 | tf_op jit(solution)/shard_map/to_boxes_again/pallas_call | solution.py:182
  48.7 3.6 %all-to-all-done = bf16[8,512,128]{2,1,0:T(8,128)(2,1)S(1)} async-done(((bf16[8,512,128]{2,1,0:T(8,128)(2,1)}), bf16[8,512,128]{2,1,0:T(8,128)(2,1)S(1)}, u32[]{:S(2)}, u32[]{:S(2)}) %all-to-all-start) | async-done | bytes 1048608 | tf_op jit(solution)/shard_map/all_to_all | solution.py:445
  52.4 4.8 %all-to-all-start.1 = ((bf16[8,512,128]{2,1,0:T(8,128)(2,1)}), bf16[8,512,128]{2,1,0:T(8,128)(2,1)S(1)}, u32[]{:S(2)}, u32[]{:S(2)}) async-start(bf16[8,512,128]{2,1,0:T(8,128)(2,1)} %to_boxes_again.1), calls=%async_computation.1 | async-start | bytes 2097152 | tf_op jit(solution)/shard_map/all_to_all | solution.py:445
  57.2 14.9 %all-to-all-done.1 = bf16[8,512,128]{2,1,0:T(8,128)(2,1)S(1)} async-done(((bf16[8,512,128]{2,1,0:T(8,128)(2,1)}), bf16[8,512,128]{2,1,0:T(8,128)(2,1)S(1)}, u32[]{:S(2)}, u32[]{:S(2)}) %all-to-all-start.1) | async-done | bytes 1048608 | tf_op jit(solution)/shard_map/all_to_all | solution.py:445
  72.1 2.6 %collective-permute-done.6.four_ref = bf16[256,16,128]{2,1,0:T(8,128)(2,1)S(1)} collective-permute-done((bf16[256,16,128]{2,1,0:T(8,128)(2,1)S(1)}, bf16[256,16,128]{2,1,0:T(8,128)(2,1)S(1)}, u32[]{:S(2)}, u32[]{:S(2)}) %collective-permute-start.6) | collective-permute-done | bytes 1048608 | tf_op jit(solution)/shard_map/ppermute | solution.py:45
  74.7 8.4 %translate.3 = bf16[256,16,128]{2,1,0:T(8,128)(2,1)S(1)} custom-call(s32[6144]{0:T(1024)S(1)} %select_n.105.list_ref, f32[2,320,128]{2,1,0:T(8,128)S(1)} %pad.4.oper_ref, bf16[256,16,128]{2,1,0:T(8,128)(2,1)S(1)} %bitcast.25, bf16[256,16,128]{2,1,0:T(8,128)(2,1)S(1)} %collective-permute-done.5.two_ref, bf16[256,16,128]{2,1,0:T(8,128)(2,1)S(1)} %bitcast.28, ...), custom_call_target="tpu_custom_call" | custom-call | flops 1000000 | bytes 25000000 | tf_op jit(solution)/shard_map/translate/pallas_call | solution.py:250
  84.1 3.6 %all-to-all-start.3 = ((bf16[8,512,128]{2,1,0:T(8,128)(2,1)}), bf16[8,512,128]{2,1,0:T(8,128)(2,1)S(1)}, u32[]{:S(2)}, u32[]{:S(2)}) async-start(bf16[8,512,128]{2,1,0:T(8,128)(2,1)} %bitcast.30), calls=%async_computation.3 | async-start | bytes 2097152 | tf_op jit(solution)/shard_map/all_to_all | solution.py:445
  90.1 9.4 %translate.2 = bf16[256,16,128]{2,1,0:T(8,128)(2,1)} custom-call(s32[6144]{0:T(1024)S(1)} %select_n.103.list_ref, f32[2,320,128]{2,1,0:T(8,128)S(1)} %pad.4.oper_ref, bf16[256,16,128]{2,1,0:T(8,128)(2,1)S(1)} %bitcast.26, bf16[256,16,128]{2,1,0:T(8,128)(2,1)S(1)} %copy-done.6, bf16[256,16,128]{2,1,0:T(8,128)(2,1)S(1)} %bitcast.29, ...), custom_call_target="tpu_custom_call" | custom-call | flops 1000000 | bytes 25000000 | tf_op jit(solution)/shard_map/translate/pallas_call | solution.py:250
  99.6 4.0 %all-to-all-done.3.got_ref = bf16[8,512,128]{2,1,0:T(8,128)(2,1)S(1)} async-done(((bf16[8,512,128]{2,1,0:T(8,128)(2,1)}), bf16[8,512,128]{2,1,0:T(8,128)(2,1)S(1)}, u32[]{:S(2)}, u32[]{:S(2)}) %all-to-all-start.3) | async-done | bytes 1048608 | tf_op jit(solution)/shard_map/all_to_all | solution.py:445
  103.6 3.6 %all-to-all-start.2 = ((bf16[8,512,128]{2,1,0:T(8,128)(2,1)}), bf16[8,512,128]{2,1,0:T(8,128)(2,1)S(1)}, u32[]{:S(2)}, u32[]{:S(2)}) async-start(bf16[8,512,128]{2,1,0:T(8,128)(2,1)} %bitcast.7), calls=%async_computation.2 | async-start | bytes 2097152 | tf_op jit(solution)/shard_map/all_to_all | solution.py:445
  107.2 2.2 %copy-done.1 = bf16[1024,2048]{1,0:T(8,128)(2,1)S(1)} copy-done((bf16[1024,2048]{1,0:T(8,128)(2,1)S(1)}, bf16[1024,2048]{1,0:T(8,128)(2,1)}, u32[]{:S(2)}) %copy-start.1) | copy-done | bytes 4194328
  109.4 1.9 %from_boxes.3 = bf16[256,1024]{1,0:T(8,128)(2,1)S(1)} custom-call(bf16[8,512,128]{2,1,0:T(8,128)(2,1)S(1)} %all-to-all-done.3.got_ref, bf16[1024,2048]{1,0:T(8,128)(2,1)S(1)} %copy-done.1), custom_call_target="tpu_custom_call" | custom-call | flops 1000000 | bytes 1000000 | tf_op jit(solution)/shard_map/from_boxes/pallas_call | solution.py:379
  111.4 14.7 %near_part.1.near_ref = f32[2,8,8192]{2,1,0:T(8,128)} custom-call(s32[2048]{0:T(1024)} %reshape.37.idx_ref, bf16[2,8,8192]{2,1,0:T(8,128)(2,1)} %get-tuple-element.29.below_ref, bf16[2,8,8192]{2,1,0:T(8,128)(2,1)} %own_ref.1, bf16[2,8,8192]{2,1,0:T(8,128)(2,1)} %get-tuple-element.30.above_ref, bf16[2,8192,256]{2,1,0:T(8,128)(2,1)} %bitcast.31), custom_call_target="tpu_custom_call" | custom-call | flops 1000000 | bytes 1000000 | tf_op jit(solution)/shard_map/near_part/pallas_call | solution.py:334
  127.3 2.2 %copy-done.2 = bf16[1024,2048]{1,0:T(8,128)(2,1)S(1)} copy-done((bf16[1024,2048]{1,0:T(8,128)(2,1)S(1)}, bf16[1024,2048]{1,0:T(8,128)(2,1)}, u32[]{:S(2)}) %copy-start.2) | copy-done | bytes 4194328
  129.5 1.9 %from_boxes.2.own_ref = bf16[256,1024]{1,0:T(8,128)(2,1)S(1)} custom-call(bf16[8,512,128]{2,1,0:T(8,128)(2,1)S(1)} %all-to-all-done.2.got_ref, bf16[1024,2048]{1,0:T(8,128)(2,1)S(1)} %copy-done.2), custom_call_target="tpu_custom_call" | custom-call | flops 1000000 | bytes 1000000 | tf_op jit(solution)/shard_map/from_boxes/pallas_call | solution.py:379
  131.5 5.2 %collective-permute-done.7.other_ref = bf16[256,1024]{1,0:T(8,128)(2,1)S(1)} collective-permute-done((bf16[256,1024]{1,0:T(8,128)(2,1)S(1)}, bf16[256,1024]{1,0:T(8,128)(2,1)S(1)}, u32[]{:S(2)}, u32[]{:S(2)}) %collective-permute-start.7) | collective-permute-done | bytes 524320 | tf_op jit(solution)/shard_map/ppermute | solution.py:45
  136.7 2.7 %far_part.1 = f32[2,8,8192]{2,1,0:T(8,128)} custom-call(s32[1]{0:T(128)} %bitcast.hi_ref, bf16[256,1024]{1,0:T(8,128)(2,1)S(1)} %from_boxes.2.own_ref, bf16[256,1024]{1,0:T(8,128)(2,1)S(1)} %collective-permute-done.7.other_ref, bf16[2,8192,128]{2,1,0:T(8,128)(2,1)S(1)} %bitcast.23, f32[2,8,8192]{2,1,0:T(8,128)S(1)} %copy-done.9), custom_call_target="tpu_custom_call" | custom-call | flops 1000000 | bytes 1000000 | tf_op jit(solution)/shard_map/far_part/pallas_call | solution.py:429
  (55 shorter events, 11.1 us)
Async XLA Ops:
  0.0 24.9 %copy-start.11 = (s32[1024,12]{0,1:T(8,128)S(1)}, s32[1024,12]{0,1:T(8,128)}, u32[]{:S(2)}) copy-start(s32[1024,12]{0,1:T(8,128)} %param.18) | copy-start | bytes 147460
  0.0 25.2 %copy-start.10 = (s32[1024,12]{0,1:T(8,128)S(1)}, s32[1024,12]{0,1:T(8,128)}, u32[]{:S(2)}) copy-start(s32[1024,12]{0,1:T(8,128)} %param.19) | copy-start | bytes 147460
  0.0 28.0 %collective-permute-start.3 = (bf16[2,8,8192]{2,1,0:T(8,128)(2,1)}, bf16[2,8,8192]{2,1,0:T(8,128)(2,1)S(1)}, u32[]{:S(2)}, u32[]{:S(2)}) collective-permute-start(bf16[2,8,8192]{2,1,0:T(8,128)(2,1)} %own_ref.1), channel_id=1, source_target_pairs={{1,2},{3,4},{5,6},{7,8},{9,10},{11,12},{13,14},{15,16},{17,18},{19... | collective-permute-start | bytes 786440 | tf_op jit(solution)/shard_map/ppermute | solution.py:38
  0.8 27.2 %collective-permute-start.4 = (bf16[2,8,8192]{2,1,0:T(8,128)(2,1)}, bf16[2,8,8192]{2,1,0:T(8,128)(2,1)S(1)}, u32[]{:S(2)}, u32[]{:S(2)}) collective-permute-start(bf16[2,8,8192]{2,1,0:T(8,128)(2,1)} %own_ref.1), channel_id=1, source_target_pairs={{0,1},{1,0},{2,3},{3,2},{4,5},{5,4},{6,7},{7,6},{8,9},{9,8},{10,11... | collective-permute-start | bytes 786440 | tf_op jit(solution)/shard_map/ppermute | solution.py:45
  6.3 19.9 %collective-permute-start.1 = (bf16[2,64,316]{1,2,0:T(8,128)(2,1)S(1)}, bf16[2,64,316]{1,2,0:T(8,128)(2,1)S(1)}, u32[]{:S(2)}, u32[]{:S(2)}) collective-permute-start(bf16[2,64,316]{1,2,0:T(8,128)(2,1)S(1)} %bitcast.32), channel_id=1, source_target_pairs={{0,0},{1,1},{2,2},{3,3},{16,4},{17,5},{18,6},{19,7},{4,8},{5,9},{6... | collective-permute-start | bytes 242696 | tf_op jit(solution)/shard_map/ppermute | solution.py:480
  10.7 15.7 %copy-start.12 = (s32[256,8]{0,1:T(8,128)S(1)}, s32[256,8]{0,1:T(8,128)}, u32[]{:S(2)}) copy-start(s32[256,8]{0,1:T(8,128)} %param.12) | copy-start | bytes 24580
  10.7 15.7 %copy-start.13 = (s32[256]{0:T(256)S(1)}, s32[256]{0:T(256)}, u32[]{:S(2)}) copy-start(s32[256]{0:T(256)} %param.13) | copy-start | bytes 3076
  10.7 33.4 %collective-permute-start = (bf16[256,1024]{1,0:T(8,128)(2,1)}, bf16[256,1024]{1,0:T(8,128)(2,1)S(1)}, u32[]{:S(2)}, u32[]{:S(2)}) collective-permute-start(bf16[256,1024]{1,0:T(8,128)(2,1)} %get-tuple-element.18), channel_id=1, source_target_pairs={{0,4},{4,0},{1,5},{5,1},{2,6},{6,2},{3,7},{7,3},{8,12},{12,8},{9,1... | collective-permute-start | bytes 1572872 | tf_op jit(solution)/shard_map/ppermute | solution.py:45
  21.3 31.0 %all-to-all-start = ((bf16[8,512,128]{2,1,0:T(8,128)(2,1)}), bf16[8,512,128]{2,1,0:T(8,128)(2,1)S(1)}, u32[]{:S(2)}, u32[]{:S(2)}) async-start(bf16[8,512,128]{2,1,0:T(8,128)(2,1)} %get-tuple-element.22), calls=%async_computation | async-start | bytes 2097152 | tf_op jit(solution)/shard_map/all_to_all | solution.py:445
  26.3 1.5 %collective-permute-start.2 = (bf16[2,64,316]{1,2,0:T(8,128)(2,1)S(1)}, bf16[2,64,316]{1,2,0:T(8,128)(2,1)S(1)}, u32[]{:S(2)}, u32[]{:S(2)}) collective-permute-start(bf16[2,64,316]{1,2,0:T(8,128)(2,1)S(1)} %collective-permute-done.1), channel_id=1, source_target_pairs={{0,1},{1,0},{2,3},{3,2},{4,5},{5,4},{6,7},{7,6},{8,9},{9,8},{10,11... | collective-permute-start | bytes 242696 | tf_op jit(solution)/shard_map/ppermute | solution.py:45
  44.0 2.2 %copy-start = (bf16[1024,2048]{1,0:T(8,128)(2,1)S(1)}, bf16[1024,2048]{1,0:T(8,128)(2,1)}, u32[]{:S(2)}) copy-start(bf16[1024,2048]{1,0:T(8,128)(2,1)} %get-tuple-element.24.mat_ref) | copy-start | bytes 12582916
  52.4 19.7 %all-to-all-start.1 = ((bf16[8,512,128]{2,1,0:T(8,128)(2,1)}), bf16[8,512,128]{2,1,0:T(8,128)(2,1)S(1)}, u32[]{:S(2)}, u32[]{:S(2)}) async-start(bf16[8,512,128]{2,1,0:T(8,128)(2,1)} %to_boxes_again.1), calls=%async_computation.1 | async-start | bytes 2097152 | tf_op jit(solution)/shard_map/all_to_all | solution.py:445
  57.2 14.9 %collective-permute-start.5 = (bf16[256,16,128]{2,1,0:T(8,128)(2,1)S(1)}, bf16[256,16,128]{2,1,0:T(8,128)(2,1)S(1)}, u32[]{:S(2)}, u32[]{:S(2)}) collective-permute-start(bf16[256,16,128]{2,1,0:T(8,128)(2,1)S(1)} %bitcast.24), channel_id=1, source_target_pairs={{0,1},{1,0},{2,3},{3,2},{4,5},{5,4},{6,7},{7,6},{8,9},{9,8},{10,11... | collective-permute-start | bytes 3145736 | tf_op jit(solution)/shard_map/ppermute | solution.py:45
  72.1 2.7 %collective-permute-start.6 = (bf16[256,16,128]{2,1,0:T(8,128)(2,1)S(1)}, bf16[256,16,128]{2,1,0:T(8,128)(2,1)S(1)}, u32[]{:S(2)}, u32[]{:S(2)}) collective-permute-start(bf16[256,16,128]{2,1,0:T(8,128)(2,1)S(1)} %bitcast.27), channel_id=1, source_target_pairs={{0,1},{1,0},{2,3},{3,2},{4,5},{5,4},{6,7},{7,6},{8,9},{9,8},{10,11... | collective-permute-start | bytes 3145736 | tf_op jit(solution)/shard_map/ppermute | solution.py:45
  72.1 12.1 %copy-start.5 = (bf16[256,16,128]{2,1,0:T(8,128)(2,1)}, bf16[256,16,128]{2,1,0:T(8,128)(2,1)S(1)}, u32[]{:S(2)}) copy-start(bf16[256,16,128]{2,1,0:T(8,128)(2,1)S(1)} %collective-permute-done.5.two_ref) | copy-start | bytes 3145732
  74.7 8.4 %copy-start.7 = (bf16[256,16,128]{2,1,0:T(8,128)(2,1)}, bf16[256,16,128]{2,1,0:T(8,128)(2,1)S(1)}, u32[]{:S(2)}) copy-start(bf16[256,16,128]{2,1,0:T(8,128)(2,1)S(1)} %collective-permute-done.6.four_ref) | copy-start | bytes 3145732
  84.1 19.5 %all-to-all-start.3 = ((bf16[8,512,128]{2,1,0:T(8,128)(2,1)}), bf16[8,512,128]{2,1,0:T(8,128)(2,1)S(1)}, u32[]{:S(2)}, u32[]{:S(2)}) async-start(bf16[8,512,128]{2,1,0:T(8,128)(2,1)} %bitcast.30), calls=%async_computation.3 | async-start | bytes 2097152 | tf_op jit(solution)/shard_map/all_to_all | solution.py:445
  87.7 1.2 copy-start.6
  103.6 23.7 %all-to-all-start.2 = ((bf16[8,512,128]{2,1,0:T(8,128)(2,1)}), bf16[8,512,128]{2,1,0:T(8,128)(2,1)S(1)}, u32[]{:S(2)}, u32[]{:S(2)}) async-start(bf16[8,512,128]{2,1,0:T(8,128)(2,1)} %bitcast.7), calls=%async_computation.2 | async-start | bytes 2097152 | tf_op jit(solution)/shard_map/all_to_all | solution.py:445
  107.2 2.2 %copy-start.1 = (bf16[1024,2048]{1,0:T(8,128)(2,1)S(1)}, bf16[1024,2048]{1,0:T(8,128)(2,1)}, u32[]{:S(2)}) copy-start(bf16[1024,2048]{1,0:T(8,128)(2,1)} %get-tuple-element.24.mat_ref) | copy-start | bytes 12582916
  111.3 25.4 %collective-permute-start.7 = (bf16[256,1024]{1,0:T(8,128)(2,1)S(1)}, bf16[256,1024]{1,0:T(8,128)(2,1)S(1)}, u32[]{:S(2)}, u32[]{:S(2)}) collective-permute-start(bf16[256,1024]{1,0:T(8,128)(2,1)S(1)} %from_boxes.3), channel_id=1, source_target_pairs={{0,4},{4,0},{1,5},{5,1},{2,6},{6,2},{3,7},{7,3},{8,12},{12,8},{9,1... | collective-permute-start | bytes 1572872 | tf_op jit(solution)/shard_map/ppermute | solution.py:45
  127.3 2.2 %copy-start.2 = (bf16[1024,2048]{1,0:T(8,128)(2,1)S(1)}, bf16[1024,2048]{1,0:T(8,128)(2,1)}, u32[]{:S(2)}) copy-start(bf16[1024,2048]{1,0:T(8,128)(2,1)} %get-tuple-element.24.mat_ref) | copy-start | bytes 12582916
  129.5 7.2 %copy-start.3 = (bf16[2,256,32,128]{3,2,1,0:T(8,128)(2,1)S(1)}, bf16[2,256,32,128]{3,2,1,0:T(8,128)(2,1)}, u32[]{:S(2)}) copy-start(bf16[2,256,32,128]{3,2,1,0:T(8,128)(2,1)} %param.14) | copy-start | bytes 12582916
  129.5 7.2 %copy-start.9 = (f32[2,8,8192]{2,1,0:T(8,128)S(1)}, f32[2,8,8192]{2,1,0:T(8,128)}, u32[]{:S(2)}) copy-start(f32[2,8,8192]{2,1,0:T(8,128)} %near_part.1.near_ref) | copy-start | bytes 1572868
  (2 other events, 2.2 us)

commit v9 on v8

--- a/solution.py
+++ b/solution.py
@@ -177,7 +177,7 @@
 
 def to_boxes_again(lhs, matrix):
     rows = lhs.shape[0]
-    steps = 2
+    steps = 1
     chips = CHIPS // steps
     return pl.pallas_call(
         again_kernel,
@@ -248,7 +248,7 @@
     per_step = targets // steps
     anywhere = pl.BlockSpec(memory_space=pl.ANY)
     return pl.pallas_call(
-        functools.partial(translate_kernel, group=8),
+        functools.partial(translate_kernel, group=16),
         grid_spec=pltpu.PrefetchScalarGridSpec(
             num_scalar_prefetch=1,
             grid=(steps,),
@@ -328,7 +328,7 @@
 
 def near_part(index, below, own, above, blocks):
     width = own.shape[2]
-    steps = 4
+    steps = 2
     per_step = width // steps
     whole = pl.BlockSpec((2, R, width), lambda s, *_: (0, 0, 0))
     return pl.pallas_call(
@@ -350,31 +350,18 @@
     )(index, below, own, above, blocks)
 
 
-def down_kernel(got_ref, mat_ref, out_ref, sum_ref):
-    step = pl.program_id(0)
-    last = pl.num_programs(0) - 1
+def down_kernel(got_ref, mat_ref, out_ref):
     pieces = []
     for chip in range(got_ref.shape[0]):
         both = got_ref[chip].astype(F32).reshape(-1, 2, R, LANES)
         pieces += [both[:, 0].reshape(-1, LANES), both[:, 1].reshape(-1, LANES)]
-    added = times_transposed(jnp.concatenate(pieces, axis=1).astype(BF16), mat_ref[...])
-
-    @pl.when(step == 0)
-    def begin():
-        sum_ref[...] = added
-
-    @pl.when(jnp.logical_and(step > 0, step < last))
-    def go_on():
-        sum_ref[...] += added
-
-    @pl.when(step == last)
-    def end():
-        out_ref[...] = (sum_ref[...] + added).astype(BF16)
+    fields = jnp.concatenate(pieces, axis=1).astype(BF16)
+    out_ref[...] = times_transposed(fields, mat_ref[...]).astype(BF16)
 
 
 def from_boxes(received, matrix):
     rows = received.shape[1] // 2
-    steps = 2
+    steps = 1
     chips = CHIPS // steps
     return pl.pallas_call(
         down_kernel,
@@ -385,7 +372,6 @@
         ],
         out_specs=pl.BlockSpec((rows, DEPTH), lambda s: (0, 0)),
         out_shape=jax.ShapeDtypeStruct((rows, DEPTH), BF16),
-        scratch_shapes=[pltpu.VMEM((rows, DEPTH), F32)],
         compiler_params=LESS,
         cost_estimate=cost(1),
         name="from_boxes",

time: 140 us -> 139 us (level)
  Pallas kernels: 49.5 us -> 47.8 us
    all_to_all x4, waiting for transfers between devices: 23.8 us -> 25.3 us  [swapped(): lax.all_to_all(array, INSIDE, split_axis=0, concat_axis=0, tiled=True)]
  transfers between devices with their start and end apart: 12 -> 12, of which waited for: 8 -> 8; matrix products, arithmetic and copies ran while one was open for 3% -> 3% of each run, Pallas kernels for 28% -> 27%
where the time goes in v9:
time: 139 us
  waiting for transfers between devices  48 us (35%)
  Pallas kernels  47.8 us (34%)
  starting transfers between devices  28 us (20%)
  local copies, waits for them, and re-layouts  13.1 us (9%)
    all_to_all x4, waiting for transfers between devices, swapped(): lax.all_to_all(array, INSIDE, split_axis=0, concat_axis=0, tiled=True)  25.3 us
    ppermute x6, waiting for transfers between devices, across(): return lax.ppermute(array, axis, [(0, 1), (1, 0)])  22.7 us
    pallas_call x2, Pallas kernels, translate(): pl.pallas_call(functools.partial(translate_kernel, group=16), grid_spec=p...  17.5 us
    all_to_all x4, starting transfers between devices, swapped(): lax.all_to_all(array, INSIDE, split_axis=0, concat_axis=0, tiled=True)  15.5 us
    pallas_call x1, Pallas kernels, near_part(): pl.pallas_call(near_kernel, grid_spec=pltpu.PrefetchScalarGridSpec(num_sc...  15 us
    unnamed x31, local copies, waits for them, and re-layouts  11.4 us
    ppermute x6, starting transfers between devices, across(): return lax.ppermute(array, axis, [(0, 1), (1, 0)])  11.1 us
    pallas_call x1, Pallas kernels, to_boxes(): pl.pallas_call(up_kernel, grid=(steps,), in_specs=[pl.BlockSpec((rows, DE...  4.19 us
  transfers between devices with their start and end apart: 12, of which 8 were waited for; matrix products, arithmetic and copies ran while one was open for 3% of the time, Pallas kernels for 27%

profile of v9, /device:TPU:0, one launch (start us, length us, event | category | flops | bytes accessed | tf_op | source)
XLA Modules:
  0.0 138.6 jit_solution(16906444117926621125)
XLA Ops:
  0.8 4.4 %collective-permute-start.4 = (bf16[2,8,8192]{2,1,0:T(8,128)(2,1)}, bf16[2,8,8192]{2,1,0:T(8,128)(2,1)S(1)}, u32[]{:S(2)}, u32[]{:S(2)}) collective-permute-start(bf16[2,8,8192]{2,1,0:T(8,128)(2,1)} %own_ref.1), channel_id=1, source_target_pairs={{0,1},{1,0},{2,3},{3,2},{4,5},{5,4},{6,7},{7,6},{8,9},{9,8},{10,11... | collective-permute-start | bytes 786440 | tf_op jit(solution)/shard_map/ppermute | solution.py:45
  7.0 3.7 %leaves.1 = (bf16[256,1024]{1,0:T(8,128)(2,1)}, bf16[256,1024]{1,0:T(8,128)(2,1)}) custom-call(s32[1]{0:T(128)} %bitcast.hi_ref, bf16[2,8,8192]{2,1,0:T(8,128)(2,1)} %own_ref.1, bf16[2,8192,128]{2,1,0:T(8,128)(2,1)} %bitcast.22), custom_call_target="tpu_custom_call" | custom-call | flops 1000000 | bytes 1000000 | tf_op jit(solution)/shard_map/leaves/pallas_call | solution.py:103
  10.7 6.5 %collective-permute-start = (bf16[256,1024]{1,0:T(8,128)(2,1)}, bf16[256,1024]{1,0:T(8,128)(2,1)S(1)}, u32[]{:S(2)}, u32[]{:S(2)}) collective-permute-start(bf16[256,1024]{1,0:T(8,128)(2,1)} %get-tuple-element.18), channel_id=1, source_target_pairs={{0,4},{4,0},{1,5},{5,1},{2,6},{6,2},{3,7},{7,3},{8,12},{12,8},{9,1... | collective-permute-start | bytes 1572872 | tf_op jit(solution)/shard_map/ppermute | solution.py:45
  17.1 4.2 %to_boxes.1 = (bf16[8,512,128]{2,1,0:T(8,128)(2,1)}, bf16[1024,2048]{1,0:T(8,128)(2,1)}) custom-call(bf16[256,1024]{1,0:T(8,128)(2,1)} %get-tuple-element.21.lhs_ref, bf16[64,1024]{1,0:T(8,128)(2,1)} %interp_ref.1, f32[8,1024]{1,0:T(8,128)} %angle_ref.1), custom_call_target="tpu_custom_call" | custom-call | flops 1000000 | bytes 1000000 | tf_op jit(solution)/shard_map/to_boxes/pallas_call | solution.py:156
  21.3 3.6 %all-to-all-start = ((bf16[8,512,128]{2,1,0:T(8,128)(2,1)}), bf16[8,512,128]{2,1,0:T(8,128)(2,1)S(1)}, u32[]{:S(2)}, u32[]{:S(2)}) async-start(bf16[8,512,128]{2,1,0:T(8,128)(2,1)} %get-tuple-element.22), calls=%async_computation | async-start | bytes 2097152 | tf_op jit(solution)/shard_map/all_to_all | solution.py:431
  28.9 15.2 %collective-permute-done.lhs_ref = bf16[256,1024]{1,0:T(8,128)(2,1)S(1)} collective-permute-done((bf16[256,1024]{1,0:T(8,128)(2,1)}, bf16[256,1024]{1,0:T(8,128)(2,1)S(1)}, u32[]{:S(2)}, u32[]{:S(2)}) %collective-permute-start) | collective-permute-done | bytes 524320 | tf_op jit(solution)/shard_map/ppermute | solution.py:45
  44.0 2.2 %copy-done = bf16[1024,2048]{1,0:T(8,128)(2,1)S(1)} copy-done((bf16[1024,2048]{1,0:T(8,128)(2,1)S(1)}, bf16[1024,2048]{1,0:T(8,128)(2,1)}, u32[]{:S(2)}) %copy-start) | copy-done | bytes 4194328
  46.2 2.2 %to_boxes_again.1 = bf16[8,512,128]{2,1,0:T(8,128)(2,1)} custom-call(bf16[256,1024]{1,0:T(8,128)(2,1)S(1)} %collective-permute-done.lhs_ref, bf16[1024,2048]{1,0:T(8,128)(2,1)S(1)} %copy-done), custom_call_target="tpu_custom_call" | custom-call | flops 1000000 | bytes 6000000 | tf_op jit(solution)/shard_map/to_boxes_again/pallas_call | solution.py:182
  48.5 3.9 %all-to-all-done = bf16[8,512,128]{2,1,0:T(8,128)(2,1)S(1)} async-done(((bf16[8,512,128]{2,1,0:T(8,128)(2,1)}), bf16[8,512,128]{2,1,0:T(8,128)(2,1)S(1)}, u32[]{:S(2)}, u32[]{:S(2)}) %all-to-all-start) | async-done | bytes 1048608 | tf_op jit(solution)/shard_map/all_to_all | solution.py:431
  52.4 4.8 %all-to-all-start.1 = ((bf16[8,512,128]{2,1,0:T(8,128)(2,1)}), bf16[8,512,128]{2,1,0:T(8,128)(2,1)S(1)}, u32[]{:S(2)}, u32[]{:S(2)}) async-start(bf16[8,512,128]{2,1,0:T(8,128)(2,1)} %to_boxes_again.1), calls=%async_computation.1 | async-start | bytes 2097152 | tf_op jit(solution)/shard_map/all_to_all | solution.py:431
  57.2 14.9 %all-to-all-done.1 = bf16[8,512,128]{2,1,0:T(8,128)(2,1)S(1)} async-done(((bf16[8,512,128]{2,1,0:T(8,128)(2,1)}), bf16[8,512,128]{2,1,0:T(8,128)(2,1)S(1)}, u32[]{:S(2)}, u32[]{:S(2)}) %all-to-all-start.1) | async-done | bytes 1048608 | tf_op jit(solution)/shard_map/all_to_all | solution.py:431
  72.1 2.6 %collective-permute-done.6.four_ref = bf16[256,16,128]{2,1,0:T(8,128)(2,1)S(1)} collective-permute-done((bf16[256,16,128]{2,1,0:T(8,128)(2,1)S(1)}, bf16[256,16,128]{2,1,0:T(8,128)(2,1)S(1)}, u32[]{:S(2)}, u32[]{:S(2)}) %collective-permute-start.6) | collective-permute-done | bytes 1048608 | tf_op jit(solution)/shard_map/ppermute | solution.py:45
  74.7 8.2 %translate.3 = bf16[256,16,128]{2,1,0:T(8,128)(2,1)S(1)} custom-call(s32[6144]{0:T(1024)S(1)} %select_n.105.list_ref, f32[2,320,128]{2,1,0:T(8,128)S(1)} %pad.4.oper_ref, bf16[256,16,128]{2,1,0:T(8,128)(2,1)S(1)} %bitcast.25, bf16[256,16,128]{2,1,0:T(8,128)(2,1)S(1)} %collective-permute-done.5.two_ref, bf16[256,16,128]{2,1,0:T(8,128)(2,1)S(1)} %bitcast.28, ...), custom_call_target="tpu_custom_call" | custom-call | flops 1000000 | bytes 25000000 | tf_op jit(solution)/shard_map/translate/pallas_call | solution.py:250
  84.0 3.6 %all-to-all-start.3 = ((bf16[8,512,128]{2,1,0:T(8,128)(2,1)}), bf16[8,512,128]{2,1,0:T(8,128)(2,1)S(1)}, u32[]{:S(2)}, u32[]{:S(2)}) async-start(bf16[8,512,128]{2,1,0:T(8,128)(2,1)} %bitcast.30), calls=%async_computation.3 | async-start | bytes 2097152 | tf_op jit(solution)/shard_map/all_to_all | solution.py:431
  90.0 9.3 %translate.2 = bf16[256,16,128]{2,1,0:T(8,128)(2,1)} custom-call(s32[6144]{0:T(1024)S(1)} %select_n.103.list_ref, f32[2,320,128]{2,1,0:T(8,128)S(1)} %pad.4.oper_ref, bf16[256,16,128]{2,1,0:T(8,128)(2,1)S(1)} %bitcast.26, bf16[256,16,128]{2,1,0:T(8,128)(2,1)S(1)} %copy-done.6, bf16[256,16,128]{2,1,0:T(8,128)(2,1)S(1)} %bitcast.29, ...), custom_call_target="tpu_custom_call" | custom-call | flops 1000000 | bytes 25000000 | tf_op jit(solution)/shard_map/translate/pallas_call | solution.py:250
  99.3 4.2 %all-to-all-done.3.got_ref = bf16[8,512,128]{2,1,0:T(8,128)(2,1)S(1)} async-done(((bf16[8,512,128]{2,1,0:T(8,128)(2,1)}), bf16[8,512,128]{2,1,0:T(8,128)(2,1)S(1)}, u32[]{:S(2)}, u32[]{:S(2)}) %all-to-all-start.3) | async-done | bytes 1048608 | tf_op jit(solution)/shard_map/all_to_all | solution.py:431
  103.4 3.6 %all-to-all-start.2 = ((bf16[8,512,128]{2,1,0:T(8,128)(2,1)}), bf16[8,512,128]{2,1,0:T(8,128)(2,1)S(1)}, u32[]{:S(2)}, u32[]{:S(2)}) async-start(bf16[8,512,128]{2,1,0:T(8,128)(2,1)} %bitcast.7), calls=%async_computation.2 | async-start | bytes 2097152 | tf_op jit(solution)/shard_map/all_to_all | solution.py:431
  107.0 2.2 %copy-done.1 = bf16[1024,2048]{1,0:T(8,128)(2,1)S(1)} copy-done((bf16[1024,2048]{1,0:T(8,128)(2,1)S(1)}, bf16[1024,2048]{1,0:T(8,128)(2,1)}, u32[]{:S(2)}) %copy-start.1) | copy-done | bytes 4194328
  110.6 15.0 %near_part.1.near_ref = f32[2,8,8192]{2,1,0:T(8,128)} custom-call(s32[2048]{0:T(1024)} %reshape.37.idx_ref, bf16[2,8,8192]{2,1,0:T(8,128)(2,1)} %get-tuple-element.29.below_ref, bf16[2,8,8192]{2,1,0:T(8,128)(2,1)} %own_ref.1, bf16[2,8,8192]{2,1,0:T(8,128)(2,1)} %get-tuple-element.30.above_ref, bf16[2,8192,256]{2,1,0:T(8,128)(2,1)} %bitcast.31), custom_call_target="tpu_custom_call" | custom-call | flops 1000000 | bytes 1000000 | tf_op jit(solution)/shard_map/near_part/pallas_call | solution.py:334
  125.5 2.3 %all-to-all-done.2.got_ref = bf16[8,512,128]{2,1,0:T(8,128)(2,1)S(1)} async-done(((bf16[8,512,128]{2,1,0:T(8,128)(2,1)}), bf16[8,512,128]{2,1,0:T(8,128)(2,1)S(1)}, u32[]{:S(2)}, u32[]{:S(2)}) %all-to-all-start.2) | async-done | bytes 1048608 | tf_op jit(solution)/shard_map/all_to_all | solution.py:431
  127.8 2.2 %copy-done.2 = bf16[1024,2048]{1,0:T(8,128)(2,1)S(1)} copy-done((bf16[1024,2048]{1,0:T(8,128)(2,1)S(1)}, bf16[1024,2048]{1,0:T(8,128)(2,1)}, u32[]{:S(2)}) %copy-start.2) | copy-done | bytes 4194328
  130.0 1.3 from_boxes.2.own_ref
  131.3 4.6 %collective-permute-done.7.other_ref = bf16[256,1024]{1,0:T(8,128)(2,1)S(1)} collective-permute-done((bf16[256,1024]{1,0:T(8,128)(2,1)S(1)}, bf16[256,1024]{1,0:T(8,128)(2,1)S(1)}, u32[]{:S(2)}, u32[]{:S(2)}) %collective-permute-start.7) | collective-permute-done | bytes 524320 | tf_op jit(solution)/shard_map/ppermute | solution.py:45
  135.9 2.7 %far_part.1 = f32[2,8,8192]{2,1,0:T(8,128)} custom-call(s32[1]{0:T(128)} %bitcast.hi_ref, bf16[256,1024]{1,0:T(8,128)(2,1)S(1)} %from_boxes.2.own_ref, bf16[256,1024]{1,0:T(8,128)(2,1)S(1)} %collective-permute-done.7.other_ref, bf16[2,8192,128]{2,1,0:T(8,128)(2,1)S(1)} %bitcast.23, f32[2,8,8192]{2,1,0:T(8,128)S(1)} %copy-done.9), custom_call_target="tpu_custom_call" | custom-call | flops 1000000 | bytes 1000000 | tf_op jit(solution)/shard_map/far_part/pallas_call | solution.py:415
  (55 shorter events, 11.1 us)
Async XLA Ops:
  0.0 24.9 %copy-start.11 = (s32[1024,12]{0,1:T(8,128)S(1)}, s32[1024,12]{0,1:T(8,128)}, u32[]{:S(2)}) copy-start(s32[1024,12]{0,1:T(8,128)} %param.18) | copy-start | bytes 147460
  0.0 25.2 %copy-start.10 = (s32[1024,12]{0,1:T(8,128)S(1)}, s32[1024,12]{0,1:T(8,128)}, u32[]{:S(2)}) copy-start(s32[1024,12]{0,1:T(8,128)} %param.19) | copy-start | bytes 147460
  0.0 28.0 %collective-permute-start.3 = (bf16[2,8,8192]{2,1,0:T(8,128)(2,1)}, bf16[2,8,8192]{2,1,0:T(8,128)(2,1)S(1)}, u32[]{:S(2)}, u32[]{:S(2)}) collective-permute-start(bf16[2,8,8192]{2,1,0:T(8,128)(2,1)} %own_ref.1), channel_id=1, source_target_pairs={{1,2},{3,4},{5,6},{7,8},{9,10},{11,12},{13,14},{15,16},{17,18},{19... | collective-permute-start | bytes 786440 | tf_op jit(solution)/shard_map/ppermute | solution.py:38
  0.8 27.2 %collective-permute-start.4 = (bf16[2,8,8192]{2,1,0:T(8,128)(2,1)}, bf16[2,8,8192]{2,1,0:T(8,128)(2,1)S(1)}, u32[]{:S(2)}, u32[]{:S(2)}) collective-permute-start(bf16[2,8,8192]{2,1,0:T(8,128)(2,1)} %own_ref.1), channel_id=1, source_target_pairs={{0,1},{1,0},{2,3},{3,2},{4,5},{5,4},{6,7},{7,6},{8,9},{9,8},{10,11... | collective-permute-start | bytes 786440 | tf_op jit(solution)/shard_map/ppermute | solution.py:45
  6.3 19.9 %collective-permute-start.1 = (bf16[2,64,316]{1,2,0:T(8,128)(2,1)S(1)}, bf16[2,64,316]{1,2,0:T(8,128)(2,1)S(1)}, u32[]{:S(2)}, u32[]{:S(2)}) collective-permute-start(bf16[2,64,316]{1,2,0:T(8,128)(2,1)S(1)} %bitcast.32), channel_id=1, source_target_pairs={{0,0},{1,1},{2,2},{3,3},{16,4},{17,5},{18,6},{19,7},{4,8},{5,9},{6... | collective-permute-start | bytes 242696 | tf_op jit(solution)/shard_map/ppermute | solution.py:466
  10.7 15.7 %copy-start.12 = (s32[256,8]{0,1:T(8,128)S(1)}, s32[256,8]{0,1:T(8,128)}, u32[]{:S(2)}) copy-start(s32[256,8]{0,1:T(8,128)} %param.12) | copy-start | bytes 24580
  10.7 15.7 %copy-start.13 = (s32[256]{0:T(256)S(1)}, s32[256]{0:T(256)}, u32[]{:S(2)}) copy-start(s32[256]{0:T(256)} %param.13) | copy-start | bytes 3076
  10.7 33.4 %collective-permute-start = (bf16[256,1024]{1,0:T(8,128)(2,1)}, bf16[256,1024]{1,0:T(8,128)(2,1)S(1)}, u32[]{:S(2)}, u32[]{:S(2)}) collective-permute-start(bf16[256,1024]{1,0:T(8,128)(2,1)} %get-tuple-element.18), channel_id=1, source_target_pairs={{0,4},{4,0},{1,5},{5,1},{2,6},{6,2},{3,7},{7,3},{8,12},{12,8},{9,1... | collective-permute-start | bytes 1572872 | tf_op jit(solution)/shard_map/ppermute | solution.py:45
  21.3 31.0 %all-to-all-start = ((bf16[8,512,128]{2,1,0:T(8,128)(2,1)}), bf16[8,512,128]{2,1,0:T(8,128)(2,1)S(1)}, u32[]{:S(2)}, u32[]{:S(2)}) async-start(bf16[8,512,128]{2,1,0:T(8,128)(2,1)} %get-tuple-element.22), calls=%async_computation | async-start | bytes 2097152 | tf_op jit(solution)/shard_map/all_to_all | solution.py:431
  26.3 1.5 %collective-permute-start.2 = (bf16[2,64,316]{1,2,0:T(8,128)(2,1)S(1)}, bf16[2,64,316]{1,2,0:T(8,128)(2,1)S(1)}, u32[]{:S(2)}, u32[]{:S(2)}) collective-permute-start(bf16[2,64,316]{1,2,0:T(8,128)(2,1)S(1)} %collective-permute-done.1), channel_id=1, source_target_pairs={{0,1},{1,0},{2,3},{3,2},{4,5},{5,4},{6,7},{7,6},{8,9},{9,8},{10,11... | collective-permute-start | bytes 242696 | tf_op jit(solution)/shard_map/ppermute | solution.py:45
  44.0 2.2 %copy-start = (bf16[1024,2048]{1,0:T(8,128)(2,1)S(1)}, bf16[1024,2048]{1,0:T(8,128)(2,1)}, u32[]{:S(2)}) copy-start(bf16[1024,2048]{1,0:T(8,128)(2,1)} %get-tuple-element.24.mat_ref) | copy-start | bytes 12582916
  52.4 19.7 %all-to-all-start.1 = ((bf16[8,512,128]{2,1,0:T(8,128)(2,1)}), bf16[8,512,128]{2,1,0:T(8,128)(2,1)S(1)}, u32[]{:S(2)}, u32[]{:S(2)}) async-start(bf16[8,512,128]{2,1,0:T(8,128)(2,1)} %to_boxes_again.1), calls=%async_computation.1 | async-start | bytes 2097152 | tf_op jit(solution)/shard_map/all_to_all | solution.py:431
  57.2 14.9 %collective-permute-start.5 = (bf16[256,16,128]{2,1,0:T(8,128)(2,1)S(1)}, bf16[256,16,128]{2,1,0:T(8,128)(2,1)S(1)}, u32[]{:S(2)}, u32[]{:S(2)}) collective-permute-start(bf16[256,16,128]{2,1,0:T(8,128)(2,1)S(1)} %bitcast.24), channel_id=1, source_target_pairs={{0,1},{1,0},{2,3},{3,2},{4,5},{5,4},{6,7},{7,6},{8,9},{9,8},{10,11... | collective-permute-start | bytes 3145736 | tf_op jit(solution)/shard_map/ppermute | solution.py:45
  72.1 2.7 %collective-permute-start.6 = (bf16[256,16,128]{2,1,0:T(8,128)(2,1)S(1)}, bf16[256,16,128]{2,1,0:T(8,128)(2,1)S(1)}, u32[]{:S(2)}, u32[]{:S(2)}) collective-permute-start(bf16[256,16,128]{2,1,0:T(8,128)(2,1)S(1)} %bitcast.27), channel_id=1, source_target_pairs={{0,1},{1,0},{2,3},{3,2},{4,5},{5,4},{6,7},{7,6},{8,9},{9,8},{10,11... | collective-permute-start | bytes 3145736 | tf_op jit(solution)/shard_map/ppermute | solution.py:45
  72.1 11.9 %copy-start.5 = (bf16[256,16,128]{2,1,0:T(8,128)(2,1)}, bf16[256,16,128]{2,1,0:T(8,128)(2,1)S(1)}, u32[]{:S(2)}) copy-start(bf16[256,16,128]{2,1,0:T(8,128)(2,1)S(1)} %collective-permute-done.5.two_ref) | copy-start | bytes 3145732
  74.7 8.2 %copy-start.7 = (bf16[256,16,128]{2,1,0:T(8,128)(2,1)}, bf16[256,16,128]{2,1,0:T(8,128)(2,1)S(1)}, u32[]{:S(2)}) copy-start(bf16[256,16,128]{2,1,0:T(8,128)(2,1)S(1)} %collective-permute-done.6.four_ref) | copy-start | bytes 3145732
  84.0 19.5 %all-to-all-start.3 = ((bf16[8,512,128]{2,1,0:T(8,128)(2,1)}), bf16[8,512,128]{2,1,0:T(8,128)(2,1)S(1)}, u32[]{:S(2)}, u32[]{:S(2)}) async-start(bf16[8,512,128]{2,1,0:T(8,128)(2,1)} %bitcast.30), calls=%async_computation.3 | async-start | bytes 2097152 | tf_op jit(solution)/shard_map/all_to_all | solution.py:431
  87.5 1.2 copy-start.6
  103.4 24.4 %all-to-all-start.2 = ((bf16[8,512,128]{2,1,0:T(8,128)(2,1)}), bf16[8,512,128]{2,1,0:T(8,128)(2,1)S(1)}, u32[]{:S(2)}, u32[]{:S(2)}) async-start(bf16[8,512,128]{2,1,0:T(8,128)(2,1)} %bitcast.7), calls=%async_computation.2 | async-start | bytes 2097152 | tf_op jit(solution)/shard_map/all_to_all | solution.py:431
  107.0 2.2 %copy-start.1 = (bf16[1024,2048]{1,0:T(8,128)(2,1)S(1)}, bf16[1024,2048]{1,0:T(8,128)(2,1)}, u32[]{:S(2)}) copy-start(bf16[1024,2048]{1,0:T(8,128)(2,1)} %get-tuple-element.24.mat_ref) | copy-start | bytes 12582916
  110.5 25.4 %collective-permute-start.7 = (bf16[256,1024]{1,0:T(8,128)(2,1)S(1)}, bf16[256,1024]{1,0:T(8,128)(2,1)S(1)}, u32[]{:S(2)}, u32[]{:S(2)}) collective-permute-start(bf16[256,1024]{1,0:T(8,128)(2,1)S(1)} %from_boxes.3), channel_id=1, source_target_pairs={{0,4},{4,0},{1,5},{5,1},{2,6},{6,2},{3,7},{7,3},{8,12},{12,8},{9,1... | collective-permute-start | bytes 1572872 | tf_op jit(solution)/shard_map/ppermute | solution.py:45
  127.8 2.2 %copy-start.2 = (bf16[1024,2048]{1,0:T(8,128)(2,1)S(1)}, bf16[1024,2048]{1,0:T(8,128)(2,1)}, u32[]{:S(2)}) copy-start(bf16[1024,2048]{1,0:T(8,128)(2,1)} %get-tuple-element.24.mat_ref) | copy-start | bytes 12582916
  130.0 5.9 %copy-start.3 = (bf16[2,256,32,128]{3,2,1,0:T(8,128)(2,1)S(1)}, bf16[2,256,32,128]{3,2,1,0:T(8,128)(2,1)}, u32[]{:S(2)}) copy-start(bf16[2,256,32,128]{3,2,1,0:T(8,128)(2,1)} %param.14) | copy-start | bytes 12582916
  130.0 5.9 %copy-start.9 = (f32[2,8,8192]{2,1,0:T(8,128)S(1)}, f32[2,8,8192]{2,1,0:T(8,128)}, u32[]{:S(2)}) copy-start(f32[2,8,8192]{2,1,0:T(8,128)} %near_part.1.near_ref) | copy-start | bytes 1572868
  (2 other events, 2.2 us)

commit v10 on v9

--- a/solution.py
+++ b/solution.py
@@ -408,7 +408,7 @@
 def far_part(hi, own, other, radiation, near_field):
     width = near_field.shape[2]
     rows = own.shape[0]
-    steps = 2
+    steps = 1
     per_step = width // steps
     field = pl.BlockSpec((rows // steps, DEPTH), lambda s, *_: (s, 0))
     wave = pl.BlockSpec((2, R, per_step), lambda s, *_: (0, 0, s))

time: 139 us -> 139 us (level)
  no operation moved by 1% of the time
where the time goes in v10:
time: 139 us; the launch traced here: 138 us
  waiting for transfers between devices  48 us (35%)
  Pallas kernels  47.4 us (34%)
  starting transfers between devices  28 us (20%)
  local copies, waits for them, and re-layouts  13.1 us (9%)
    all_to_all x4, waiting for transfers between devices, swapped(): lax.all_to_all(array, INSIDE, split_axis=0, concat_axis=0, tiled=True)  25.3 us
    ppermute x6, waiting for transfers between devices, across(): return lax.ppermute(array, axis, [(0, 1), (1, 0)])  22.7 us
    pallas_call x2, Pallas kernels, translate(): pl.pallas_call(functools.partial(translate_kernel, group=16), grid_spec=p...  17.5 us
    all_to_all x4, starting transfers between devices, swapped(): lax.all_to_all(array, INSIDE, split_axis=0, concat_axis=0, tiled=True)  15.5 us
    pallas_call x1, Pallas kernels, near_part(): pl.pallas_call(near_kernel, grid_spec=pltpu.PrefetchScalarGridSpec(num_sc...  15 us
    unnamed x31, local copies, waits for them, and re-layouts  11.4 us
    ppermute x6, starting transfers between devices, across(): return lax.ppermute(array, axis, [(0, 1), (1, 0)])  11.1 us
    pallas_call x1, Pallas kernels, to_boxes(): pl.pallas_call(up_kernel, grid=(steps,), in_specs=[pl.BlockSpec((rows, DE...  4.19 us
  transfers between devices with their start and end apart: 12, of which 8 were waited for; matrix products, arithmetic and copies ran while one was open for 3% of the time, Pallas kernels for 27%

profile of v10, /device:TPU:0, one launch (start us, length us, event | category | flops | bytes accessed | tf_op | source)
XLA Modules:
  0.0 138.2 jit_solution(4445789774359918954)
XLA Ops:
  0.8 4.4 %collective-permute-start.4 = (bf16[2,8,8192]{2,1,0:T(8,128)(2,1)}, bf16[2,8,8192]{2,1,0:T(8,128)(2,1)S(1)}, u32[]{:S(2)}, u32[]{:S(2)}) collective-permute-start(bf16[2,8,8192]{2,1,0:T(8,128)(2,1)} %own_ref.1), channel_id=1, source_target_pairs={{0,1},{1,0},{2,3},{3,2},{4,5},{5,4},{6,7},{7,6},{8,9},{9,8},{10,11... | collective-permute-start | bytes 786440 | tf_op jit(solution)/shard_map/ppermute | solution.py:45
  7.0 3.7 %leaves.1 = (bf16[256,1024]{1,0:T(8,128)(2,1)}, bf16[256,1024]{1,0:T(8,128)(2,1)}) custom-call(s32[1]{0:T(128)} %bitcast.hi_ref, bf16[2,8,8192]{2,1,0:T(8,128)(2,1)} %own_ref.1, bf16[2,8192,128]{2,1,0:T(8,128)(2,1)} %bitcast.22), custom_call_target="tpu_custom_call" | custom-call | flops 1000000 | bytes 1000000 | tf_op jit(solution)/shard_map/leaves/pallas_call | solution.py:103
  10.7 6.5 %collective-permute-start = (bf16[256,1024]{1,0:T(8,128)(2,1)}, bf16[256,1024]{1,0:T(8,128)(2,1)S(1)}, u32[]{:S(2)}, u32[]{:S(2)}) collective-permute-start(bf16[256,1024]{1,0:T(8,128)(2,1)} %get-tuple-element.18), channel_id=1, source_target_pairs={{0,4},{4,0},{1,5},{5,1},{2,6},{6,2},{3,7},{7,3},{8,12},{12,8},{9,1... | collective-permute-start | bytes 1572872 | tf_op jit(solution)/shard_map/ppermute | solution.py:45
  17.1 4.2 %to_boxes.1 = (bf16[8,512,128]{2,1,0:T(8,128)(2,1)}, bf16[1024,2048]{1,0:T(8,128)(2,1)}) custom-call(bf16[256,1024]{1,0:T(8,128)(2,1)} %get-tuple-element.21.lhs_ref, bf16[64,1024]{1,0:T(8,128)(2,1)} %interp_ref.1, f32[8,1024]{1,0:T(8,128)} %angle_ref.1), custom_call_target="tpu_custom_call" | custom-call | flops 1000000 | bytes 1000000 | tf_op jit(solution)/shard_map/to_boxes/pallas_call | solution.py:156
  21.3 3.6 %all-to-all-start = ((bf16[8,512,128]{2,1,0:T(8,128)(2,1)}), bf16[8,512,128]{2,1,0:T(8,128)(2,1)S(1)}, u32[]{:S(2)}, u32[]{:S(2)}) async-start(bf16[8,512,128]{2,1,0:T(8,128)(2,1)} %get-tuple-element.22), calls=%async_computation | async-start | bytes 2097152 | tf_op jit(solution)/shard_map/all_to_all | solution.py:431
  28.9 15.2 %collective-permute-done.lhs_ref = bf16[256,1024]{1,0:T(8,128)(2,1)S(1)} collective-permute-done((bf16[256,1024]{1,0:T(8,128)(2,1)}, bf16[256,1024]{1,0:T(8,128)(2,1)S(1)}, u32[]{:S(2)}, u32[]{:S(2)}) %collective-permute-start) | collective-permute-done | bytes 524320 | tf_op jit(solution)/shard_map/ppermute | solution.py:45
  44.0 2.2 %copy-done = bf16[1024,2048]{1,0:T(8,128)(2,1)S(1)} copy-done((bf16[1024,2048]{1,0:T(8,128)(2,1)S(1)}, bf16[1024,2048]{1,0:T(8,128)(2,1)}, u32[]{:S(2)}) %copy-start) | copy-done | bytes 4194328
  46.2 2.2 %to_boxes_again.1 = bf16[8,512,128]{2,1,0:T(8,128)(2,1)} custom-call(bf16[256,1024]{1,0:T(8,128)(2,1)S(1)} %collective-permute-done.lhs_ref, bf16[1024,2048]{1,0:T(8,128)(2,1)S(1)} %copy-done), custom_call_target="tpu_custom_call" | custom-call | flops 1000000 | bytes 6000000 | tf_op jit(solution)/shard_map/to_boxes_again/pallas_call | solution.py:182
  48.5 3.9 %all-to-all-done = bf16[8,512,128]{2,1,0:T(8,128)(2,1)S(1)} async-done(((bf16[8,512,128]{2,1,0:T(8,128)(2,1)}), bf16[8,512,128]{2,1,0:T(8,128)(2,1)S(1)}, u32[]{:S(2)}, u32[]{:S(2)}) %all-to-all-start) | async-done | bytes 1048608 | tf_op jit(solution)/shard_map/all_to_all | solution.py:431
  52.4 4.8 %all-to-all-start.1 = ((bf16[8,512,128]{2,1,0:T(8,128)(2,1)}), bf16[8,512,128]{2,1,0:T(8,128)(2,1)S(1)}, u32[]{:S(2)}, u32[]{:S(2)}) async-start(bf16[8,512,128]{2,1,0:T(8,128)(2,1)} %to_boxes_again.1), calls=%async_computation.1 | async-start | bytes 2097152 | tf_op jit(solution)/shard_map/all_to_all | solution.py:431
  57.2 14.9 %all-to-all-done.1 = bf16[8,512,128]{2,1,0:T(8,128)(2,1)S(1)} async-done(((bf16[8,512,128]{2,1,0:T(8,128)(2,1)}), bf16[8,512,128]{2,1,0:T(8,128)(2,1)S(1)}, u32[]{:S(2)}, u32[]{:S(2)}) %all-to-all-start.1) | async-done | bytes 1048608 | tf_op jit(solution)/shard_map/all_to_all | solution.py:431
  72.1 2.6 %collective-permute-done.6.four_ref = bf16[256,16,128]{2,1,0:T(8,128)(2,1)S(1)} collective-permute-done((bf16[256,16,128]{2,1,0:T(8,128)(2,1)S(1)}, bf16[256,16,128]{2,1,0:T(8,128)(2,1)S(1)}, u32[]{:S(2)}, u32[]{:S(2)}) %collective-permute-start.6) | collective-permute-done | bytes 1048608 | tf_op jit(solution)/shard_map/ppermute | solution.py:45
  74.7 8.2 %translate.3 = bf16[256,16,128]{2,1,0:T(8,128)(2,1)S(1)} custom-call(s32[6144]{0:T(1024)S(1)} %select_n.105.list_ref, f32[2,320,128]{2,1,0:T(8,128)S(1)} %pad.4.oper_ref, bf16[256,16,128]{2,1,0:T(8,128)(2,1)S(1)} %bitcast.25, bf16[256,16,128]{2,1,0:T(8,128)(2,1)S(1)} %collective-permute-done.5.two_ref, bf16[256,16,128]{2,1,0:T(8,128)(2,1)S(1)} %bitcast.28, ...), custom_call_target="tpu_custom_call" | custom-call | flops 1000000 | bytes 25000000 | tf_op jit(solution)/shard_map/translate/pallas_call | solution.py:250
  84.0 3.6 %all-to-all-start.3 = ((bf16[8,512,128]{2,1,0:T(8,128)(2,1)}), bf16[8,512,128]{2,1,0:T(8,128)(2,1)S(1)}, u32[]{:S(2)}, u32[]{:S(2)}) async-start(bf16[8,512,128]{2,1,0:T(8,128)(2,1)} %bitcast.30), calls=%async_computation.3 | async-start | bytes 2097152 | tf_op jit(solution)/shard_map/all_to_all | solution.py:431
  90.0 9.3 %translate.2 = bf16[256,16,128]{2,1,0:T(8,128)(2,1)} custom-call(s32[6144]{0:T(1024)S(1)} %select_n.103.list_ref, f32[2,320,128]{2,1,0:T(8,128)S(1)} %pad.4.oper_ref, bf16[256,16,128]{2,1,0:T(8,128)(2,1)S(1)} %bitcast.26, bf16[256,16,128]{2,1,0:T(8,128)(2,1)S(1)} %copy-done.6, bf16[256,16,128]{2,1,0:T(8,128)(2,1)S(1)} %bitcast.29, ...), custom_call_target="tpu_custom_call" | custom-call | flops 1000000 | bytes 25000000 | tf_op jit(solution)/shard_map/translate/pallas_call | solution.py:250
  99.3 4.2 %all-to-all-done.3.got_ref = bf16[8,512,128]{2,1,0:T(8,128)(2,1)S(1)} async-done(((bf16[8,512,128]{2,1,0:T(8,128)(2,1)}), bf16[8,512,128]{2,1,0:T(8,128)(2,1)S(1)}, u32[]{:S(2)}, u32[]{:S(2)}) %all-to-all-start.3) | async-done | bytes 1048608 | tf_op jit(solution)/shard_map/all_to_all | solution.py:431
  103.4 3.6 %all-to-all-start.2 = ((bf16[8,512,128]{2,1,0:T(8,128)(2,1)}), bf16[8,512,128]{2,1,0:T(8,128)(2,1)S(1)}, u32[]{:S(2)}, u32[]{:S(2)}) async-start(bf16[8,512,128]{2,1,0:T(8,128)(2,1)} %bitcast.7), calls=%async_computation.2 | async-start | bytes 2097152 | tf_op jit(solution)/shard_map/all_to_all | solution.py:431
  107.0 2.2 %copy-done.1 = bf16[1024,2048]{1,0:T(8,128)(2,1)S(1)} copy-done((bf16[1024,2048]{1,0:T(8,128)(2,1)S(1)}, bf16[1024,2048]{1,0:T(8,128)(2,1)}, u32[]{:S(2)}) %copy-start.1) | copy-done | bytes 4194328
  110.6 15.0 %near_part.1.near_ref = f32[2,8,8192]{2,1,0:T(8,128)} custom-call(s32[2048]{0:T(1024)} %reshape.37.idx_ref, bf16[2,8,8192]{2,1,0:T(8,128)(2,1)} %get-tuple-element.29.below_ref, bf16[2,8,8192]{2,1,0:T(8,128)(2,1)} %own_ref.1, bf16[2,8,8192]{2,1,0:T(8,128)(2,1)} %get-tuple-element.30.above_ref, bf16[2,8192,256]{2,1,0:T(8,128)(2,1)} %bitcast.31), custom_call_target="tpu_custom_call" | custom-call | flops 1000000 | bytes 1000000 | tf_op jit(solution)/shard_map/near_part/pallas_call | solution.py:334
  125.5 2.3 %all-to-all-done.2.got_ref = bf16[8,512,128]{2,1,0:T(8,128)(2,1)S(1)} async-done(((bf16[8,512,128]{2,1,0:T(8,128)(2,1)}), bf16[8,512,128]{2,1,0:T(8,128)(2,1)S(1)}, u32[]{:S(2)}, u32[]{:S(2)}) %all-to-all-start.2) | async-done | bytes 1048608 | tf_op jit(solution)/shard_map/all_to_all | solution.py:431
  127.8 2.2 %copy-done.2 = bf16[1024,2048]{1,0:T(8,128)(2,1)S(1)} copy-done((bf16[1024,2048]{1,0:T(8,128)(2,1)S(1)}, bf16[1024,2048]{1,0:T(8,128)(2,1)}, u32[]{:S(2)}) %copy-start.2) | copy-done | bytes 4194328
  130.0 1.3 from_boxes.2.own_ref
  131.3 4.6 %collective-permute-done.7.other_ref = bf16[256,1024]{1,0:T(8,128)(2,1)S(1)} collective-permute-done((bf16[256,1024]{1,0:T(8,128)(2,1)S(1)}, bf16[256,1024]{1,0:T(8,128)(2,1)S(1)}, u32[]{:S(2)}, u32[]{:S(2)}) %collective-permute-start.7) | collective-permute-done | bytes 524320 | tf_op jit(solution)/shard_map/ppermute | solution.py:45
  135.9 2.3 %far_part.1 = f32[2,8,8192]{2,1,0:T(8,128)} custom-call(s32[1]{0:T(128)} %bitcast.hi_ref, bf16[256,1024]{1,0:T(8,128)(2,1)S(1)} %from_boxes.2.own_ref, bf16[256,1024]{1,0:T(8,128)(2,1)S(1)} %collective-permute-done.7.other_ref, bf16[2,8192,128]{2,1,0:T(8,128)(2,1)S(1)} %bitcast.23, f32[2,8,8192]{2,1,0:T(8,128)S(1)} %copy-done.9), custom_call_target="tpu_custom_call" | custom-call | flops 1000000 | bytes 1000000 | tf_op jit(solution)/shard_map/far_part/pallas_call | solution.py:415
  (55 shorter events, 11.1 us)
Async XLA Ops:
  0.0 24.9 %copy-start.11 = (s32[1024,12]{0,1:T(8,128)S(1)}, s32[1024,12]{0,1:T(8,128)}, u32[]{:S(2)}) copy-start(s32[1024,12]{0,1:T(8,128)} %param.18) | copy-start | bytes 147460
  0.0 25.2 %copy-start.10 = (s32[1024,12]{0,1:T(8,128)S(1)}, s32[1024,12]{0,1:T(8,128)}, u32[]{:S(2)}) copy-start(s32[1024,12]{0,1:T(8,128)} %param.19) | copy-start | bytes 147460
  0.0 28.0 %collective-permute-start.3 = (bf16[2,8,8192]{2,1,0:T(8,128)(2,1)}, bf16[2,8,8192]{2,1,0:T(8,128)(2,1)S(1)}, u32[]{:S(2)}, u32[]{:S(2)}) collective-permute-start(bf16[2,8,8192]{2,1,0:T(8,128)(2,1)} %own_ref.1), channel_id=1, source_target_pairs={{1,2},{3,4},{5,6},{7,8},{9,10},{11,12},{13,14},{15,16},{17,18},{19... | collective-permute-start | bytes 786440 | tf_op jit(solution)/shard_map/ppermute | solution.py:38
  0.8 27.2 %collective-permute-start.4 = (bf16[2,8,8192]{2,1,0:T(8,128)(2,1)}, bf16[2,8,8192]{2,1,0:T(8,128)(2,1)S(1)}, u32[]{:S(2)}, u32[]{:S(2)}) collective-permute-start(bf16[2,8,8192]{2,1,0:T(8,128)(2,1)} %own_ref.1), channel_id=1, source_target_pairs={{0,1},{1,0},{2,3},{3,2},{4,5},{5,4},{6,7},{7,6},{8,9},{9,8},{10,11... | collective-permute-start | bytes 786440 | tf_op jit(solution)/shard_map/ppermute | solution.py:45
  6.3 19.9 %collective-permute-start.1 = (bf16[2,64,316]{1,2,0:T(8,128)(2,1)S(1)}, bf16[2,64,316]{1,2,0:T(8,128)(2,1)S(1)}, u32[]{:S(2)}, u32[]{:S(2)}) collective-permute-start(bf16[2,64,316]{1,2,0:T(8,128)(2,1)S(1)} %bitcast.32), channel_id=1, source_target_pairs={{0,0},{1,1},{2,2},{3,3},{16,4},{17,5},{18,6},{19,7},{4,8},{5,9},{6... | collective-permute-start | bytes 242696 | tf_op jit(solution)/shard_map/ppermute | solution.py:466
  10.7 15.7 %copy-start.12 = (s32[256,8]{0,1:T(8,128)S(1)}, s32[256,8]{0,1:T(8,128)}, u32[]{:S(2)}) copy-start(s32[256,8]{0,1:T(8,128)} %param.12) | copy-start | bytes 24580
  10.7 15.7 %copy-start.13 = (s32[256]{0:T(256)S(1)}, s32[256]{0:T(256)}, u32[]{:S(2)}) copy-start(s32[256]{0:T(256)} %param.13) | copy-start | bytes 3076
  10.7 33.4 %collective-permute-start = (bf16[256,1024]{1,0:T(8,128)(2,1)}, bf16[256,1024]{1,0:T(8,128)(2,1)S(1)}, u32[]{:S(2)}, u32[]{:S(2)}) collective-permute-start(bf16[256,1024]{1,0:T(8,128)(2,1)} %get-tuple-element.18), channel_id=1, source_target_pairs={{0,4},{4,0},{1,5},{5,1},{2,6},{6,2},{3,7},{7,3},{8,12},{12,8},{9,1... | collective-permute-start | bytes 1572872 | tf_op jit(solution)/shard_map/ppermute | solution.py:45
  21.3 31.0 %all-to-all-start = ((bf16[8,512,128]{2,1,0:T(8,128)(2,1)}), bf16[8,512,128]{2,1,0:T(8,128)(2,1)S(1)}, u32[]{:S(2)}, u32[]{:S(2)}) async-start(bf16[8,512,128]{2,1,0:T(8,128)(2,1)} %get-tuple-element.22), calls=%async_computation | async-start | bytes 2097152 | tf_op jit(solution)/shard_map/all_to_all | solution.py:431
  26.3 1.5 %collective-permute-start.2 = (bf16[2,64,316]{1,2,0:T(8,128)(2,1)S(1)}, bf16[2,64,316]{1,2,0:T(8,128)(2,1)S(1)}, u32[]{:S(2)}, u32[]{:S(2)}) collective-permute-start(bf16[2,64,316]{1,2,0:T(8,128)(2,1)S(1)} %collective-permute-done.1), channel_id=1, source_target_pairs={{0,1},{1,0},{2,3},{3,2},{4,5},{5,4},{6,7},{7,6},{8,9},{9,8},{10,11... | collective-permute-start | bytes 242696 | tf_op jit(solution)/shard_map/ppermute | solution.py:45
  44.0 2.2 %copy-start = (bf16[1024,2048]{1,0:T(8,128)(2,1)S(1)}, bf16[1024,2048]{1,0:T(8,128)(2,1)}, u32[]{:S(2)}) copy-start(bf16[1024,2048]{1,0:T(8,128)(2,1)} %get-tuple-element.24.mat_ref) | copy-start | bytes 12582916
  52.4 19.7 %all-to-all-start.1 = ((bf16[8,512,128]{2,1,0:T(8,128)(2,1)}), bf16[8,512,128]{2,1,0:T(8,128)(2,1)S(1)}, u32[]{:S(2)}, u32[]{:S(2)}) async-start(bf16[8,512,128]{2,1,0:T(8,128)(2,1)} %to_boxes_again.1), calls=%async_computation.1 | async-start | bytes 2097152 | tf_op jit(solution)/shard_map/all_to_all | solution.py:431
  57.2 14.9 %collective-permute-start.5 = (bf16[256,16,128]{2,1,0:T(8,128)(2,1)S(1)}, bf16[256,16,128]{2,1,0:T(8,128)(2,1)S(1)}, u32[]{:S(2)}, u32[]{:S(2)}) collective-permute-start(bf16[256,16,128]{2,1,0:T(8,128)(2,1)S(1)} %bitcast.24), channel_id=1, source_target_pairs={{0,1},{1,0},{2,3},{3,2},{4,5},{5,4},{6,7},{7,6},{8,9},{9,8},{10,11... | collective-permute-start | bytes 3145736 | tf_op jit(solution)/shard_map/ppermute | solution.py:45
  72.1 2.7 %collective-permute-start.6 = (bf16[256,16,128]{2,1,0:T(8,128)(2,1)S(1)}, bf16[256,16,128]{2,1,0:T(8,128)(2,1)S(1)}, u32[]{:S(2)}, u32[]{:S(2)}) collective-permute-start(bf16[256,16,128]{2,1,0:T(8,128)(2,1)S(1)} %bitcast.27), channel_id=1, source_target_pairs={{0,1},{1,0},{2,3},{3,2},{4,5},{5,4},{6,7},{7,6},{8,9},{9,8},{10,11... | collective-permute-start | bytes 3145736 | tf_op jit(solution)/shard_map/ppermute | solution.py:45
  72.1 11.9 %copy-start.5 = (bf16[256,16,128]{2,1,0:T(8,128)(2,1)}, bf16[256,16,128]{2,1,0:T(8,128)(2,1)S(1)}, u32[]{:S(2)}) copy-start(bf16[256,16,128]{2,1,0:T(8,128)(2,1)S(1)} %collective-permute-done.5.two_ref) | copy-start | bytes 3145732
  74.7 8.2 %copy-start.7 = (bf16[256,16,128]{2,1,0:T(8,128)(2,1)}, bf16[256,16,128]{2,1,0:T(8,128)(2,1)S(1)}, u32[]{:S(2)}) copy-start(bf16[256,16,128]{2,1,0:T(8,128)(2,1)S(1)} %collective-permute-done.6.four_ref) | copy-start | bytes 3145732
  84.0 19.5 %all-to-all-start.3 = ((bf16[8,512,128]{2,1,0:T(8,128)(2,1)}), bf16[8,512,128]{2,1,0:T(8,128)(2,1)S(1)}, u32[]{:S(2)}, u32[]{:S(2)}) async-start(bf16[8,512,128]{2,1,0:T(8,128)(2,1)} %bitcast.30), calls=%async_computation.3 | async-start | bytes 2097152 | tf_op jit(solution)/shard_map/all_to_all | solution.py:431
  87.5 1.2 copy-start.6
  103.4 24.4 %all-to-all-start.2 = ((bf16[8,512,128]{2,1,0:T(8,128)(2,1)}), bf16[8,512,128]{2,1,0:T(8,128)(2,1)S(1)}, u32[]{:S(2)}, u32[]{:S(2)}) async-start(bf16[8,512,128]{2,1,0:T(8,128)(2,1)} %bitcast.7), calls=%async_computation.2 | async-start | bytes 2097152 | tf_op jit(solution)/shard_map/all_to_all | solution.py:431
  107.0 2.2 %copy-start.1 = (bf16[1024,2048]{1,0:T(8,128)(2,1)S(1)}, bf16[1024,2048]{1,0:T(8,128)(2,1)}, u32[]{:S(2)}) copy-start(bf16[1024,2048]{1,0:T(8,128)(2,1)} %get-tuple-element.24.mat_ref) | copy-start | bytes 12582916
  110.5 25.4 %collective-permute-start.7 = (bf16[256,1024]{1,0:T(8,128)(2,1)S(1)}, bf16[256,1024]{1,0:T(8,128)(2,1)S(1)}, u32[]{:S(2)}, u32[]{:S(2)}) collective-permute-start(bf16[256,1024]{1,0:T(8,128)(2,1)S(1)} %from_boxes.3), channel_id=1, source_target_pairs={{0,4},{4,0},{1,5},{5,1},{2,6},{6,2},{3,7},{7,3},{8,12},{12,8},{9,1... | collective-permute-start | bytes 1572872 | tf_op jit(solution)/shard_map/ppermute | solution.py:45
  127.8 2.2 %copy-start.2 = (bf16[1024,2048]{1,0:T(8,128)(2,1)S(1)}, bf16[1024,2048]{1,0:T(8,128)(2,1)}, u32[]{:S(2)}) copy-start(bf16[1024,2048]{1,0:T(8,128)(2,1)} %get-tuple-element.24.mat_ref) | copy-start | bytes 12582916
  130.0 5.9 %copy-start.3 = (bf16[2,256,32,128]{3,2,1,0:T(8,128)(2,1)S(1)}, bf16[2,256,32,128]{3,2,1,0:T(8,128)(2,1)}, u32[]{:S(2)}) copy-start(bf16[2,256,32,128]{3,2,1,0:T(8,128)(2,1)} %param.14) | copy-start | bytes 12582916
  130.0 5.9 %copy-start.9 = (f32[2,8,8192]{2,1,0:T(8,128)S(1)}, f32[2,8,8192]{2,1,0:T(8,128)}, u32[]{:S(2)}) copy-start(f32[2,8,8192]{2,1,0:T(8,128)} %near_part.1.near_ref) | copy-start | bytes 1572868
  (2 other events, 2.2 us)
